TPU v7x, 256 devices: a whole 4x4x8 slice. The times are simulated.
256 devices in a mesh: seq: 32 (over z_lo, y, x), dp: 8 (over z_hi, core).
Axes of the slice: x: 4, y: 4, z: 8 (z_hi: 4, z_lo: 2; z = z_hi * 2 + z_lo), core: 2. Of those that a mesh axis runs over, the one named last changes fastest.
Arguments:
- query_rows: bfloat16 [8, 4096, 4096], P('dp', 'seq'), may hold values from -6 to 6
- key_rows: bfloat16 [8, 4096, 4096], P('dp', 'seq'), may hold values from -6 to 6
- value_rows: bfloat16 [8, 4096, 4096], P('dp', 'seq'), may hold values from -6 to 6
- cotangent: bfloat16 [8, 4096, 4096], P('dp', 'seq'), may hold values from -6 to 6
- short_filter: float32 [3, 3, 4096], replicated, may hold values from -3 to 3
- residue: float32 [4096, 16], P('seq'), may hold values from -1.5 to 1.5
- decay_rate: float32 [4096, 16], P('seq'), as said below
Outputs:
- query_grad: bfloat16 [8, 4096, 4096], P('dp', 'seq')
- key_grad: bfloat16 [8, 4096, 4096], P('dp', 'seq')
- value_grad: bfloat16 [8, 4096, 4096], P('dp', 'seq')
- short_grad: float32 [3, 3, 4096], replicated
- residue_grad: float32 [4096, 16], P('seq')
- decay_grad: float32 [4096, 16], P('seq')
Inputs may be any that keep to these rules, and one draw needn't show every extreme that they name: `decay_rate`: every rate lies between 1 / 40960 and 1 / 32.
All inputs are finite; a program needn't handle non-finite values.
Results may differ from a plain program's by a relative error of at most 0.012.
Values may be sent and summed in bfloat16 or wider, within the bound.
No kernel may reach another device: no remote copies, remote signals or barrier semaphores. Data moves between devices by JAX's collectives and lax.ppermute only.
A program may use at most 128 MiB of HBM per device.

v0:
```python
import math

import jax
import jax.numpy as jnp
from jax import lax
from jax.sharding import PartitionSpec as P

precise = lax.Precision.HIGH


def passed_along(shard, axis, by):
    count = lax.axis_size(axis)
    pairs = [(i, i + by) for i in range(count) if 0 <= i + by < count]
    return lax.ppermute(shard, axis, pairs)


def modal_impulse(residue, decay_rate, length):
    times = jnp.arange(length).astype(residue.dtype)
    weights = residue * jnp.sqrt(-jnp.expm1(-2.0 * decay_rate))
    return jnp.sum(weights[None] * jnp.exp(-decay_rate[None] * times[:, None, None]), axis=2)


def modal_pullback(residue, decay_rate, grad_impulse):
    length = grad_impulse.shape[0]
    times = jnp.arange(length).astype(residue.dtype)
    weighted = grad_impulse[:, :, None] * jnp.exp(-decay_rate[None] * times[:, None, None])
    first_sum = jnp.sum(weighted, axis=0)
    second_sum = jnp.sum(weighted * times[:, None, None], axis=0)
    root = jnp.sqrt(-jnp.expm1(-2.0 * decay_rate))
    residue_local = root * first_sum
    rate_local = (
        residue * jnp.exp(-2.0 * decay_rate) / root * first_sum - residue * root * second_sum
    )
    return (residue_local, rate_local)


def dft_tables(points):
    inner = points // 128
    freq_k = jnp.arange(65, dtype=jnp.int32)
    first = jnp.arange(64, dtype=jnp.int32)
    rows_b = jnp.arange(inner, dtype=jnp.int32)
    angle_one = 2.0 * math.pi / 128 * (first[:, None] * freq_k[None, :] % 128).astype(jnp.float32)
    fore_one = jnp.stack([jnp.cos(angle_one), -jnp.sin(angle_one)], axis=1)
    whole = freq_k[:, None, None] + 128 * rows_b[None, None, :]
    angle_two = (
        2.0 * math.pi / points * (rows_b[None, :, None] * whole % points).astype(jnp.float32)
    )
    cos_two = jnp.cos(angle_two)
    sin_two = jnp.sin(angle_two)
    fore_two = jnp.stack([jnp.stack([cos_two, -sin_two]), jnp.stack([sin_two, cos_two])])
    cos_back = cos_two.transpose(0, 2, 1)
    sin_back = sin_two.transpose(0, 2, 1)
    back_two = jnp.stack([jnp.stack([cos_back, sin_back]), jnp.stack([-sin_back, cos_back])])
    scaling = jnp.where((freq_k == 0) | (freq_k == 64), 1.0, 2.0).astype(jnp.float32) / points
    back_one = jnp.stack(
        [scaling[:, None] * jnp.cos(angle_one.T), -scaling[:, None] * jnp.sin(angle_one.T)]
    )
    return (fore_one, fore_two, back_two, back_one)


def forward_dft(signal, tables):
    fore_one, fore_two, back_two, back_one = tables
    inner = fore_two.shape[3]
    shaped = signal.reshape(signal.shape[0], 64, inner, signal.shape[-1])
    section_one = jnp.einsum("zabc,apk->zpkbc", shaped, fore_one, precision=precise)
    return jnp.einsum("zpkbc,pqkbm->zqkmc", section_one, fore_two, precision=precise)


def inverse_dft(spectrum, tables):
    fore_one, fore_two, back_two, back_one = tables
    inner = fore_two.shape[3]
    turned = jnp.einsum("zqkmc,qpkmb->zpkbc", spectrum, back_two, precision=precise)
    signal = jnp.einsum("zpkbc,pka->zabc", turned, back_one, precision=precise)
    return signal.reshape(signal.shape[0], 64 * inner, signal.shape[-1])


def complex_product(left, right, conjugate):
    left_real, left_imag = (left[:, 0], left[:, 1])
    right_real, right_imag = (right[:, 0], right[:, 1])
    if conjugate:
        right_imag = -right_imag
    return jnp.stack(
        [
            left_real * right_real - left_imag * right_imag,
            left_real * right_imag + left_imag * right_real,
        ],
        axis=1,
    )


def body(query_rows, key_rows, value_rows, cotangent, short_filter, residue, decay_rate):
    tokens = query_rows.shape[1]
    margin = short_filter.shape[1] - 1
    length = tokens * lax.axis_size("seq")
    tables = dft_tables(2 * length)
    stacked = jnp.stack([query_rows, key_rows, value_rows])
    before = passed_along(stacked[:, :, tokens - margin :, :], "seq", 1)
    widened = jnp.concatenate([before, stacked], axis=2)
    shorted = jnp.zeros(stacked.shape, jnp.float32)
    for offset in range(margin + 1):
        shorted = shorted + short_filter[:, offset][:, None, None, :] * widened[
            :, :, margin - offset : margin - offset + tokens, :
        ].astype(jnp.float32)
    query_short, key_short, value_short = (shorted[0], shorted[1], shorted[2])
    upstream = cotangent.astype(jnp.float32)
    gated = (key_short * value_short).astype(jnp.bfloat16)
    grad_mixed = (upstream * query_short).astype(jnp.bfloat16)
    impulse = modal_impulse(residue, decay_rate, length)
    impulse_spec = forward_dft(impulse[None], tables)
    gated_cols = lax.all_to_all(gated, "seq", split_axis=2, concat_axis=1, tiled=True)
    spectra = forward_dft(gated_cols.astype(jnp.float32), tables)
    mixed_cols = inverse_dft(complex_product(spectra, impulse_spec, False), tables)
    spectra, mixed_cols = (spectra, mixed_cols.astype(jnp.bfloat16))
    mixed = lax.all_to_all(mixed_cols, "seq", split_axis=1, concat_axis=2, tiled=True)
    grad_cols = lax.all_to_all(grad_mixed, "seq", split_axis=2, concat_axis=1, tiled=True)
    grad_spec = forward_dft(grad_cols.astype(jnp.float32), tables)
    grad_gated_cols = inverse_dft(complex_product(grad_spec, impulse_spec, True), tables)
    cross = jnp.sum(complex_product(grad_spec, spectra, True), axis=0, keepdims=True)
    grad_impulse = inverse_dft(cross, tables)[0]
    grad_gated_cols, grad_impulse = (grad_gated_cols.astype(jnp.bfloat16), grad_impulse)
    grad_gated = lax.all_to_all(grad_gated_cols, "seq", split_axis=1, concat_axis=2, tiled=True)
    grad_gated_wide = grad_gated.astype(jnp.float32)
    grad_short = jnp.stack(
        [
            upstream * mixed.astype(jnp.float32),
            grad_gated_wide * value_short,
            grad_gated_wide * key_short,
        ]
    )
    after = passed_along(grad_short[:, :, :margin, :], "seq", -1)
    trailing = jnp.concatenate([grad_short, after], axis=2)
    grad_inputs = jnp.zeros_like(grad_short)
    filter_terms = []
    for offset in range(margin + 1):
        grad_inputs = (
            grad_inputs
            + short_filter[:, offset][:, None, None, :]
            * trailing[:, :, offset : offset + tokens, :]
        )
        filter_terms.append(
            jnp.sum(
                grad_short
                * widened[:, :, margin - offset : margin - offset + tokens, :].astype(jnp.float32),
                axis=(1, 2),
            )
        )
    filter_local = jnp.stack(filter_terms, axis=1)
    residue_local, rate_local = modal_pullback(residue, decay_rate, grad_impulse)
    rate_local = decay_rate * rate_local
    factor = 1.0 / math.sqrt(query_rows.shape[0] * lax.axis_size("dp") * length)
    filter_grad = lax.psum(filter_local, ("seq", "dp"))
    residue_grad, decay_grad = lax.psum((residue_local, rate_local), "dp")
    return (
        grad_inputs[0].astype(jnp.bfloat16),
        grad_inputs[1].astype(jnp.bfloat16),
        grad_inputs[2].astype(jnp.bfloat16),
        filter_grad * factor,
        residue_grad * factor,
        decay_grad * factor,
    )


def solution(mesh):
    placed = (
        P("dp", "seq", None),
        P("dp", "seq", None),
        P("dp", "seq", None),
        P("dp", "seq", None),
        P(),
        P("seq", None),
        P("seq", None),
    )
    return jax.shard_map(
        body,
        mesh=mesh,
        in_specs=placed,
        out_specs=(
            P("dp", "seq", None),
            P("dp", "seq", None),
            P("dp", "seq", None),
            P(),
            P("seq", None),
            P("seq", None),
        ),
        check_vma=False,
    )
```

profile of v0, /device:TPU:8, one launch (start us, length us, event | category | flops | bytes accessed | tf_op | source)
XLA Modules:
  0.0 795.1 jit_solution(14131893450674865667)
XLA Ops:
  35.7 7.9 fusion.9
  45.5 16.7 %copy.284 = bf16[1,128,4096]{1,0,2:T(2,128)(2,1)S(1)} copy(bf16[1,128,4096]{1,2,0:T(8,128)(2,1)S(1)} %fusion.68) | data formatting | bytes 2097152 | tf_op jit(solution)/shard_map/convert_element_type | solution.py:107
  62.7 23.4 %reduce = bf16[4096,128]{1,0:T(8,128)(2,1)} reduce(bf16[4096,1,128]{2,1,0:T(2,128)(2,1)S(1)} %bitcast.194, bf16[]{:T(256)} %broadcast.536), dimensions={1}, to_apply=%bitcast.165.reduce_sub_computation | reduce | bytes 2097154
  98.1 16.7 %copy.286 = bf16[1,128,4096]{1,0,2:T(2,128)(2,1)S(1)} copy(bf16[1,128,4096]{1,2,0:T(8,128)(2,1)S(1)} %fusion.82) | data formatting | bytes 2097152 | tf_op jit(solution)/shard_map/convert_element_type | solution.py:106
  114.9 23.4 %reduce.1 = bf16[4096,128]{1,0:T(8,128)(2,1)} reduce(bf16[4096,1,128]{2,1,0:T(2,128)(2,1)S(1)} %bitcast.196, bf16[]{:T(256)} %broadcast.536), dimensions={1}, to_apply=%bitcast.167.reduce_sub_computation | reduce | bytes 2097154
  140.5 8.4 %all-to-all-start = ((bf16[32,2,8192]{2,1,0:T(2,128)(2,1)}), bf16[32,2,8192]{2,1,0:T(2,128)(2,1)}, u32[]{:S(2)}, u32[]{:S(2)}) async-start(bf16[32,2,8192]{2,1,0:T(2,128)(2,1)} %reshape.807), calls=%async_computation | async-start | bytes 2097152 | tf_op jit(solution)/shard_map/all_to_all | solution.py:110
  149.1 17.1 %fusion.80 = (f32[1,65,64,64]{2,3,0,1:T(8,128)S(1)}, f32[1,65,64,64]{2,3,0,1:T(8,128)S(1)}, f32[1,65,64,64]{2,3,0,1:T(8,128)S(1)}, f32[1,65,64,64]{2,3,0,1:T(8,1...) fusion(s32[65,64]{1,0:T(8,128)S(1)} %iota_add_fusion), kind=kLoop, calls=%fused_computation.105 | loop fusion | flops 7987200 | bytes 6406400 | tf_op jit(solution)/shard_map/sin | solution.py:49
  188.2 10.8 %copy.148 = bf16[1,32,128,128]{3,2,1,0:T(8,128)(2,1)} copy(bf16[1,32,128,128]{2,3,1,0:T(8,128)(2,1)} %bitcast.201) | data formatting | bytes 2097152 | tf_op jit(solution)/shard_map/all_to_all | solution.py:110
  209.0 9.8 %fusion.37 = f32[1,2,65,64,128]{4,3,1,2,0:T(8,128)} fusion(f32[2,65,64,128,1]{3,1,2,0,4:T(8,128)} %convolution_bitcast_fusion, f32[1,2,65,64,64]{3,4,0,1,2:T(8,128)} %get-tuple-element.61, f32[1,2,65,64,64]{3,4,0,1,2:T(8,128)S(1)} %bitcast.174), kind=kOutput, calls=%fused_computation.68 | convolution fusion | flops 818954240 | bytes 12779520 | tf_op jit(solution)/shard_map/zpkbc,pqkbm->zqkmc/dot_general | solution.py:66
  218.8 9.7 %fusion.31 = f32[1,2,65,64,128]{4,3,1,2,0:T(8,128)} fusion(f32[2,65,64,128,1]{3,1,2,0,4:T(8,128)} %convolution_bitcast_fusion.1, f32[1,2,65,64,64]{3,4,0,1,2:T(8,128)} %get-tuple-element.61, f32[1,2,65,64,64]{3,4,0,1,2:T(8,128)S(1)} %bitcast.174), kind=kOutput, calls=%fused_computation.66 | convolution fusion | flops 818954240 | bytes 12779520 | tf_op jit(solution)/shard_map/zpkbc,pqkbm->zqkmc/dot_general | solution.py:66
  234.9 7.4 fusion.50
  249.3 33.2 %multiply_reduce_fusion = (f32[128,16]{0,1:T(8,128)S(1)}, f32[128,16]{0,1:T(8,128)S(1)}, f32[4096,128]{1,0:T(8,128)S(1)}) fusion(f32[4096,128]{1,0:T(8,128)S(1)} %bitcast.207, f32[4096]{0:T(1024)S(1)} %iota_convert_fusion, f32[128,16]{0,1:T(8,128)S(1)} %get-tuple-element.74, f32[128,16]{0,1:T(8,128)S(1)} %get-tuple-element.73), kind=kLoop, calls=%fused_computation | loop fusion | flops 58191872 | bytes 4243456 | tf_op jit(solution)/shard_map/reduce_sum | solution.py:28
  287.7 9.7 %fusion.34 = f32[1,2,65,64,128]{4,3,1,2,0:T(8,128)} fusion(f32[2,65,64,128,1]{3,1,2,0,4:T(8,128)} %convolution_bitcast_fusion.2, f32[1,2,65,64,64]{3,4,0,1,2:T(8,128)} %get-tuple-element.61, f32[1,2,65,64,64]{3,4,0,1,2:T(8,128)S(1)} %bitcast.174), kind=kOutput, calls=%fused_computation.67 | convolution fusion | flops 818954240 | bytes 12779520 | tf_op jit(solution)/shard_map/zpkbc,pqkbm->zqkmc/dot_general | solution.py:66
  297.4 10.8 %multiply_subtract_fusion.2 = (f32[1,1,65,64,128]{4,3,1,2,0:T(8,128)}, f32[1,1,65,64,128]{4,3,1,2,0:T(8,128)}, f32[1,1,65,64,128]{4,3,1,2,0:T(8,128)}, f32[1,1,65,64,128]{4,3,1,2,0:T(8,128)}) fusion(f32[1,2,65,64,128]{4,3,1,2,0:T(8,128)} %fusion.34, f32[1,2,65,64,128]{4,3,1,2,0:T(8,128)} %fusion.31, f32[1,2,65,64,128]{4,3,1,2,0:T(8,128)} %fusion.37), kind=kLoop, calls=%fused_computation.83 | loop fusion | flops 6922240 | bytes 21299200 | tf_op jit(solution)/shard_map/sub | solution.py:84
  318.2 16.7 %copy.283 = bf16[1,4096,128]{2,0,1:T(2,128)(2,1)S(1)} copy(bf16[1,4096,128]{2,1,0:T(8,128)(2,1)S(1)} %bitcast.202) | data formatting | bytes 2097152 | tf_op jit(solution)/shard_map/convert_element_type | solution.py:120
  334.9 23.4 %reduce.2 = bf16[4096,128]{1,0:T(8,128)(2,1)} reduce(bf16[4096,1,128]{2,1,0:T(2,128)(2,1)S(1)} %bitcast.197, bf16[]{:T(256)} %broadcast.536), dimensions={1}, to_apply=%bitcast.164.reduce_sub_computation | reduce | bytes 2097154
  360.4 8.8 %all-to-all-start.3 = ((bf16[32,2,8192]{2,1,0:T(2,128)(2,1)}), bf16[32,2,8192]{2,1,0:T(2,128)(2,1)}, u32[]{:S(2)}, u32[]{:S(2)}) async-start(bf16[32,2,8192]{2,1,0:T(2,128)(2,1)} %reshape.809), calls=%async_computation.3 | async-start | bytes 2097152 | tf_op jit(solution)/shard_map/all_to_all | solution.py:121
  369.2 8.6 %fusion.40 = f32[2,65,64,128]{3,2,1,0:T(8,128)S(1)} fusion(f32[1,1,65,64,128]{4,3,1,2,0:T(8,128)} %get-tuple-element.45, f32[1,1,65,64,128]{4,3,1,2,0:T(8,128)} %get-tuple-element.44, f32[1,2,65,64,64]{3,4,1,2,0:T(8,128)} %get-tuple-element.59, f32[1,2,65,64,64]{3,4,1,2,0:T(8,128)} %get-tuple-element.58), kind=kOutput, calls=%fused_computation.69 | convolution fusion | flops 820019200 | bytes 12779520 | tf_op jit(solution)/shard_map/zqkmc,qpkmb->zpkbc/dot_general | solution.py:72
  382.2 16.7 %copy.285 = bf16[1,4096,128]{2,0,1:T(2,128)(2,1)S(1)} copy(bf16[1,4096,128]{2,1,0:T(8,128)(2,1)S(1)} %bitcast.203) | data formatting | bytes 2097152 | tf_op jit(solution)/shard_map/convert_element_type | solution.py:113
  399.0 23.6 %reduce.3 = bf16[4096,128]{1,0:T(8,128)(2,1)} reduce(bf16[4096,1,128]{2,1,0:T(2,128)(2,1)S(1)} %bitcast.195, bf16[]{:T(256)} %broadcast.536), dimensions={1}, to_apply=%bitcast.166.reduce_sub_computation | reduce | bytes 2097154
  424.7 8.4 %all-to-all-start.1 = ((bf16[32,2,8192]{2,1,0:T(2,128)(2,1)}), bf16[32,2,8192]{2,1,0:T(2,128)(2,1)}, u32[]{:S(2)}, u32[]{:S(2)}) async-start(bf16[32,2,8192]{2,1,0:T(2,128)(2,1)} %reshape.811), calls=%async_computation.1 | async-start | bytes 2097152 | tf_op jit(solution)/shard_map/all_to_all | solution.py:114
  433.2 31.8 %all-reduce = (f32[128,16]{0,1:T(8,128)S(1)}, f32[128,16]{0,1:T(8,128)S(1)}) all-reduce(f32[128,16]{0,1:T(8,128)S(1)} %get-tuple-element.72, f32[128,16]{0,1:T(8,128)S(1)} %get-tuple-element.71), channel_id=1, replica_groups=mesh['seq'=32,'dp'=8] {'dp'}, use_global_device_ids=true, to_apply=%region_6.7 | all-reduce | flops 4096 | bytes 32768 | tf_op jit(solution)/shard_map/psum | solution.py:152
  518.0 16.5 %fusion.11 = (f32[3,4096]{1,0:T(4,128)S(1)}, f32[3,4096]{1,0:T(4,128)S(1)}, f32[3,4096]{1,0:T(4,128)S(1)}, bf16[3,1,128,4096]{2,3,1,0:T(8,128)(2,1)}) fusion(bf16[3,1,130,4096]{2,3,1,0:T(8,128)(2,1)S(1)} %bitcast.176, f32[1,1,128,4096]{2,3,1,0:T(8,128)S(1)} %copy-done.4, f32[1,1,128,4096]{2,3,1,0:T(8,128)S(1)} %copy-done.2, ...), kind=kLoop, calls=%fused_computation.23 | loop fusion | flops 29847552 | bytes 31752192 | tf_op jit(solution)/shard_map/reduce_sum | solution.py:141
  541.2 244.9 %all-reduce.3.cloned.1.call-done = f32[3,3,4096]{2,0,1:T(4,128)} async-done(((f32[3,3,4096]{2,0,1:T(4,128)}), f32[3,3,4096]{2,0,1:T(4,128)}) %all-reduce.3.cloned.1.call-update) | async-done | bytes 147472 | tf_op jit(solution)/shard_map/psum | solution.py:151
  (130 shorter events, 175.6 us)
Async XLA Ops:
  10.4 25.3 %copy-start.7 = (bf16[1,128,4096]{1,2,0:T(8,128)(2,1)}, bf16[1,128,4096]{1,2,0:T(8,128)(2,1)S(1)}, u32[]{:S(2)}) copy-start(bf16[1,128,4096]{1,2,0:T(8,128)(2,1)S(1)} %copy.143) | copy-start | bytes 3145732
  12.4 23.3 %copy-start.9 = (bf16[1,128,4096]{1,2,0:T(8,128)(2,1)}, bf16[1,128,4096]{1,2,0:T(8,128)(2,1)S(1)}, u32[]{:S(2)}) copy-start(bf16[1,128,4096]{1,2,0:T(8,128)(2,1)S(1)} %copy.144) | copy-start | bytes 3145732
  12.8 9.2 %copy-start.12 = (f32[3,3,4096]{2,1,0:T(4,128)S(1)}, f32[3,3,4096]{2,1,0:T(4,128)}, u32[]{:S(2)}) copy-start(f32[3,3,4096]{2,1,0:T(4,128)} %param.11) | copy-start | bytes 442372
  18.5 8.1 %collective-permute-start = (bf16[3,1,2,4096]{3,2,1,0:T(2,128)(2,1)S(1)}, bf16[3,1,2,4096]{3,2,1,0:T(2,128)(2,1)S(1)}, u32[]{:S(2)}, u32[]{:S(2)}) collective-permute-start(bf16[3,1,2,4096]{3,2,1,0:T(2,128)(2,1)S(1)} %copy.145), channel_id=1, source_target_pairs={{0,8},{8,16},{16,24},{24,32},{32,40},{40,48},{48,56},{56,64},{64,7... | collective-permute-start | bytes 147464 | tf_op jit(solution)/shard_map/ppermute | solution.py:14
  35.7 8.0 %copy-start = (bf16[3,1,130,4096]{2,3,1,0:T(8,128)(2,1)}, bf16[3,1,130,4096]{2,3,1,0:T(8,128)(2,1)S(1)}, u32[]{:S(2)}) copy-start(bf16[3,1,130,4096]{2,3,1,0:T(8,128)(2,1)S(1)} %maximum_maximum_fusion) | copy-start | bytes 9584644
  35.7 8.0 copy-start.11
  88.2 52.2 %all-to-all-start.2 = ((bf16[32,2,8192]{2,1,0:T(2,128)(2,1)}), bf16[32,2,8192]{2,1,0:T(2,128)(2,1)}, u32[]{:S(2)}, u32[]{:S(2)}) async-start(bf16[32,2,8192]{2,1,0:T(2,128)(2,1)} %reshape.805), calls=%async_computation.2 | async-start | bytes 2097152 | tf_op jit(solution)/shard_map/all_to_all | solution.py:115
  114.9 34.0 %copy-start.13 = (f32[128,16]{0,1:T(8,128)S(1)}, f32[128,16]{0,1:T(8,128)}, u32[]{:S(2)}) copy-start(f32[128,16]{0,1:T(8,128)} %param.12) | copy-start | bytes 24580
  114.9 34.0 %copy-start.14 = (f32[128,16]{0,1:T(8,128)S(1)}, f32[128,16]{0,1:T(8,128)}, u32[]{:S(2)}) copy-start(f32[128,16]{0,1:T(8,128)} %param.13) | copy-start | bytes 24580
  140.5 42.3 %all-to-all-start = ((bf16[32,2,8192]{2,1,0:T(2,128)(2,1)}), bf16[32,2,8192]{2,1,0:T(2,128)(2,1)}, u32[]{:S(2)}, u32[]{:S(2)}) async-start(bf16[32,2,8192]{2,1,0:T(2,128)(2,1)} %reshape.807), calls=%async_computation | async-start | bytes 2097152 | tf_op jit(solution)/shard_map/all_to_all | solution.py:110
  188.2 20.8 %slice-start.4 = ((s8[4259840]{0:T(1024)(128)(4,1)}), s8[65536]{0:T(1024)(128)(4,1)S(1)}, s32[]{:S(2)}) async-start(s8[4259840]{0:T(1024)(128)(4,1)} %bitcast.173), calls=%async_computation.9 | async-start | bytes 131072
  199.0 10.0 %slice-start.5 = ((s8[4259840]{0:T(1024)(128)(4,1)}), s8[4194304]{0:T(1024)(128)(4,1)S(1)}, s32[]{:S(2)}) async-start(s8[4259840]{0:T(1024)(128)(4,1)} %bitcast.173), calls=%async_computation.10 | async-start | bytes 8388608
  209.0 25.8 %slice-start = ((s8[4259840]{0:T(1024)(128)(4,1)}), s8[4194304]{0:T(1024)(128)(4,1)S(1)}, s32[]{:S(2)}) async-start(s8[4259840]{0:T(1024)(128)(4,1)} %bitcast.169), calls=%async_computation.5 | async-start | bytes 8388608
  209.0 25.8 %slice-start.2 = ((s8[4259840]{0:T(1024)(128)(4,1)}), s8[4194304]{0:T(1024)(128)(4,1)S(1)}, s32[]{:S(2)}) async-start(s8[4259840]{0:T(1024)(128)(4,1)} %bitcast.171), calls=%async_computation.7 | async-start | bytes 8388608
  218.8 16.0 %slice-start.1 = ((s8[4259840]{0:T(1024)(128)(4,1)}), s8[65536]{0:T(1024)(128)(4,1)S(1)}, s32[]{:S(2)}) async-start(s8[4259840]{0:T(1024)(128)(4,1)} %bitcast.169), calls=%async_computation.6 | async-start | bytes 131072
  218.8 16.0 %slice-start.3 = ((s8[4259840]{0:T(1024)(128)(4,1)}), s8[65536]{0:T(1024)(128)(4,1)S(1)}, s32[]{:S(2)}) async-start(s8[4259840]{0:T(1024)(128)(4,1)} %bitcast.171), calls=%async_computation.8 | async-start | bytes 131072
  360.4 64.3 %all-to-all-start.3 = ((bf16[32,2,8192]{2,1,0:T(2,128)(2,1)}), bf16[32,2,8192]{2,1,0:T(2,128)(2,1)}, u32[]{:S(2)}, u32[]{:S(2)}) async-start(bf16[32,2,8192]{2,1,0:T(2,128)(2,1)} %reshape.809), calls=%async_computation.3 | async-start | bytes 2097152 | tf_op jit(solution)/shard_map/all_to_all | solution.py:121
  424.7 51.9 %all-to-all-start.1 = ((bf16[32,2,8192]{2,1,0:T(2,128)(2,1)}), bf16[32,2,8192]{2,1,0:T(2,128)(2,1)}, u32[]{:S(2)}, u32[]{:S(2)}) async-start(bf16[32,2,8192]{2,1,0:T(2,128)(2,1)} %reshape.811), calls=%async_computation.1 | async-start | bytes 2097152 | tf_op jit(solution)/shard_map/all_to_all | solution.py:114
  433.1 353.0 %all-reduce.3.cloned.1.call-start = ((), (), s32[]{:S(2)}) async-start(), calls=%async_computation.4 | async-start | bytes 393216 | tf_op jit(solution)/shard_map/psum | solution.py:151
  476.6 14.5 %copy-start.1 = (f32[1,1,128,4096]{2,3,1,0:T(8,128)}, f32[1,1,128,4096]{2,3,1,0:T(8,128)S(1)}, u32[]{:S(2)}) copy-start(f32[1,1,128,4096]{2,3,1,0:T(8,128)S(1)} %get-tuple-element.50) | copy-start | bytes 6291460
  498.8 6.9 collective-permute-start.1
  505.7 10.2 %slice-start.6 = ((s8[6291456]{0:T(1024)(128)(4,1)}), s8[2097152]{0:T(1024)(128)(4,1)S(1)}, s32[]{:S(2)}) async-start(s8[6291456]{0:T(1024)(128)(4,1)} %bitcast.175), calls=%async_computation.11 | async-start | bytes 4194304
  509.7 7.9 copy-start.8
  509.7 8.2 %copy-start.10 = (bf16[1,128,4096]{1,2,0:T(8,128)(2,1)S(1)}, bf16[1,128,4096]{1,2,0:T(8,128)(2,1)}, u32[]{:S(2)}) copy-start(bf16[1,128,4096]{1,2,0:T(8,128)(2,1)} %copy-done.9) | copy-start | bytes 3145732
  (6 other events, 33.4 us)
Sparse Core Ops, SparseCore 0:
  535.3 250.7 all-reduce.2
where the time goes:
time: 806 us; the launch traced here: 795 us
  waiting for transfers between devices  249 us (31%)
  other arithmetic  226 us (28%)
  local copies, waits for them, and re-layouts  153 us (19%)
  matrix products  79.2 us (10%)
  starting transfers between devices  40.9 us (5%)
  blocking collectives  31.8 us (4%)
  between operations  15 us (2%)
    psum x1, waiting for transfers between devices, body(): filter_grad = lax.psum(filter_local, ('seq', 'dp'))  245 us
    unnamed x8, other arithmetic  93.7 us
    unnamed x67, local copies, waits for them, and re-layouts  44.9 us
    reduce_sum x1, other arithmetic, modal_pullback(): second_sum = jnp.sum(weighted * times[:, None, None], axis=0)  33.2 us
    psum x1, blocking collectives, body(): residue_grad, decay_grad = lax.psum((residue_local, rate_local), 'dp')  31.8 us
    dot_general x3, matrix products, forward_dft(): jnp.einsum('zpkbc,pqkbm->zqkmc', section_one, fore_two, precision=precise)  29.2 us
    dot_general x3, matrix products, inverse_dft(): jnp.einsum('zqkmc,qpkmb->zpkbc', spectrum, back_two, precision=precise)  21.6 us
    convert_element_type x2, local copies, waits for them, and re-layouts, body(): grad_gated_cols.astype(jnp.bfloat16)  17.4 us
  transfers between devices with their start and end apart: 7, of which 3 were waited for; matrix products, arithmetic and copies ran while one was open for 19% of the time, Pallas kernels for 0%

commit v1 on v0

v1 whole, which is shorter than its diff:
```python
import math

import jax
import jax.numpy as jnp
import numpy as np
from jax import lax
from jax.experimental import pallas as pl
from jax.experimental.pallas import tpu as pltpu
from jax.sharding import PartitionSpec as P

BLOCK = 128
TERMS = 16
TOP_RATE = 1.0 / 32.0
FREQS = 128
LANES = 128
BF16 = jnp.bfloat16
F32 = jnp.float32
VMEM_LIMIT = 48 * 1024 * 1024


def decay_terms(times):
    points = 64
    theta = (np.arange(points) + 0.5) * np.pi / points
    rates = (np.cos(theta) + 1.0) * TOP_RATE / 2.0
    values = np.exp(-np.asarray(times, np.float64)[:, None] * rates[None, :])
    basis = np.cos(np.arange(TERMS)[None, :] * theta[:, None]) * (2.0 / points)
    basis[:, 0] *= 0.5
    return values @ basis


def halves(table):
    table = np.asarray(table, np.float32)
    high = table.astype(BF16)
    low = (table - high.astype(np.float32)).astype(BF16)
    return high, low


def paired(table):
    return np.concatenate(halves(table), axis=1)


def make_tables():
    t = np.arange(BLOCK)
    angle = 2.0 * np.pi / (2 * FREQS) * (np.arange(FREQS)[:, None] + 0.5) * t[None, :]
    fore = np.concatenate([np.cos(angle), -np.sin(angle)], axis=0)
    back = np.concatenate([np.cos(angle.T), -np.sin(angle.T)], axis=1) / FREQS
    ahead = decay_terms(t)
    behind = decay_terms(BLOCK - t)
    fore_u = paired(np.concatenate([fore, behind.T], axis=0))
    fore_g = paired(np.concatenate([fore, ahead.T], axis=0))
    impulse_high, impulse_low = halves(fore @ ahead)
    impulse = np.concatenate([impulse_high, impulse_high, impulse_low], axis=1)
    taps = np.zeros((8, TERMS))
    taps[:3] = decay_terms([0, 1, -1])
    taps_high, taps_low = halves(taps)
    return dict(
        fore_u=fore_u,
        fore_g=fore_g,
        impulse=impulse,
        back=back.astype(BF16),
        lag=(ahead.T @ back).astype(BF16),
        ahead_t=ahead.T.astype(BF16),
        behind_t=behind.T.astype(BF16),
        ahead=paired(ahead),
        behind=paired(behind),
        taps3=np.concatenate([taps_high, taps_high, taps_low], axis=1),
        taps2=np.concatenate([taps_high, taps_low], axis=1),
        first=[float(x) for x in taps[0]],
        second=[float(x) for x in taps[1]],
    )


def dot(left, right):
    return jnp.dot(left, right, preferred_element_type=F32)


def whole(shape):
    return pl.BlockSpec(shape, lambda *_: (0,) * len(shape))


def lagged(values, before):
    row = lax.broadcasted_iota(jnp.int32, values.shape, 0)
    one = jnp.where(row == 0, before[1:2], pltpu.roll(values, 1, 0))
    two = pltpu.roll(values, 2, 0)
    two = jnp.where(row == 0, before[0:1], jnp.where(row == 1, before[1:2], two))
    return one, two


def leading(values, after):
    count = values.shape[0]
    row = lax.broadcasted_iota(jnp.int32, values.shape, 0)
    one = jnp.where(row == count - 1, after[0:1], pltpu.roll(values, count - 1, 0))
    two = pltpu.roll(values, count - 2, 0)
    two = jnp.where(
        row == count - 2, after[0:1], jnp.where(row == count - 1, after[1:2], two)
    )
    return one, two


def lanes_of(ref, rows):
    return jnp.concatenate([ref[i, rows, :] for i in range(ref.shape[0])], axis=1)


def prep_kernel(weight_ref, rate_ref, basis_ref, slope_ref, loaded_ref, spread_ref):
    weight = weight_ref[...]
    spot = rate_ref[...] * (2.0 / TOP_RATE) - 1.0
    value, older = jnp.ones_like(spot), spot
    slope, older_slope = jnp.zeros_like(spot), jnp.zeros_like(spot)
    rows = []
    for k in range(TERMS):
        basis_ref[k] = value
        slope_ref[k] = slope * (-2.0 / TOP_RATE)
        loaded = value * weight
        loaded_ref[k] = loaded
        rows.append(jnp.sum(loaded, axis=0, keepdims=True))
        if k == 0:
            following, following_slope = spot, jnp.ones_like(spot)
        else:
            following = 2.0 * spot * value - older
            following_slope = 2.0 * value + 2.0 * spot * slope - older_slope
        older, older_slope = value, slope
        value, slope = following, following_slope
    coefs = jnp.concatenate(rows, axis=0)
    high = coefs.astype(BF16)
    low = (coefs - high.astype(F32)).astype(BF16)
    both = jnp.concatenate([high, low], axis=0)
    spread_ref[...] = jnp.broadcast_to(both[None], spread_ref.shape)


def block_kernel(
    query_ref, key_ref, value_ref, cot_ref, filter_ref, before_ref, coefs_ref,
    fore_u_ref, fore_g_ref, impulse_ref, back_ref, lag_ref, ahead_t_ref, behind_t_ref,
    sent_ref, mixed_ref, grad_ref,
):
    taps = filter_ref[...]
    before = before_ref[...]
    query, key, value = (ref[0].astype(F32) for ref in (query_ref, key_ref, value_ref))
    cot = cot_ref[0].astype(F32)
    queries = (query, *lagged(query, before[0:2]))
    keys = (key, *lagged(key, before[2:4]))
    values = (value, *lagged(value, before[4:6]))

    def short(i, inputs):
        return sum(taps[3 * i + j : 3 * i + j + 1] * inputs[j] for j in range(3))

    key_short, value_short = short(1, keys), short(2, values)
    gated = (key_short * value_short).astype(BF16)
    grad_mixed = (cot * short(0, queries)).astype(BF16)
    u = dot(fore_u_ref[...], jnp.concatenate([gated, gated], axis=0))
    g = dot(fore_g_ref[...], jnp.concatenate([grad_mixed, grad_mixed], axis=0))
    coefs = lanes_of(coefs_ref, slice(None))
    h = dot(impulse_ref[...], jnp.concatenate([coefs, coefs[:TERMS]], axis=0))
    ur, ui, gr, gi, hr, hi = (
        x[part * FREQS : (part + 1) * FREQS] for x in (u, g, h) for part in (0, 1)
    )

    def spectrum(real, imag):
        return jnp.concatenate([real.astype(BF16), imag.astype(BF16)], axis=0)

    mixed = dot(back_ref[...], spectrum(ur * hr - ui * hi, ur * hi + ui * hr))
    grad = dot(back_ref[...], spectrum(gr * hr + gi * hi, gi * hr - gr * hi))
    lag = dot(lag_ref[...], spectrum(gr * ur + gi * ui, gi * ur - gr * ui))
    mixed_ref[...] = mixed
    grad_ref[...] = grad
    rows = [u[2 * FREQS :], g[2 * FREQS :], lag]
    sums = []
    for left, inputs, total, table_ref in (
        (cot, queries, mixed, ahead_t_ref),
        (value_short, keys, grad, behind_t_ref),
        (key_short, values, grad, behind_t_ref),
    ):
        for j in range(3):
            product = left * inputs[j]
            rows.append(dot(table_ref[...], product.astype(BF16)))
            sums.append(jnp.sum(product * total, axis=0, keepdims=True))
    sums.append(jnp.zeros((16 - len(sums), sums[0].shape[1]), F32))
    rows.append(jnp.concatenate(sums, axis=0))
    for index, part in enumerate(rows):
        part = part.astype(BF16)
        for i in range(sent_ref.shape[0]):
            sent_ref[i, index * 16 : index * 16 + 16, :] = part[:, i * LANES : (i + 1) * LANES]


def owner_kernel(first, second, moments_ref, basis_ref, slope_ref, loaded_ref, rate_ref, carry_ref, grads_ref, ahead, behind):
    blocks = moments_ref.shape[1]
    modes = rate_ref.shape[0]
    row = lax.broadcasted_iota(jnp.int32, (blocks, LANES), 0)

    def later(x, by):
        return jnp.where(row >= by, pltpu.roll(x, by, 0), 0.0)

    def sooner(x, by):
        return jnp.where(row < blocks - by, pltpu.roll(x, blocks - by, 0), 0.0)

    lag_rows = [jnp.sum(moments_ref[2 * TERMS + k], axis=0, keepdims=True) for k in range(TERMS)]
    first_rows, second_rows = [], []
    for n in range(modes):
        basis = [basis_ref[k, n : n + 1, :] for k in range(TERMS)]
        slope = [slope_ref[k, n : n + 1, :] for k in range(TERMS)]
        state = sum(basis[k] * moments_ref[k] for k in range(TERMS))
        state_slope = sum(slope[k] * moments_ref[k] for k in range(1, TERMS))
        grad = sum(basis[k] * moments_ref[TERMS + k] for k in range(TERMS))
        grad_slope = sum(slope[k] * moments_ref[TERMS + k] for k in range(1, TERMS))
        factor = jnp.exp(-float(BLOCK) * rate_ref[n : n + 1, :])
        forward, forward_slope, backward = later(state, 1), later(state_slope, 1), sooner(grad, 1)
        by = 1
        while by < blocks:
            moved = later(forward, by)
            forward_slope = forward_slope + factor * (
                later(forward_slope, by) + float(BLOCK * by) * moved
            )
            forward = forward + factor * moved
            backward = backward + factor * sooner(backward, by)
            factor = factor * factor
            by *= 2
        ahead[n] = forward
        behind[n] = backward
        first_sum = jnp.sum(forward * grad, axis=0, keepdims=True)
        second_sum = jnp.sum(forward_slope * grad + forward * grad_slope, axis=0, keepdims=True)
        first_rows.append(first_sum + sum(basis[k] * lag_rows[k] for k in range(TERMS)))
        second_rows.append(second_sum + sum(slope[k] * lag_rows[k] for k in range(1, TERMS)))
    grads_ref[...] = jnp.concatenate(first_rows + second_rows, axis=0)
    totals = [moments_ref[12 * TERMS + i] for i in range(9)]
    edge_one, edge_two = 0.0, 0.0
    for k in range(TERMS):
        carry = sum(loaded_ref[k, n : n + 1, :] * ahead[n] for n in range(modes))
        back = sum(loaded_ref[k, n : n + 1, :] * behind[n] for n in range(modes))
        carry_ref[k] = carry
        carry_ref[TERMS + k] = back
        edge_one = edge_one + first[k] * carry
        edge_two = edge_two + second[k] * carry
        for i in range(9):
            totals[i] = totals[i] + (carry if i < 3 else back) * moments_ref[(3 + i) * TERMS + k]
    carry_ref[2 * TERMS] = sooner(edge_one, 1)
    carry_ref[2 * TERMS + 1] = sooner(edge_two, 1)
    for i in range(9):
        total = jnp.sum(totals[i], axis=0, keepdims=True)
        high = total.astype(BF16).astype(F32)
        carry_ref[2 * TERMS + 2 + i] = jnp.broadcast_to(high, (blocks, LANES))
        carry_ref[2 * TERMS + 11 + i] = jnp.broadcast_to(total - high, (blocks, LANES))
    for i in range(2 * TERMS + 20, carry_ref.shape[0]):
        carry_ref[i] = jnp.zeros((blocks, LANES), F32)


def finish_kernel(
    query_ref, key_ref, value_ref, cot_ref, filter_ref, before_ref, after_ref, coefs_ref,
    mixed_ref, grad_ref, carry_ref, ahead_ref, behind_ref, taps3_ref, taps2_ref,
    query_out, key_out, value_out,
):
    taps = filter_ref[...]
    before, after = before_ref[...], after_ref[...]
    query, key, value = (ref[0].astype(F32) for ref in (query_ref, key_ref, value_ref))
    cot = cot_ref[0].astype(F32)

    def tap(i, j):
        return taps[3 * i + j : 3 * i + j + 1]

    def short(i, inputs):
        return sum(tap(i, j) * inputs[j] for j in range(3))

    def rounded(x):
        return x.astype(BF16).astype(F32)

    key_short = short(1, (key, *lagged(key, before[2:4])))
    value_short = short(2, (value, *lagged(value, before[4:6])))

    def short_after(i, inputs):
        last, next_two = inputs[inputs.shape[0] - 2 :], after[2 * i : 2 * i + 2]
        one = jnp.concatenate([last[1:2], next_two[0:1]], axis=0)
        return tap(i, 0) * next_two + tap(i, 1) * one + tap(i, 2) * last

    query_next, key_next, value_next = (
        short_after(i, x) for i, x in enumerate((query, key, value))
    )
    cot_next = after[6:8]
    gated_next = rounded(key_next * value_next)
    grad_mixed_next = rounded(cot_next[0:1] * query_next[0:1])

    ahead = lanes_of(carry_ref, slice(0, TERMS))
    behind = lanes_of(carry_ref, slice(TERMS, 2 * TERMS))
    rest = lanes_of(carry_ref, slice(2 * TERMS, 3 * TERMS)).astype(F32)
    coefs = lanes_of(coefs_ref, slice(None))
    mixed = mixed_ref[...] + dot(ahead_ref[...], jnp.concatenate([ahead, ahead], axis=0))
    grad = grad_ref[...] + dot(behind_ref[...], jnp.concatenate([behind, behind], axis=0))
    impulse = dot(taps3_ref[...], jnp.concatenate([coefs, coefs[:TERMS]], axis=0))
    edge = dot(taps2_ref[...], jnp.concatenate([behind, behind], axis=0))
    mixed_next = rounded(
        jnp.concatenate(
            [
                rest[0:1] + impulse[0:1] * gated_next[0:1],
                rest[1:2] + impulse[0:1] * gated_next[1:2] + impulse[1:2] * gated_next[0:1],
            ],
            axis=0,
        )
    )
    grad_next = rounded(
        jnp.concatenate([edge[0:1], edge[2:3] - grad_mixed_next * impulse[2:3]], axis=0)
    )
    mixed, grad = rounded(mixed), rounded(grad)
    for i, (out_ref, short_grad, after_grad) in enumerate(
        (
            (query_out, cot * mixed, cot_next * mixed_next),
            (key_out, grad * value_short, grad_next * value_next),
            (value_out, grad * key_short, grad_next * key_next),
        )
    ):
        one, two = leading(short_grad, after_grad)
        out_ref[0] = (tap(i, 0) * short_grad + tap(i, 1) * one + tap(i, 2) * two).astype(BF16)


def body(query_rows, key_rows, value_rows, cotangent, short_filter, residue, decay_rate):
    width = query_rows.shape[2]
    blocks = lax.axis_size("seq")
    groups = lax.axis_size("dp")
    modes = residue.shape[1]
    length = BLOCK * blocks
    wide = min(512, width)
    parts = wide // LANES
    grid = (width // wide,)
    tables = make_tables()
    first, second = tables.pop("first"), tables.pop("second")
    tables = {name: jnp.asarray(table) for name, table in tables.items()}
    params = pltpu.CompilerParams(vmem_limit_bytes=VMEM_LIMIT)

    edge_last = jnp.concatenate([x[0, BLOCK - 2 :] for x in (query_rows, key_rows, value_rows)], axis=0)
    edge_first = jnp.concatenate([x[0, :2] for x in (query_rows, key_rows, value_rows, cotangent)], axis=0)
    before = lax.ppermute(edge_last, "seq", [(i, i + 1) for i in range(blocks - 1)]).astype(F32)
    after = lax.ppermute(edge_first, "seq", [(i + 1, i) for i in range(blocks - 1)]).astype(F32)
    before = jnp.concatenate([before, jnp.zeros((2, width), F32)], axis=0)

    root = jnp.sqrt(-jnp.expm1(-2.0 * decay_rate))
    weight_t = (residue * root).T
    rate_t = decay_rate.T
    small = jax.ShapeDtypeStruct((TERMS, modes, LANES), F32)
    basis, slope, loaded, spread = pl.pallas_call(
        prep_kernel,
        out_shape=(small, small, small, jax.ShapeDtypeStruct((blocks, 2 * TERMS, LANES), BF16)),
        compiler_params=params,
        name="prep",
    )(weight_t, rate_t)
    coefs = lax.all_to_all(spread, "seq", 0, 0, tiled=True)

    filters = short_filter.reshape(9, width)
    tall = pl.BlockSpec((1, BLOCK, wide), lambda c: (0, 0, c))
    flat = pl.BlockSpec((BLOCK, wide), lambda c: (0, c))
    nine = pl.BlockSpec((9, wide), lambda c: (0, c))
    eight = pl.BlockSpec((8, wide), lambda c: (0, c))

    def chunks(rows):
        return pl.BlockSpec((parts, rows, LANES), lambda c: (c, 0, 0))

    names = ("fore_u", "fore_g", "impulse", "back", "lag", "ahead_t", "behind_t")
    sent, mixed, grad = pl.pallas_call(
        block_kernel,
        grid=grid,
        in_specs=[tall] * 4
        + [nine, eight, chunks(2 * TERMS)]
        + [whole(tables[name].shape) for name in names],
        out_specs=(chunks(13 * TERMS), flat, flat),
        out_shape=(
            jax.ShapeDtypeStruct((blocks, 13 * TERMS, LANES), BF16),
            jax.ShapeDtypeStruct((BLOCK, width), F32),
            jax.ShapeDtypeStruct((BLOCK, width), F32),
        ),
        compiler_params=params,
        name="block",
    )(
        query_rows, key_rows, value_rows, cotangent, filters, before, coefs,
        *[tables[name] for name in names],
    )
    moments = lax.all_to_all(sent, "seq", 0, 0, tiled=True)
    moments = moments.transpose(1, 0, 2).astype(F32)

    carry, sums = pl.pallas_call(
        lambda *refs: owner_kernel(first, second, *refs),
        out_shape=(
            jax.ShapeDtypeStruct((4 * TERMS, blocks, LANES), F32),
            jax.ShapeDtypeStruct((2 * modes, LANES), F32),
        ),
        scratch_shapes=[pltpu.VMEM((modes, blocks, LANES), F32)] * 2,
        compiler_params=params,
        name="owner",
    )(moments, basis, slope, loaded, rate_t)
    carry = lax.all_to_all(carry.astype(BF16).transpose(1, 0, 2), "seq", 0, 0, tiled=True)

    root_t = root.T
    first_sum, second_sum = sums[:modes], sums[modes:]
    residue_local = root_t * first_sum
    rate_local = residue.T * (jnp.exp(-2.0 * rate_t) / root_t * first_sum - root_t * second_sum)
    decay_local = rate_t * rate_local
    begin = 2 * TERMS + 2
    shared = carry[:, begin : begin + 9].astype(F32) + carry[:, begin + 9 : begin + 18].astype(F32)
    local = jnp.concatenate([shared.reshape(9 * blocks, LANES), residue_local, decay_local], axis=0)
    local = local.astype(BF16)
    total = lax.all_to_all(
        jnp.broadcast_to(local[None], (groups, *local.shape)), "dp", 0, 0, tiled=True
    )
    names = ("ahead", "behind", "taps3", "taps2")
    outs = pl.pallas_call(
        finish_kernel,
        grid=grid,
        in_specs=[tall] * 4
        + [nine, eight, eight, chunks(2 * TERMS), flat, flat, chunks(4 * TERMS)]
        + [whole(tables[name].shape) for name in names],
        out_specs=[tall] * 3,
        out_shape=[jax.ShapeDtypeStruct(query_rows.shape, BF16)] * 3,
        compiler_params=params,
        name="finish",
    )(
        query_rows, key_rows, value_rows, cotangent, filters, before, after, coefs, mixed, grad, carry,
        *[tables[name] for name in names],
    )
    factor = 1.0 / math.sqrt(query_rows.shape[0] * groups * length)
    total = jnp.sum(total.astype(F32), axis=0) * factor
    filter_grad = total[: 9 * blocks].reshape(blocks, 3, 3, LANES).transpose(1, 2, 0, 3).reshape(3, 3, width)
    residue_grad = total[9 * blocks : 9 * blocks + modes].T
    decay_grad = total[9 * blocks + modes :].T
    return (*outs, filter_grad, residue_grad, decay_grad)


def solution(mesh):
    rows = P("dp", "seq", None)
    return jax.shard_map(
        body,
        mesh=mesh,
        in_specs=(rows, rows, rows, rows, P(), P("seq", None), P("seq", None)),
        out_specs=(rows, rows, rows, P(), P("seq", None), P("seq", None)),
        check_vma=False,
    )
```

time: 806 us -> 140 us (0.17)
  the two profiles are of different devices: /device:TPU:8 before, /device:TPU:31 now
where the time goes in v1:
time: 140 us; the launch traced here: 139 us
  starting transfers between devices  33.1 us (24%)
  blocking collectives  26.2 us (19%)
  Pallas kernels  24.7 us (18%)
  local copies, waits for them, and re-layouts  24.2 us (17%)
  waiting for transfers between devices  22.1 us (16%)
  other arithmetic  7.57 us (5%)
    all_to_all x1, blocking collectives, body(): moments = lax.all_to_all(sent, 'seq', 0, 0, tiled=True)  26.2 us
    ppermute x1, waiting for transfers between devices, body(): lax.ppermute(edge_first, 'seq', [(i + 1, i) for i in range(blocks - 1)])  16.2 us
    unnamed x46, local copies, waits for them, and re-layouts  13.9 us
    all_to_all x1, starting transfers between devices, body(): lax.all_to_all(jnp.broadcast_to(local[None], (groups, *local.shape)), 'dp...  12.5 us
    pallas_call x1, Pallas kernels, body(): pl.pallas_call(block_kernel, grid=grid, in_specs=[tall] * 4 + [nine, eigh...  12.3 us
    pallas_call x1, Pallas kernels, body(): pl.pallas_call(finish_kernel, grid=grid, in_specs=[tall] * 4 + [nine, eig...  9.06 us
    all_to_all x1, starting transfers between devices, body(): coefs = lax.all_to_all(spread, 'seq', 0, 0, tiled=True)  8.02 us
    all_to_all x1, starting transfers between devices, body(): lax.all_to_all(carry.astype(BF16).transpose(1, 0, 2), 'seq', 0, 0, tiled=...  7.5 us
  transfers between devices with their start and end apart: 5, of which 3 were waited for; matrix products, arithmetic and copies ran while one was open for 5% of the time, Pallas kernels for 7%

profile of v1, /device:TPU:31, one launch (start us, length us, event | category | flops | bytes accessed | tf_op | source)
XLA Modules:
  0.0 138.7 jit_solution(8720815230355392284)
XLA Ops:
  2.9 8.0 %all-to-all-start = ((bf16[32,32,128]{2,1,0:T(8,128)(2,1)}), bf16[32,32,128]{2,1,0:T(8,128)(2,1)S(1)}, u32[]{:S(2)}, u32[]{:S(2)}) async-start(bf16[32,32,128]{2,1,0:T(8,128)(2,1)} %get-tuple-element.18), calls=%async_computation | async-start | bytes 524288 | tf_op jit(solution)/shard_map/all_to_all | solution.py:341
  11.0 1.5 %slice_bitcast_fusion.3 = (bf16[2,4096]{1,0:T(2,128)(2,1)}, bf16[2,4096]{1,0:T(2,128)(2,1)S(1)}) fusion(bf16[1,128,4096]{2,1,0:T(8,128)(2,1)} %query_ref.3), kind=kLoop, calls=%fused_computation.13 | loop fusion | bytes 65536 | tf_op jit(solution)/shard_map/squeeze | solution.py:326
  12.5 1.6 %slice_bitcast_fusion.1 = (bf16[2,4096]{1,0:T(2,128)(2,1)}, bf16[2,4096]{1,0:T(2,128)(2,1)S(1)}, bf16[2,4096]{1,0:T(2,128)(2,1)S(1)}, bf16[2,4096]{1,0:T(2,128)(2,1)}) fusion(bf16[1,128,4096]{2,1,0:T(8,128)(2,1)} %value_ref.3, bf16[1,128,4096]{2,1,0:T(8,128)(2,1)} %key_ref.3), kind=kLoop, calls=%fused_computation.11 | loop fusion | bytes 131072 | tf_op jit(solution)/shard_map/squeeze | solution.py:326
  14.1 3.1 %collective-permute-start = (bf16[6,4096]{1,0:T(8,128)(2,1)S(1)}, bf16[6,4096]{1,0:T(8,128)(2,1)S(1)}, u32[]{:S(2)}, u32[]{:S(2)}) collective-permute-start(bf16[6,4096]{1,0:T(8,128)(2,1)S(1)} %pad_maximum_fusion.1), channel_id=1, source_target_pairs={{0,8},{8,16},{16,24},{24,32},{32,40},{40,48},{48,56},{56,64},{64,7... | collective-permute-start | bytes 147464 | tf_op jit(solution)/shard_map/ppermute | solution.py:327
  17.2 1.0 reshape.46.filter_ref
  19.2 1.2 copy-done.1
  20.4 1.2 copy-done.3
  21.6 1.2 copy-done.5
  28.4 12.3 %block.1 = (bf16[32,208,128]{2,1,0:T(8,128)(2,1)}, f32[128,4096]{1,0:T(8,128)}, f32[128,4096]{1,0:T(8,128)}) custom-call(bf16[1,128,4096]{2,1,0:T(8,128)(2,1)S(1)} %copy-done, bf16[1,128,4096]{2,1,0:T(8,128)(2,1)S(1)} %copy-done.1, bf16[1,128,4096]{2,1,0:T(8,128)(2,1)S(1)} %copy-done.3, bf16[1,128,4096]{2,1,0:T(8,128)(2,1)S(1)} %copy-done.5, ...), custom_call_target="tpu_custom_call" | custom-call | tf_op jit(solution)/shard_map/block/pallas_call | solution.py:353
  40.7 26.2 %all_to_all.20 = bf16[32,208,128]{2,1,0:T(8,128)(2,1)S(1)} all-to-all(bf16[32,208,128]{2,1,0:T(8,128)(2,1)} %get-tuple-element.21), channel_id=1, replica_groups=mesh['seq'=32,'dp'=8] {'seq'}, dimensions={0} | all-to-all | bytes 3407872 | tf_op jit(solution)/shard_map/all_to_all | solution.py:371
  67.6 2.6 %owner.1 = (f32[64,32,128]{2,1,0:T(8,128)S(1)}, f32[32,128]{1,0:T(8,128)S(1)}) custom-call(f32[208,32,128]{2,1,0:T(8,128)S(1)} %convert_bitcast_fusion.refs_0_, f32[16,16,128]{2,1,0:T(8,128)S(1)} %get-tuple-element.22.refs_1_, f32[16,16,128]{2,1,0:T(8,128)S(1)} %get-tuple-element.23.refs_2_, f32[16,16,128]{2,1,0:T(8,128)S(1)} %get-tuple-element.24.refs_3_, ...), custom_call_target="tpu_custom_call" | custom-call | tf_op jit(solution)/shard_map/owner/pallas_call | solution.py:374
  70.2 1.4 %copy.42 = bf16[64,32,128]{2,0,1:T(8,128)(2,1)} copy(f32[64,32,128]{2,1,0:T(8,128)S(1)} %get-tuple-element.25) | data formatting | bytes 1572864 | tf_op jit(solution)/shard_map/owner/pallas_call | solution.py:374
  71.6 7.5 %all-to-all-start.2 = ((bf16[32,64,128]{2,1,0:T(8,128)(2,1)}), bf16[32,64,128]{2,1,0:T(8,128)(2,1)}, u32[]{:S(2)}, u32[]{:S(2)}) async-start(bf16[32,64,128]{2,1,0:T(8,128)(2,1)} %bitcast.49), calls=%async_computation.2 | async-start | bytes 1048576 | tf_op jit(solution)/shard_map/all_to_all | solution.py:384
  79.2 1.5 %fusion.3 = (bf16[16,128]{1,0:T(8,128)(2,1)}, bf16[16,128]{1,0:T(8,128)(2,1)}) fusion(f32[32,128]{1,0:T(8,128)} %copy-done.17, f32[128,16]{0,1:T(8,128)S(1)} %copy-done.12, f32[128,16]{0,1:T(8,128)} %param.23), kind=kLoop, calls=%fused_computation.25 | loop fusion | flops 24576 | bytes 40960 | tf_op jit(solution)/shard_map/convert.4
  80.7 5.0 %all-to-all-done.2.carry_ref = bf16[32,64,128]{2,1,0:T(8,128)(2,1)} async-done(((bf16[32,64,128]{2,1,0:T(8,128)(2,1)}), bf16[32,64,128]{2,1,0:T(8,128)(2,1)}, u32[]{:S(2)}, u32[]{:S(2)}) %all-to-all-start.2) | async-done | bytes 524320 | tf_op jit(solution)/shard_map/all_to_all | solution.py:384
  85.7 1.8 %add_convert_fusion = bf16[32,9,128]{2,1,0:T(8,128)(2,1)} fusion(bf16[32,64,128]{2,1,0:T(8,128)(2,1)} %all-to-all-done.2.carry_ref), kind=kLoop, calls=%fused_computation.4 | loop fusion | flops 147456 | bytes 221184 | tf_op jit(solution)/shard_map/convert.6
  87.4 1.6 %concatenate.25 = bf16[288,128]{1,0:T(8,128)(2,1)} reshape(bf16[32,9,128]{2,1,0:T(8,128)(2,1)} %add_convert_fusion) | data formatting | bytes 147456 | tf_op jit(solution)/shard_map/concatenate | solution.py:393
  89.9 1.0 broadcast_in_dim.2
  90.9 12.5 %all-to-all-start.3 = ((bf16[8,320,128]{2,1,0:T(8,128)(2,1)}), bf16[8,320,128]{2,1,0:T(8,128)(2,1)}, u32[]{:S(2)}, u32[]{:S(2)}) async-start(bf16[8,320,128]{2,1,0:T(8,128)(2,1)} %broadcast_in_dim.2), calls=%async_computation.3 | async-start | bytes 1310720 | tf_op jit(solution)/shard_map/all_to_all | solution.py:395
  105.1 1.9 %collective-permute-start.1 = (bf16[8,4096]{1,0:T(8,128)(2,1)S(1)}, bf16[8,4096]{1,0:T(8,128)(2,1)S(1)}, u32[]{:S(2)}, u32[]{:S(2)}) collective-permute-start(bf16[8,4096]{1,0:T(8,128)(2,1)S(1)} %pad_maximum_fusion.2), channel_id=1, source_target_pairs={{8,0},{16,8},{24,16},{32,24},{40,32},{48,40},{56,48},{64,56},{72,6... | collective-permute-start | bytes 196616 | tf_op jit(solution)/shard_map/ppermute | solution.py:328
  107.0 16.2 %collective-permute-done.1 = bf16[8,4096]{1,0:T(8,128)(2,1)S(1)} collective-permute-done((bf16[8,4096]{1,0:T(8,128)(2,1)S(1)}, bf16[8,4096]{1,0:T(8,128)(2,1)S(1)}, u32[]{:S(2)}, u32[]{:S(2)}) %collective-permute-start.1) | collective-permute-done | bytes 65568 | tf_op jit(solution)/shard_map/ppermute | solution.py:328
  123.3 1.2 copy-done.6
  127.0 9.1 %finish.1 = (bf16[1,128,4096]{2,1,0:T(8,128)(2,1)}, bf16[1,128,4096]{2,1,0:T(8,128)(2,1)}, bf16[1,128,4096]{2,1,0:T(8,128)(2,1)}) custom-call(bf16[1,128,4096]{2,1,0:T(8,128)(2,1)S(1)} %copy-done, bf16[1,128,4096]{2,1,0:T(8,128)(2,1)S(1)} %copy-done.2, bf16[1,128,4096]{2,1,0:T(8,128)(2,1)S(1)} %copy-done.4, bf16[1,128,4096]{2,1,0:T(8,128)(2,1)S(1)} %copy-done.6, ...), custom_call_target="tpu_custom_call" | custom-call | tf_op jit(solution)/shard_map/finish/pallas_call | solution.py:399
  136.1 1.2 convert_reduce_fusion
  (60 shorter events, 16.1 us)
Async XLA Ops:
  0.6 18.5 %copy-start = (bf16[1,128,4096]{2,1,0:T(8,128)(2,1)S(1)}, bf16[1,128,4096]{2,1,0:T(8,128)(2,1)}, u32[]{:S(2)}) copy-start(bf16[1,128,4096]{2,1,0:T(8,128)(2,1)} %query_ref.3) | copy-start | bytes 3145732
  1.5 0.7 copy-start.11
  2.9 16.2 %all-to-all-start = ((bf16[32,32,128]{2,1,0:T(8,128)(2,1)}), bf16[32,32,128]{2,1,0:T(8,128)(2,1)S(1)}, u32[]{:S(2)}, u32[]{:S(2)}) async-start(bf16[32,32,128]{2,1,0:T(8,128)(2,1)} %get-tuple-element.18), calls=%async_computation | async-start | bytes 524288 | tf_op jit(solution)/shard_map/all_to_all | solution.py:341
  14.1 5.0 %collective-permute-start = (bf16[6,4096]{1,0:T(8,128)(2,1)S(1)}, bf16[6,4096]{1,0:T(8,128)(2,1)S(1)}, u32[]{:S(2)}, u32[]{:S(2)}) collective-permute-start(bf16[6,4096]{1,0:T(8,128)(2,1)S(1)} %pad_maximum_fusion.1), channel_id=1, source_target_pairs={{0,8},{8,16},{16,24},{24,32},{32,40},{40,48},{48,56},{56,64},{64,7... | collective-permute-start | bytes 147464 | tf_op jit(solution)/shard_map/ppermute | solution.py:327
  19.2 1.2 copy-start.1
  20.4 1.2 copy-start.3
  21.6 1.2 copy-start.5
  22.8 0.9 copy-start.9
  23.8 0.9 copy-start.10
  24.7 0.8 copy-start.13
  25.5 0.8 copy-start.14
  28.4 12.3 %copy-start.7 = (bf16[32,32,128]{2,1,0:T(8,128)(2,1)}, bf16[32,32,128]{2,1,0:T(8,128)(2,1)S(1)}, u32[]{:S(2)}) copy-start(bf16[32,32,128]{2,1,0:T(8,128)(2,1)S(1)} %all-to-all-done.coefs_ref) | copy-start | bytes 786436
  70.2 1.4 %copy-start.17 = (f32[32,128]{1,0:T(8,128)}, f32[32,128]{1,0:T(8,128)S(1)}, u32[]{:S(2)}) copy-start(f32[32,128]{1,0:T(8,128)S(1)} %get-tuple-element.29) | copy-start | bytes 49156
  71.6 14.1 %all-to-all-start.2 = ((bf16[32,64,128]{2,1,0:T(8,128)(2,1)}), bf16[32,64,128]{2,1,0:T(8,128)(2,1)}, u32[]{:S(2)}, u32[]{:S(2)}) async-start(bf16[32,64,128]{2,1,0:T(8,128)(2,1)} %bitcast.49), calls=%async_computation.2 | async-start | bytes 1048576 | tf_op jit(solution)/shard_map/all_to_all | solution.py:384
  79.1 44.1 %copy-start.2 = (bf16[1,128,4096]{2,1,0:T(8,128)(2,1)S(1)}, bf16[1,128,4096]{2,1,0:T(8,128)(2,1)}, u32[]{:S(2)}) copy-start(bf16[1,128,4096]{2,1,0:T(8,128)(2,1)} %key_ref.3) | copy-start | bytes 3145732
  79.1 44.1 %copy-start.4 = (bf16[1,128,4096]{2,1,0:T(8,128)(2,1)S(1)}, bf16[1,128,4096]{2,1,0:T(8,128)(2,1)}, u32[]{:S(2)}) copy-start(bf16[1,128,4096]{2,1,0:T(8,128)(2,1)} %value_ref.3) | copy-start | bytes 3145732
  79.1 44.1 %copy-start.21 = (bf16[8,48]{1,0:T(8,128)(2,1)S(1)}, bf16[8,48]{1,0:T(8,128)(2,1)}, u32[]{:S(2)}) copy-start(bf16[8,48]{1,0:T(8,128)(2,1)} %constant.41.clone.taps3_ref) | copy-start | bytes 2308
  79.2 44.1 %copy-start.22 = (bf16[8,32]{1,0:T(8,128)(2,1)S(1)}, bf16[8,32]{1,0:T(8,128)(2,1)}, u32[]{:S(2)}) copy-start(bf16[8,32]{1,0:T(8,128)(2,1)} %constant.42.clone.taps2_ref) | copy-start | bytes 1540
  90.9 45.2 %all-to-all-start.3 = ((bf16[8,320,128]{2,1,0:T(8,128)(2,1)}), bf16[8,320,128]{2,1,0:T(8,128)(2,1)}, u32[]{:S(2)}, u32[]{:S(2)}) async-start(bf16[8,320,128]{2,1,0:T(8,128)(2,1)} %broadcast_in_dim.2), calls=%async_computation.3 | async-start | bytes 1310720 | tf_op jit(solution)/shard_map/all_to_all | solution.py:395
  105.1 18.1 %collective-permute-start.1 = (bf16[8,4096]{1,0:T(8,128)(2,1)S(1)}, bf16[8,4096]{1,0:T(8,128)(2,1)S(1)}, u32[]{:S(2)}, u32[]{:S(2)}) collective-permute-start(bf16[8,4096]{1,0:T(8,128)(2,1)S(1)} %pad_maximum_fusion.2), channel_id=1, source_target_pairs={{8,0},{16,8},{24,16},{32,24},{40,32},{48,40},{56,48},{64,56},{72,6... | collective-permute-start | bytes 196616 | tf_op jit(solution)/shard_map/ppermute | solution.py:328
  123.3 1.2 copy-start.6
  124.5 0.9 copy-start.8
  125.5 0.8 copy-start.15
  126.2 0.8 copy-start.16
  (4 other events, 2.8 us)

commit v2 on v1

v2 whole, which is shorter than its diff:
```python
import math

import jax
import jax.numpy as jnp
import numpy as np
from jax import lax
from jax.experimental import pallas as pl
from jax.experimental.pallas import tpu as pltpu
from jax.sharding import PartitionSpec as P

BLOCK = 128
CENTRE = BLOCK // 2
TERMS = 10
SHORT_TERMS = 9
PRODUCTS = 9
SENT_ROWS = 128
EARLY_ROWS = 80
CARRY_ROWS = 48
TOP_RATE = 1.0 / 32.0
FREQS = 128
LANES = 128
BF16 = jnp.bfloat16
F32 = jnp.float32
VMEM_LIMIT = 60 * 1024 * 1024
SMALL_LIMIT = 16 * 1024 * 1024
WIDE = 1024


def decay_terms(times, terms=TERMS):
    points = 64
    theta = (np.arange(points) + 0.5) * np.pi / points
    rates = (np.cos(theta) + 1.0) * TOP_RATE / 2.0
    values = np.exp(-np.asarray(times, np.float64)[:, None] * rates[None, :])
    basis = np.cos(np.arange(terms)[None, :] * theta[:, None]) * (2.0 / points)
    basis[:, 0] *= 0.5
    return values @ basis


def halves(table):
    table = np.asarray(table, np.float32)
    high = table.astype(BF16)
    low = (table - high.astype(np.float32)).astype(BF16)
    return high, low


def paired(table):
    return np.concatenate(halves(table), axis=1)


def make_tables():
    t = np.arange(BLOCK)
    angle = 2.0 * np.pi / (2 * FREQS) * (np.arange(FREQS)[:, None] + 0.5) * t[None, :]
    fore = np.concatenate([np.cos(angle), -np.sin(angle)], axis=0)
    back = np.concatenate([np.cos(angle.T), -np.sin(angle.T)], axis=1) / FREQS
    ahead = decay_terms(t - CENTRE)
    behind = decay_terms(CENTRE - t)
    total = PRODUCTS * SHORT_TERMS
    product = np.zeros((total, PRODUCTS, BLOCK))
    for m in range(PRODUCTS):
        part = decay_terms(t - CENTRE if m < 3 else CENTRE - t, SHORT_TERMS).T
        product[m * SHORT_TERMS : (m + 1) * SHORT_TERMS, m] = part
    late = np.zeros((SENT_ROWS - EARLY_ROWS, 7 * BLOCK))
    high, low = halves(behind.T)
    late[1 : 1 + TERMS, : 2 * BLOCK] = np.concatenate([high, low], axis=1)
    high, low = halves(ahead.T)
    late[1 + TERMS : 1 + 2 * TERMS, 2 * BLOCK : 4 * BLOCK] = np.concatenate([high, low], axis=1)
    late[1 + 2 * TERMS : 1 + 3 * TERMS, 4 * BLOCK : 6 * BLOCK] = ahead.T @ back
    late[0, 6 * BLOCK :] = product[total - 1, PRODUCTS - 1]
    impulse_high, impulse_low = halves(fore @ ahead)
    taps = np.zeros((8, TERMS))
    taps[:3] = decay_terms([-CENTRE, 1 - CENTRE, -1 - CENTRE])
    edge = np.zeros((8, TERMS))
    edge[:2] = decay_terms([-CENTRE, -1 - CENTRE])

    def padded(table, repeat=0):
        out = np.zeros((table.shape[0], 16))
        out[:, :TERMS] = table
        out[:, TERMS : TERMS + repeat] = table[:, :repeat]
        return out

    first, second = decay_terms([-CENTRE, 1 - CENTRE])

    def tripled(table):
        high, low = halves(padded(table))
        return np.concatenate([high, high, low], axis=1)

    return dict(
        product=product[:EARLY_ROWS].reshape(EARLY_ROWS, PRODUCTS * BLOCK).astype(BF16),
        late=late.astype(BF16),
        fore=paired(fore),
        impulse=tripled(fore @ ahead),
        back=back.astype(BF16),
        ahead=paired(padded(ahead, 16 - TERMS)),
        behind=paired(padded(behind, 16 - TERMS)),
        taps=tripled(taps),
        edge=paired(padded(edge, 16 - TERMS)),
        first=[float(x) for x in first],
        second=[float(x) for x in second],
    )


def dot(left, right):
    return jnp.dot(left, right, preferred_element_type=F32)


def whole(shape):
    return pl.BlockSpec(shape, lambda *_: (0,) * len(shape))


def later_rows(values, before, by):
    moved = pltpu.roll(values, by, 0)
    top = moved[:8]
    row = lax.broadcasted_iota(jnp.int32, top.shape, 0)
    for i in range(by):
        top = jnp.where(row == i, before[2 - by + i : 3 - by + i], top)
    return jnp.concatenate([top, moved[8:]], axis=0)


def sooner_rows(values, after):
    count = values.shape[0]
    moved = pltpu.roll(values, count - 1, 0)
    row = lax.broadcasted_iota(jnp.int32, (8, values.shape[1]), 0)
    bottom = jnp.where(row == 7, after, moved[count - 8 :])
    return jnp.concatenate([moved[: count - 8], bottom], axis=0)


def lanes_of(ref, rows):
    return jnp.concatenate([ref[i, rows, :] for i in range(ref.shape[0])], axis=1)


def store_chunks(ref, start, rows):
    rows = rows.astype(BF16)
    for i in range(ref.shape[0]):
        ref[i, start : start + rows.shape[0], :] = rows[:, i * LANES : (i + 1) * LANES]


def edges_kernel(query_ref, key_ref, value_ref, cot_ref, query_end, key_end, value_end, last_ref, first_ref):
    ends = [ref[0].astype(F32)[14:] for ref in (query_end, key_end, value_end)]
    ends.append(jnp.zeros_like(ends[0]))
    last_ref[...] = jnp.concatenate(ends, axis=0)
    starts = [ref[0].astype(F32)[:2] for ref in (query_ref, key_ref, value_ref, cot_ref)]
    first_ref[...] = jnp.concatenate(starts, axis=0)


def prep_kernel(weight_ref, rate_ref, basis_ref, slope_ref, loaded_ref, spread_ref):
    weight, rate = weight_ref[...], rate_ref[...]
    centred = weight * jnp.exp(-float(CENTRE) * rate)
    spot = rate * (2.0 / TOP_RATE) - 1.0
    value, older = jnp.ones_like(spot), spot
    slope, older_slope = jnp.zeros_like(spot), jnp.zeros_like(spot)
    rows = []
    for k in range(TERMS):
        basis_ref[k] = value
        slope_ref[k] = slope * (-2.0 / TOP_RATE)
        loaded_ref[k] = value * weight
        rows.append(jnp.sum(value * centred, axis=0, keepdims=True))
        if k == 0:
            following, following_slope = spot, jnp.ones_like(spot)
        else:
            following = 2.0 * spot * value - older
            following_slope = 2.0 * value + 2.0 * spot * slope - older_slope
        older, older_slope = value, slope
        value, slope = following, following_slope
    rows.append(jnp.zeros((16 - TERMS, LANES), F32))
    coefs = jnp.concatenate(rows, axis=0)
    high = coefs.astype(BF16)
    low = (coefs - high.astype(F32)).astype(BF16)
    both = jnp.concatenate([high, low], axis=0)
    spread_ref[...] = jnp.broadcast_to(both[None], spread_ref.shape)


def block_kernel(
    query_ref, key_ref, value_ref, cot_ref, filter_ref, before_ref, coefs_ref,
    fore_ref, impulse_ref, back_ref, product_ref, late_ref,
    sent_ref, mixed_ref, grad_ref, key_short_ref, value_short_ref, products,
):
    before = before_ref[...]
    query, key, value = (ref[0].astype(F32) for ref in (query_ref, key_ref, value_ref))
    cot = cot_ref[0].astype(F32)

    def lagged(i, x):
        edge = before[2 * i : 2 * i + 2]
        return (x, later_rows(x, edge, 1), later_rows(x, edge, 2))

    def short(i, inputs):
        return sum(filter_ref[i, j : j + 1, :] * inputs[j] for j in range(3))

    queries, keys, values = lagged(0, query), lagged(1, key), lagged(2, value)
    key_short, value_short = short(1, keys), short(2, values)
    key_short_ref[...] = key_short.astype(BF16)
    value_short_ref[...] = value_short.astype(BF16)
    gated = (key_short * value_short).astype(BF16)
    grad_mixed = (cot * short(0, queries)).astype(BF16)
    for i, (left, inputs) in enumerate(((cot, queries), (value_short, keys), (key_short, values))):
        for j in range(3):
            start = (3 * i + j) * BLOCK
            products[start : start + BLOCK, :] = (left * inputs[j]).astype(BF16)

    gated_twice = jnp.concatenate([gated, gated], axis=0)
    grad_twice = jnp.concatenate([grad_mixed, grad_mixed], axis=0)
    u = dot(fore_ref[...], gated_twice)
    g = dot(fore_ref[...], grad_twice)
    coefs = lanes_of(coefs_ref, slice(None))
    h = dot(impulse_ref[...], jnp.concatenate([coefs, coefs[:16]], axis=0))
    ur, ui, gr, gi, hr, hi = (
        x[part * FREQS : (part + 1) * FREQS] for x in (u, g, h) for part in (0, 1)
    )

    def spectrum(real, imag):
        return jnp.concatenate([real.astype(BF16), imag.astype(BF16)], axis=0)

    mixed = dot(back_ref[...], spectrum(ur * hr - ui * hi, ur * hi + ui * hr))
    grad = dot(back_ref[...], spectrum(gr * hr + gi * hi, gi * hr - gr * hi))
    lags = spectrum(gr * ur + gi * ui, gi * ur - gr * ui)
    mixed_ref[...] = mixed.astype(BF16)
    grad_ref[...] = grad.astype(BF16)
    late = dot(
        late_ref[...],
        jnp.concatenate([gated_twice, grad_twice, lags, products[(PRODUCTS - 1) * BLOCK :, :]], axis=0),
    )
    row = lax.broadcasted_iota(jnp.int32, (16, late.shape[1]), 0)
    sums = late[32:48]
    for m in range(PRODUCTS):
        product = products[m * BLOCK : (m + 1) * BLOCK, :].astype(F32)
        local = jnp.sum(product * (mixed if m < 3 else grad), axis=0, keepdims=True)
        sums = jnp.where(row == m, local, sums)
    store_chunks(sent_ref, 0, dot(product_ref[...], products[...]))
    store_chunks(sent_ref, EARLY_ROWS, late[:32])
    store_chunks(sent_ref, EARLY_ROWS + 32, sums)


def owner_kernel(
    first, second, moments_ref, basis_ref, slope_ref, loaded_ref, rate_ref, root_ref, amount_ref,
    carry_ref, message_ref, ahead, behind,
):
    blocks = moments_ref.shape[1]
    modes = rate_ref.shape[0]
    row = lax.broadcasted_iota(jnp.int32, (blocks, LANES), 0)
    sum_u = PRODUCTS * SHORT_TERMS
    sum_g, lag, local = sum_u + TERMS, sum_u + 2 * TERMS, EARLY_ROWS + 32

    def later(x, by):
        return jnp.where(row >= by, pltpu.roll(x, by, 0), 0.0)

    def sooner(x, by):
        return jnp.where(row < blocks - by, pltpu.roll(x, blocks - by, 0), 0.0)

    lag_rows = [jnp.sum(moments_ref[lag + k], axis=0, keepdims=True) for k in range(TERMS)]
    first_rows, second_rows = [], []
    for n in range(modes):
        basis = [basis_ref[k, n : n + 1, :] for k in range(TERMS)]
        slope = [slope_ref[k, n : n + 1, :] for k in range(TERMS)]
        state = sum(basis[k] * moments_ref[sum_u + k] for k in range(TERMS))
        state_slope = sum(slope[k] * moments_ref[sum_u + k] for k in range(1, TERMS))
        grad = sum(basis[k] * moments_ref[sum_g + k] for k in range(TERMS))
        grad_slope = sum(slope[k] * moments_ref[sum_g + k] for k in range(1, TERMS))
        rate = rate_ref[n : n + 1, :]
        half = jnp.exp(-float(CENTRE) * rate)
        factor = half * half
        moved = later(state, 1)
        forward = factor * moved
        forward_slope = factor * (later(state_slope, 1) + float(BLOCK) * moved)
        backward = factor * sooner(grad, 1)
        by = 1
        while by < blocks:
            moved = later(forward, by)
            forward_slope = forward_slope + factor * (
                later(forward_slope, by) + float(BLOCK * by) * moved
            )
            forward = forward + factor * moved
            backward = backward + factor * sooner(backward, by)
            factor = factor * factor
            by *= 2
        ahead[n] = forward
        behind[n] = backward
        first_sum = jnp.sum(forward * grad, axis=0, keepdims=True)
        second_sum = jnp.sum(forward_slope * grad + forward * grad_slope, axis=0, keepdims=True)
        near = half * sum(basis[k] * lag_rows[k] for k in range(TERMS))
        near_slope = half * sum(slope[k] * lag_rows[k] for k in range(1, TERMS))
        first_rows.append(first_sum + near)
        second_rows.append(second_sum + near_slope + float(CENTRE) * near)
    totals = [moments_ref[local + m] for m in range(PRODUCTS)]
    edge_one, edge_two = 0.0, 0.0
    for k in range(TERMS):
        carry = sum(loaded_ref[k, n : n + 1, :] * ahead[n] for n in range(modes))
        back = sum(loaded_ref[k, n : n + 1, :] * behind[n] for n in range(modes))
        for start, value in ((0, carry), (16, back)):
            high = value.astype(BF16)
            carry_ref[start + k] = high
            if k < 16 - TERMS:
                carry_ref[start + TERMS + k] = (value - high.astype(F32)).astype(BF16)
        edge_one = edge_one + first[k] * carry
        edge_two = edge_two + second[k] * carry
        if k < SHORT_TERMS:
            for m in range(PRODUCTS):
                totals[m] = totals[m] + (carry if m < 3 else back) * moments_ref[m * SHORT_TERMS + k]
    carry_ref[32] = sooner(edge_one, 1).astype(BF16)
    carry_ref[33] = sooner(edge_two, 1).astype(BF16)
    root, amount = root_ref[...], amount_ref[...]
    first_sum = jnp.concatenate(first_rows, axis=0)
    second_sum = jnp.concatenate(second_rows, axis=0)
    rate = rate_ref[...]
    steep = amount * (jnp.exp(-2.0 * rate) / root * first_sum - root * second_sum)
    for i in range(34, CARRY_ROWS):
        carry_ref[i] = jnp.zeros((blocks, LANES), BF16)
    rows = [jnp.zeros((2, LANES), F32)]
    rows.extend(jnp.sum(total, axis=0, keepdims=True) for total in totals)
    rows.append(jnp.zeros((14 - PRODUCTS, LANES), F32))
    message = jnp.concatenate([*rows, root * first_sum, rate * steep], axis=0).astype(BF16)
    message_ref[...] = jnp.broadcast_to(message[None], message_ref.shape)


def total_kernel(factor, message_ref, carry_ref, sent_ref, residue_ref, decay_ref):
    total = message_ref[0].astype(F32)
    for i in range(1, message_ref.shape[0]):
        total = total + message_ref[i].astype(F32)
    total = total * factor
    modes = residue_ref.shape[1]
    residue_ref[...] = total[16 : 16 + modes].T
    decay_ref[...] = total[16 + modes :].T
    shared = total[:16]
    for block in range(sent_ref.shape[0]):
        sent_ref[block, :32, :] = carry_ref[block, :32, :]
        sent_ref[block, 32:48, :] = (carry_ref[block, 32:48, :].astype(F32) + shared).astype(BF16)


def finish_kernel(
    cot_ref, query_end, key_end, value_end, filter_ref, after_ref, coefs_ref, key_short_ref, value_short_ref,
    mixed_ref, grad_ref, carry_ref, ahead_ref, behind_ref, edge_ref, taps_ref,
    query_out, key_out, value_out, filter_out,
):
    after = after_ref[...]

    def tap(i, j):
        return filter_ref[i, j : j + 1, :]

    def rounded(x):
        return x.astype(BF16).astype(F32)

    def short_after(i, ref):
        last, following = ref[0].astype(F32)[14:], after[2 * i : 2 * i + 2]
        middle = jnp.concatenate([last[1:2], following[0:1]], axis=0)
        return tap(i, 0) * following + tap(i, 1) * middle + tap(i, 2) * last

    ahead = lanes_of(carry_ref, slice(0, 16))
    behind = lanes_of(carry_ref, slice(16, 32))
    rest = lanes_of(carry_ref, slice(32, 48)).astype(F32)
    for m in range(PRODUCTS):
        filter_out[m // 3, m % 3 : m % 3 + 1, :] = rest[2 + m : 3 + m]
    behind_twice = jnp.concatenate([behind, behind], axis=0)
    mixed = mixed_ref[...].astype(F32) + dot(ahead_ref[...], jnp.concatenate([ahead, ahead], axis=0))
    grad = grad_ref[...].astype(F32) + dot(behind_ref[...], behind_twice)
    mixed, grad = rounded(mixed), rounded(grad)

    coefs = lanes_of(coefs_ref, slice(None))
    impulse = dot(taps_ref[...], jnp.concatenate([coefs, coefs[:16]], axis=0))
    edge = dot(edge_ref[...], behind_twice)
    query_next, key_next, value_next = (
        short_after(i, ref) for i, ref in enumerate((query_end, key_end, value_end))
    )
    gated_next = rounded(key_next * value_next)
    grad_mixed_next = rounded(after[6:7] * query_next[0:1])
    mixed_next = (
        rounded(rest[0:1] + impulse[0:1] * gated_next[0:1]),
        rounded(rest[1:2] + impulse[0:1] * gated_next[1:2] + impulse[1:2] * gated_next[0:1]),
    )
    grad_next = rounded(edge[0:1]), rounded(edge[1:2] - impulse[2:3] * grad_mixed_next)

    cot = cot_ref[0].astype(F32)
    for i, (out_ref, left, right, left_next, right_next) in enumerate(
        (
            (query_out, cot, mixed, after[6:8], mixed_next),
            (key_out, value_short_ref[...].astype(F32), grad, value_next, grad_next),
            (value_out, key_short_ref[...].astype(F32), grad, key_next, grad_next),
        )
    ):
        zero, one, two = (tap(i, j) for j in range(3))
        here = left * right
        following = left_next[0:1] * right_next[0]
        inner = one * here + sooner_rows(two * here, two * following)
        inner_after = one * following + two * (left_next[1:2] * right_next[1])
        out_ref[0] = (zero * here + sooner_rows(inner, inner_after)).astype(BF16)


def body(query_rows, key_rows, value_rows, cotangent, short_filter, residue, decay_rate):
    width = query_rows.shape[2]
    blocks = lax.axis_size("seq")
    groups = lax.axis_size("dp")
    modes = residue.shape[1]
    length = BLOCK * blocks
    wide = min(WIDE, width)
    parts = wide // LANES
    grid = (width // wide,)
    tables = make_tables()
    first, second = tables.pop("first"), tables.pop("second")
    tables = {name: jnp.asarray(table) for name, table in tables.items()}
    params = pltpu.CompilerParams(vmem_limit_bytes=VMEM_LIMIT)
    small_params = pltpu.CompilerParams(vmem_limit_bytes=SMALL_LIMIT)

    def shape(*dims, dtype=F32):
        return jax.ShapeDtypeStruct(dims, dtype)

    top = pl.BlockSpec((1, 16, width), lambda c: (0, 0, 0))
    end = pl.BlockSpec((1, 16, width), lambda c: (0, BLOCK // 16 - 1, 0))
    last, front = pl.pallas_call(
        edges_kernel,
        grid=(1,),
        in_specs=[top] * 4 + [end] * 3,
        out_specs=(whole((8, width)), whole((8, width))),
        out_shape=(shape(8, width), shape(8, width)),
        compiler_params=params,
        name="edges",
    )(query_rows, key_rows, value_rows, cotangent, query_rows, key_rows, value_rows)
    before = lax.ppermute(last, "seq", [(i, i + 1) for i in range(blocks - 1)])
    after = lax.ppermute(front, "seq", [(i + 1, i) for i in range(blocks - 1)])

    root = jnp.sqrt(-jnp.expm1(-2.0 * decay_rate))
    weight_t = (residue * root).T
    rate_t = decay_rate.T
    small = shape(TERMS, modes, LANES)
    basis, slope, loaded, spread = pl.pallas_call(
        prep_kernel,
        out_shape=(small, small, small, shape(blocks, 32, LANES, dtype=BF16)),
        compiler_params=params,
        name="prep",
    )(weight_t, rate_t)
    coefs = lax.all_to_all(spread, "seq", 0, 0, tiled=True)

    tall = pl.BlockSpec((1, BLOCK, wide), lambda c: (0, 0, c))
    tall_end = pl.BlockSpec((1, 16, wide), lambda c: (0, BLOCK // 16 - 1, c))
    filters = pl.BlockSpec((3, 3, wide), lambda c: (0, 0, c))

    def flat(rows):
        return pl.BlockSpec((rows, wide), lambda c: (0, c))

    def chunks(rows):
        return pl.BlockSpec((parts, rows, LANES), lambda c: (c, 0, 0))

    def table_specs(names):
        return [whole(tables[name].shape) for name in names]

    names = ("fore", "impulse", "back", "product", "late")
    half = shape(BLOCK, width, dtype=BF16)
    sent, mixed, grad, key_short, value_short = pl.pallas_call(
        block_kernel,
        grid=grid,
        in_specs=[tall] * 4 + [filters, flat(8), chunks(32)] + table_specs(names),
        out_specs=(chunks(SENT_ROWS), *[flat(BLOCK)] * 4),
        out_shape=(shape(blocks, SENT_ROWS, LANES, dtype=BF16), half, half, half, half),
        scratch_shapes=[pltpu.VMEM((PRODUCTS * BLOCK, wide), BF16)],
        compiler_params=params,
        name="block",
    )(
        query_rows, key_rows, value_rows, cotangent, short_filter, before, coefs,
        *[tables[name] for name in names],
    )
    moments = lax.all_to_all(sent, "seq", 0, 0, tiled=True)
    moments = moments.transpose(1, 0, 2).astype(F32)

    carry, message = pl.pallas_call(
        lambda *refs: owner_kernel(first, second, *refs),
        out_shape=(
            shape(CARRY_ROWS, blocks, LANES, dtype=BF16),
            shape(groups, 16 + 2 * modes, LANES, dtype=BF16),
        ),
        scratch_shapes=[pltpu.VMEM((modes, blocks, LANES), F32)] * 2,
        compiler_params=small_params,
        name="owner",
    )(moments, basis, slope, loaded, rate_t, root.T, residue.T)
    message = lax.all_to_all(message, "dp", 0, 0, tiled=True)
    factor = 1.0 / math.sqrt(query_rows.shape[0] * groups * length)
    sent, residue_grad, decay_grad = pl.pallas_call(
        lambda *refs: total_kernel(factor, *refs),
        out_shape=(shape(blocks, CARRY_ROWS, LANES, dtype=BF16), shape(LANES, modes), shape(LANES, modes)),
        compiler_params=small_params,
        name="total",
    )(message, carry.transpose(1, 0, 2))
    carry = lax.all_to_all(sent, "seq", 0, 0, tiled=True)

    names = ("ahead", "behind", "edge", "taps")
    *outs, filter_grad = pl.pallas_call(
        finish_kernel,
        grid=grid,
        in_specs=[tall] + [tall_end] * 3 + [filters, flat(8), chunks(32)] + [flat(BLOCK)] * 4
        + [chunks(CARRY_ROWS)] + table_specs(names),
        out_specs=[tall] * 3 + [filters],
        out_shape=[jax.ShapeDtypeStruct(query_rows.shape, BF16)] * 3 + [shape(3, 3, width)],
        compiler_params=params,
        name="finish",
    )(
        cotangent, query_rows, key_rows, value_rows, short_filter, after, coefs, key_short, value_short,
        mixed, grad, carry, *[tables[name] for name in names],
    )
    return (*outs, filter_grad, residue_grad, decay_grad)


def solution(mesh):
    rows = P("dp", "seq", None)
    return jax.shard_map(
        body,
        mesh=mesh,
        in_specs=(rows, rows, rows, rows, P(), P("seq", None), P("seq", None)),
        out_specs=(rows, rows, rows, P(), P("seq", None), P("seq", None)),
        check_vma=False,
    )
```

time: 140 us -> 106 us (0.76)
  the two profiles are of different devices: /device:TPU:31 before, /device:TPU:30 now
where the time goes in v2:
time: 106 us; the launch traced here: 105 us
  starting transfers between devices  29.6 us (28%)
  Pallas kernels  29.2 us (28%)
  blocking collectives  20.7 us (20%)
  waiting for transfers between devices  19.3 us (18%)
  local copies, waits for them, and re-layouts  3.99 us (4%)
  other arithmetic  1.95 us (2%)
    all_to_all x1, blocking collectives, body(): moments = lax.all_to_all(sent, 'seq', 0, 0, tiled=True)  20.7 us
    pallas_call x1, Pallas kernels, body(): pl.pallas_call(block_kernel, grid=grid, in_specs=[tall] * 4 + [filters, f...  15 us
    all_to_all x1, waiting for transfers between devices, body(): message = lax.all_to_all(message, 'dp', 0, 0, tiled=True)  8.58 us
    all_to_all x1, starting transfers between devices, body(): coefs = lax.all_to_all(spread, 'seq', 0, 0, tiled=True)  8.58 us
    all_to_all x1, starting transfers between devices, body(): message = lax.all_to_all(message, 'dp', 0, 0, tiled=True)  7.56 us
    all_to_all x1, starting transfers between devices, body(): carry = lax.all_to_all(sent, 'seq', 0, 0, tiled=True)  7.35 us
    pallas_call x1, Pallas kernels, body(): pl.pallas_call(finish_kernel, grid=grid, in_specs=[tall] + [tall_end] * 3...  7.26 us
    ppermute x1, waiting for transfers between devices, body(): after = lax.ppermute(front, 'seq', [(i + 1, i) for i in range(blocks - 1)])  6.97 us
  transfers between devices with their start and end apart: 5, of which 3 were waited for; matrix products, arithmetic and copies ran while one was open for 1% of the time, Pallas kernels for 2%

profile of v2, /device:TPU:30, one launch (start us, length us, event | category | flops | bytes accessed | tf_op | source)
XLA Modules:
  0.0 105.4 jit_solution(8535036132583034546)
XLA Ops:
  0.6 1.3 %fusion = (f32[16,128]{1,0:T(8,128)S(1)}, f32[16,128]{1,0:T(8,128)}) fusion(f32[128,16]{0,1:T(8,128)} %param.22, f32[128,16]{0,1:T(8,128)} %param.21), kind=kLoop, calls=%fused_computation.4 | loop fusion | flops 6144 | bytes 32768 | tf_op jit(solution)/shard_map/transpose | solution.py:469
  2.0 1.5 %prep.1 = (f32[10,16,128]{2,1,0:T(8,128)}, f32[10,16,128]{2,1,0:T(8,128)}, f32[10,16,128]{2,1,0:T(8,128)}, bf16[32,32,128]{2,1,0:T(8,128)(2,1)}) custom-call(f32[16,128]{1,0:T(8,128)} %get-tuple-element.59.weight_ref, f32[16,128]{1,0:T(8,128)} %bitcast.12), custom_call_target="tpu_custom_call" | custom-call | tf_op jit(solution)/shard_map/prep/pallas_call | solution.py:421
  3.5 8.6 %all-to-all-start = ((bf16[32,32,128]{2,1,0:T(8,128)(2,1)}), bf16[32,32,128]{2,1,0:T(8,128)(2,1)S(1)}, u32[]{:S(2)}, u32[]{:S(2)}) async-start(bf16[32,32,128]{2,1,0:T(8,128)(2,1)} %get-tuple-element.27), calls=%async_computation | async-start | bytes 524288 | tf_op jit(solution)/shard_map/all_to_all | solution.py:427
  12.1 2.0 %edges.1 = (f32[8,4096]{1,0:T(8,128)}, f32[8,4096]{1,0:T(8,128)}) custom-call(bf16[1,128,4096]{2,1,0:T(8,128)(2,1)} %query_end.3, bf16[1,128,4096]{2,1,0:T(8,128)(2,1)} %key_end.3, bf16[1,128,4096]{2,1,0:T(8,128)(2,1)} %value_end.3, bf16[1,128,4096]{2,1,0:T(8,128)(2,1)} %cot_ref.5, bf16[1,128,4096]{2,1,0:T(8,128)(2,1)} %query_end.3, ...), custom_call_target="tpu_custom_call" | custom-call | tf_op jit(solution)/shard_map/edges/pallas_call | solution.py:405
  14.1 3.4 %collective-permute-start.1 = (f32[8,4096]{1,0:T(8,128)}, f32[8,4096]{1,0:T(8,128)S(1)}, u32[]{:S(2)}, u32[]{:S(2)}) collective-permute-start(f32[8,4096]{1,0:T(8,128)} %get-tuple-element.28), channel_id=1, source_target_pairs={{0,8},{8,16},{16,24},{24,32},{32,40},{40,48},{48,56},{56,64},{64,7... | collective-permute-start | bytes 393224 | tf_op jit(solution)/shard_map/ppermute | solution.py:414
  17.4 3.7 %collective-permute-done.1.before_ref = f32[8,4096]{1,0:T(8,128)S(1)} collective-permute-done((f32[8,4096]{1,0:T(8,128)}, f32[8,4096]{1,0:T(8,128)S(1)}, u32[]{:S(2)}, u32[]{:S(2)}) %collective-permute-start.1) | collective-permute-done | bytes 131104 | tf_op jit(solution)/shard_map/ppermute | solution.py:414
  21.1 0.7 copy-done.8
  21.8 0.7 copy-done.5
  22.5 15.0 %block.1 = (bf16[32,128,128]{2,1,0:T(8,128)(2,1)}, bf16[128,4096]{1,0:T(8,128)(2,1)}, bf16[128,4096]{1,0:T(8,128)(2,1)}, bf16[128,4096]{1,0:T(8,128)(2,1)}, bf16[128,4096]{1,0:T(8,128)(2,1)}) custom-call(bf16[1,128,4096]{2,1,0:T(8,128)(2,1)} %query_end.3, bf16[1,128,4096]{2,1,0:T(8,128)(2,1)} %key_end.3, bf16[1,128,4096]{2,1,0:T(8,128)(2,1)} %value_end.3, ...), custom_call_target="tpu_custom_call" | custom-call | tf_op jit(solution)/shard_map/block/pallas_call | solution.py:444
  37.5 20.7 %all_to_all.20 = bf16[32,128,128]{2,1,0:T(8,128)(2,1)S(1)} all-to-all(bf16[32,128,128]{2,1,0:T(8,128)(2,1)} %get-tuple-element.33), channel_id=1, replica_groups=mesh['seq'=32,'dp'=8] {'seq'}, dimensions={0} | all-to-all | bytes 2097152 | tf_op jit(solution)/shard_map/all_to_all | solution.py:457
  58.2 0.6 convert_bitcast_fusion.refs_0_
  58.9 0.2 copy-done
  59.2 2.7 %owner.1 = (bf16[48,32,128]{2,1,0:T(8,128)(2,1)S(1)}, bf16[8,48,128]{2,1,0:T(8,128)(2,1)}) custom-call(f32[128,32,128]{2,1,0:T(8,128)S(1)} %convert_bitcast_fusion.refs_0_, f32[10,16,128]{2,1,0:T(8,128)S(1)} %copy-done, f32[10,16,128]{2,1,0:T(8,128)S(1)} %copy-done.1, f32[10,16,128]{2,1,0:T(8,128)S(1)} %copy-done.2, f32[16,128]{1,0:T(8,128)S(1)} %bitcast.13, ...), custom_call_target="tpu_custom_call" | custom-call | tf_op jit(solution)/shard_map/owner/pallas_call | solution.py:460
  61.8 7.6 %all-to-all-start.2 = ((bf16[8,48,128]{2,1,0:T(8,128)(2,1)}), bf16[8,48,128]{2,1,0:T(8,128)(2,1)S(1)}, u32[]{:S(2)}, u32[]{:S(2)}) async-start(bf16[8,48,128]{2,1,0:T(8,128)(2,1)} %get-tuple-element.37), calls=%async_computation.2 | async-start | bytes 196608 | tf_op jit(solution)/shard_map/all_to_all | solution.py:470
  69.4 0.2 copy.32
  69.6 8.6 %all-to-all-done.2.refs_0_ = bf16[8,48,128]{2,1,0:T(8,128)(2,1)S(1)} async-done(((bf16[8,48,128]{2,1,0:T(8,128)(2,1)}), bf16[8,48,128]{2,1,0:T(8,128)(2,1)S(1)}, u32[]{:S(2)}, u32[]{:S(2)}) %all-to-all-start.2) | async-done | bytes 98336 | tf_op jit(solution)/shard_map/all_to_all | solution.py:470
  78.2 0.8 total.1
  78.9 7.3 %all-to-all-start.3 = ((bf16[32,48,128]{2,1,0:T(8,128)(2,1)}), bf16[32,48,128]{2,1,0:T(8,128)(2,1)S(1)}, u32[]{:S(2)}, u32[]{:S(2)}) async-start(bf16[32,48,128]{2,1,0:T(8,128)(2,1)} %get-tuple-element.39), calls=%async_computation.3 | async-start | bytes 786432 | tf_op jit(solution)/shard_map/all_to_all | solution.py:478
  86.3 2.8 %collective-permute-start = (f32[8,4096]{1,0:T(8,128)S(1)}, f32[8,4096]{1,0:T(8,128)S(1)}, u32[]{:S(2)}, u32[]{:S(2)}) collective-permute-start(f32[8,4096]{1,0:T(8,128)S(1)} %copy-done.9), channel_id=1, source_target_pairs={{8,0},{16,8},{24,16},{32,24},{40,32},{48,40},{56,48},{64,56},{72,6... | collective-permute-start | bytes 393224 | tf_op jit(solution)/shard_map/ppermute | solution.py:415
  89.1 0.7 copy.28
  89.7 0.7 copy.29
  90.4 7.0 %collective-permute-done.after_ref = f32[8,4096]{1,0:T(8,128)S(1)} collective-permute-done((f32[8,4096]{1,0:T(8,128)S(1)}, f32[8,4096]{1,0:T(8,128)S(1)}, u32[]{:S(2)}, u32[]{:S(2)}) %collective-permute-start) | collective-permute-done | bytes 131104 | tf_op jit(solution)/shard_map/ppermute | solution.py:415
  97.4 0.6 copy-done.7
  98.2 7.3 %finish.1 = (bf16[1,128,4096]{2,1,0:T(8,128)(2,1)}, bf16[1,128,4096]{2,1,0:T(8,128)(2,1)}, bf16[1,128,4096]{2,1,0:T(8,128)(2,1)}, f32[3,3,4096]{2,1,0:T(4,128)}) custom-call(bf16[1,128,4096]{2,1,0:T(8,128)(2,1)} %cot_ref.5, bf16[1,128,4096]{2,1,0:T(8,128)(2,1)} %query_end.3, bf16[1,128,4096]{2,1,0:T(8,128)(2,1)} %key_end.3, bf16[1,128,4096]{2,1,0:T(8,128)(2,1)} %value_end.3, ...), custom_call_target="tpu_custom_call" | custom-call | tf_op jit(solution)/shard_map/finish/pallas_call | solution.py:481
  (18 shorter events, 0.3 us)
Async XLA Ops:
  3.5 17.6 %all-to-all-start = ((bf16[32,32,128]{2,1,0:T(8,128)(2,1)}), bf16[32,32,128]{2,1,0:T(8,128)(2,1)S(1)}, u32[]{:S(2)}, u32[]{:S(2)}) async-start(bf16[32,32,128]{2,1,0:T(8,128)(2,1)} %get-tuple-element.27), calls=%async_computation | async-start | bytes 524288 | tf_op jit(solution)/shard_map/all_to_all | solution.py:427
  14.1 7.1 %collective-permute-start.1 = (f32[8,4096]{1,0:T(8,128)}, f32[8,4096]{1,0:T(8,128)S(1)}, u32[]{:S(2)}, u32[]{:S(2)}) collective-permute-start(f32[8,4096]{1,0:T(8,128)} %get-tuple-element.28), channel_id=1, source_target_pairs={{0,8},{8,16},{16,24},{24,32},{32,40},{40,48},{48,56},{56,64},{64,7... | collective-permute-start | bytes 393224 | tf_op jit(solution)/shard_map/ppermute | solution.py:414
  21.1 0.7 copy-start.8
  21.8 0.7 copy-start.5
  58.2 0.9 copy-start
  58.2 0.9 copy-start.1
  58.2 1.0 copy-start.2
  58.2 1.0 copy-start.3
  58.2 1.0 copy-start.4
  59.2 27.1 %copy-start.9 = (f32[8,4096]{1,0:T(8,128)S(1)}, f32[8,4096]{1,0:T(8,128)}, u32[]{:S(2)}) copy-start(f32[8,4096]{1,0:T(8,128)} %get-tuple-element.26) | copy-start | bytes 393220
  61.8 16.3 %all-to-all-start.2 = ((bf16[8,48,128]{2,1,0:T(8,128)(2,1)}), bf16[8,48,128]{2,1,0:T(8,128)(2,1)S(1)}, u32[]{:S(2)}, u32[]{:S(2)}) async-start(bf16[8,48,128]{2,1,0:T(8,128)(2,1)} %get-tuple-element.37), calls=%async_computation.2 | async-start | bytes 196608 | tf_op jit(solution)/shard_map/all_to_all | solution.py:470
  78.9 18.5 %all-to-all-start.3 = ((bf16[32,48,128]{2,1,0:T(8,128)(2,1)}), bf16[32,48,128]{2,1,0:T(8,128)(2,1)S(1)}, u32[]{:S(2)}, u32[]{:S(2)}) async-start(bf16[32,48,128]{2,1,0:T(8,128)(2,1)} %get-tuple-element.39), calls=%async_computation.3 | async-start | bytes 786432 | tf_op jit(solution)/shard_map/all_to_all | solution.py:478
  86.3 11.1 %collective-permute-start = (f32[8,4096]{1,0:T(8,128)S(1)}, f32[8,4096]{1,0:T(8,128)S(1)}, u32[]{:S(2)}, u32[]{:S(2)}) collective-permute-start(f32[8,4096]{1,0:T(8,128)S(1)} %copy-done.9), channel_id=1, source_target_pairs={{8,0},{16,8},{24,16},{32,24},{40,32},{48,40},{56,48},{64,56},{72,6... | collective-permute-start | bytes 393224 | tf_op jit(solution)/shard_map/ppermute | solution.py:415
  97.4 0.6 copy-start.7
  97.4 0.8 copy-start.6

commit v3 on v2

v3 whole, which is shorter than its diff:
```python
import math

import jax
import jax.numpy as jnp
import numpy as np
from jax import lax
from jax.experimental import pallas as pl
from jax.experimental.pallas import tpu as pltpu
from jax.sharding import PartitionSpec as P

BLOCK = 128
CENTRE = BLOCK // 2
TERMS = 10
SHORT_TERMS = 9
PRODUCTS = 9
SENT_ROWS = 128
LAG_ROW = PRODUCTS * SHORT_TERMS
SUM_ROW = 96
CARRY_ROWS = 48
TOP_RATE = 1.0 / 32.0
FREQS = 128
LANES = 128
BF16 = jnp.bfloat16
F32 = jnp.float32
VMEM_LIMIT = 63 * 1024 * 1024
FULL_LIMIT = 64 * 1024 * 1024 - 65536
SMALL_LIMIT = 16 * 1024 * 1024
WIDE = 1024
INNER = 256
SKEW = 2
ORDERED = False


def decay_terms(times, terms=TERMS):
    points = 64
    theta = (np.arange(points) + 0.5) * np.pi / points
    rates = (np.cos(theta) + 1.0) * TOP_RATE / 2.0
    values = np.exp(-np.asarray(times, np.float64)[:, None] * rates[None, :])
    basis = np.cos(np.arange(terms)[None, :] * theta[:, None]) * (2.0 / points)
    basis[:, 0] *= 0.5
    return values @ basis


def halves(table):
    table = np.asarray(table, np.float32)
    high = table.astype(BF16)
    low = (table - high.astype(np.float32)).astype(BF16)
    return high, low


def paired(table):
    return np.concatenate(halves(table), axis=1)


def make_tables():
    t = np.arange(BLOCK)
    angle = 2.0 * np.pi / (2 * FREQS) * (np.arange(FREQS)[:, None] + 0.5) * t[None, :]
    fore = np.concatenate([np.cos(angle), -np.sin(angle)], axis=0)
    back = np.concatenate([np.cos(angle.T), -np.sin(angle.T)], axis=1) / FREQS
    ahead = decay_terms(t - CENTRE)
    behind = decay_terms(CENTRE - t)
    moments = np.zeros((SUM_ROW, (PRODUCTS + 2) * BLOCK))
    for m in range(PRODUCTS):
        part = decay_terms(t - CENTRE if m < 3 else CENTRE - t, SHORT_TERMS).T
        rows = slice(m * SHORT_TERMS, (m + 1) * SHORT_TERMS)
        moments[rows, m * BLOCK : (m + 1) * BLOCK] = part
    moments[LAG_ROW : LAG_ROW + TERMS, PRODUCTS * BLOCK :] = ahead.T @ back
    blank = np.zeros((16 - TERMS, BLOCK))
    taps = np.zeros((16, TERMS))
    taps[:3] = decay_terms([-CENTRE, 1 - CENTRE, -1 - CENTRE])
    edge = np.zeros((16, TERMS))
    edge[:2] = decay_terms([-CENTRE, -1 - CENTRE])

    def padded(table, repeat=0):
        out = np.zeros((table.shape[0], 16))
        out[:, :TERMS] = table
        out[:, TERMS : TERMS + repeat] = table[:, :repeat]
        return out

    first, second = decay_terms([-CENTRE, 1 - CENTRE])

    def tripled(table):
        high, low = halves(padded(table))
        return np.concatenate([high, high, low], axis=1)

    carried = np.zeros((2 * BLOCK + 16, 64))
    carried[:BLOCK, :32] = paired(padded(ahead, 16 - TERMS))
    carried[BLOCK : 2 * BLOCK, 32:] = paired(padded(behind, 16 - TERMS))
    carried[2 * BLOCK :, 32:] = paired(padded(edge, 16 - TERMS))
    return dict(
        moments=moments.astype(BF16),
        fore_u=paired(np.concatenate([fore, behind.T, blank], axis=0)),
        fore_g=paired(np.concatenate([fore, ahead.T, blank], axis=0)),
        impulse=tripled(np.concatenate([fore @ ahead, taps], axis=0)),
        back=back.astype(BF16),
        carried=carried.astype(BF16),
        first=[float(x) for x in first],
        second=[float(x) for x in second],
    )


def dot(left, right):
    return jnp.dot(left, right, preferred_element_type=F32)


def whole(shape):
    return pl.BlockSpec(shape, lambda *_: (0,) * len(shape))


def later_rows(values, before, by):
    moved = pltpu.roll(values, by, 0)
    top = moved[:8]
    row = lax.broadcasted_iota(jnp.int32, top.shape, 0)
    for i in range(by):
        top = jnp.where(row == i, before[2 - by + i : 3 - by + i], top)
    return jnp.concatenate([top, moved[8:]], axis=0)


def sooner_rows(values, after):
    count = values.shape[0]
    moved = pltpu.roll(values, count - 1, 0)
    row = lax.broadcasted_iota(jnp.int32, (8, values.shape[1]), 0)
    bottom = jnp.where(row == 7, after, moved[count - 8 :])
    return jnp.concatenate([moved[: count - 8], bottom], axis=0)


def lanes_of(ref, rows, chunks):
    return jnp.concatenate([ref[i, rows, :] for i in range(chunks.start, chunks.stop)], axis=1)


def store_chunks(ref, chunks, start, rows):
    rows = rows.astype(BF16)
    for i in range(chunks.stop - chunks.start):
        ref[chunks.start + i, start : start + rows.shape[0], :] = rows[:, i * LANES : (i + 1) * LANES]


def edge_rows(skip, refs):
    rows = [ref[0].astype(F32)[skip : skip + 2] for ref in refs]
    rows.extend([jnp.zeros_like(rows[0])] * (4 - len(rows)))
    return jnp.concatenate(rows, axis=0).astype(BF16)


def front_kernel(*refs):
    refs[-1][...] = edge_rows(0, refs[:-1])


def prep_kernel(
    amount_ref, rate_ref, query_ref, key_ref, value_ref,
    root_ref, basis_ref, slope_ref, loaded_ref, spread_ref, last_ref,
):
    last_ref[...] = edge_rows(14, (query_ref, key_ref, value_ref))
    amount, rate = amount_ref[...], rate_ref[...]
    square = rate * rate
    sinh = rate * (1.0 + square * (1.0 / 6.0 + square * (1.0 / 120.0)))
    root = jnp.sqrt(2.0 * jnp.exp(-rate) * sinh)
    root_ref[...] = root
    weight = amount * root
    centred = weight * jnp.exp(-float(CENTRE) * rate)
    spot = rate * (2.0 / TOP_RATE) - 1.0
    value, older = jnp.ones_like(spot), spot
    slope, older_slope = jnp.zeros_like(spot), jnp.zeros_like(spot)
    rows = []
    for k in range(TERMS):
        basis_ref[k] = value
        slope_ref[k] = slope * (-2.0 / TOP_RATE)
        loaded_ref[k] = value * weight
        rows.append(jnp.sum(value * centred, axis=0, keepdims=True))
        if k == 0:
            following, following_slope = spot, jnp.ones_like(spot)
        else:
            following = 2.0 * spot * value - older
            following_slope = 2.0 * value + 2.0 * spot * slope - older_slope
        older, older_slope = value, slope
        value, slope = following, following_slope
    rows.append(jnp.zeros((16 - TERMS, LANES), F32))
    coefs = jnp.concatenate(rows, axis=0)
    high = coefs.astype(BF16)
    low = (coefs - high.astype(F32)).astype(BF16)
    both = jnp.concatenate([high, low], axis=0)
    spread_ref[...] = jnp.broadcast_to(both[None], spread_ref.shape)


def interleave(waiting, skew):
    active, turn = [], 0
    while waiting or active:
        if waiting and turn % skew == 0:
            active.append(waiting.pop(0))
        for steps in list(active):
            if next(steps, active) is active:
                active.remove(steps)
        turn += 1


def block_kernel(
    query_ref, key_ref, value_ref, cot_ref, filter_ref, before_ref, coefs_ref,
    fore_u_ref, fore_g_ref, impulse_ref, back_ref, moments_ref,
    sent_ref, mixed_ref, grad_ref, key_short_ref, value_short_ref, impulse_out, products,
):
    width = mixed_ref.shape[1]
    step = min(INNER, width)
    waiting = [
        block_columns(
            slice(start, start + step), slice(start // LANES, (start + step) // LANES),
            query_ref, key_ref, value_ref, cot_ref, filter_ref, before_ref, coefs_ref,
            fore_u_ref, fore_g_ref, impulse_ref, back_ref, moments_ref,
            sent_ref, mixed_ref, grad_ref, key_short_ref, value_short_ref, impulse_out, products,
        )
        for start in range(0, width, step)
    ]
    interleave(waiting, SKEW)


def block_columns(
    at, chunks,
    query_ref, key_ref, value_ref, cot_ref, filter_ref, before_ref, coefs_ref,
    fore_u_ref, fore_g_ref, impulse_ref, back_ref, moments_ref,
    sent_ref, mixed_ref, grad_ref, key_short_ref, value_short_ref, impulse_out, products,
):
    before = before_ref[:, at].astype(F32)
    query, key, value = (ref[0, :, at].astype(F32) for ref in (query_ref, key_ref, value_ref))
    cot = cot_ref[0, :, at].astype(F32)

    def lagged(i, x):
        edge = before[2 * i : 2 * i + 2]
        return (x, later_rows(x, edge, 1), later_rows(x, edge, 2))

    def short(i, inputs):
        return sum(filter_ref[i, j : j + 1, at] * inputs[j] for j in range(3))

    queries, keys, values = lagged(0, query), lagged(1, key), lagged(2, value)
    key_short, value_short = short(1, keys), short(2, values)
    key_short_ref[:, at] = key_short.astype(BF16)
    value_short_ref[:, at] = value_short.astype(BF16)
    gated = (key_short * value_short).astype(BF16)
    grad_mixed = (cot * short(0, queries)).astype(BF16)
    for i, (left, inputs) in enumerate(((cot, queries), (value_short, keys), (key_short, values))):
        for j in range(3):
            start = (3 * i + j) * BLOCK
            products[start : start + BLOCK, at] = (left * inputs[j]).astype(BF16)

    yield
    u = dot(fore_u_ref[...], jnp.concatenate([gated, gated], axis=0))
    g = dot(fore_g_ref[...], jnp.concatenate([grad_mixed, grad_mixed], axis=0))
    coefs = lanes_of(coefs_ref, slice(None), chunks)
    h = dot(impulse_ref[...], jnp.concatenate([coefs, coefs[:16]], axis=0))
    impulse_out[:, at] = h[2 * FREQS : 2 * FREQS + 8]
    yield
    ur, ui, gr, gi, hr, hi = (
        x[part * FREQS : (part + 1) * FREQS] for x in (u, g, h) for part in (0, 1)
    )

    def spectrum(real, imag):
        return jnp.concatenate([real.astype(BF16), imag.astype(BF16)], axis=0)

    products[PRODUCTS * BLOCK :, at] = spectrum(gr * ur + gi * ui, gi * ur - gr * ui)
    mixed = dot(back_ref[...], spectrum(ur * hr - ui * hi, ur * hi + ui * hr))
    grad = dot(back_ref[...], spectrum(gr * hr + gi * hi, gi * hr - gr * hi))
    yield
    mixed_ref[:, at] = mixed.astype(BF16)
    grad_ref[:, at] = grad.astype(BF16)
    row = lax.broadcasted_iota(jnp.int32, (16, mixed.shape[1]), 0)
    sums = [u[2 * FREQS :], g[2 * FREQS :]]
    spare = 16 - TERMS
    for i, (inputs, weight) in enumerate(
        ((queries, cot * mixed), (keys, value_short * grad), (values, key_short * grad))
    ):
        for j in range(3):
            m = 3 * i + j
            local = jnp.sum(inputs[j] * weight, axis=0, keepdims=True)
            sums[m // spare] = jnp.where(row == TERMS + m % spare, local, sums[m // spare])
    yield
    store_chunks(sent_ref, chunks, 0, dot(moments_ref[...], products[:, at]))
    store_chunks(sent_ref, chunks, SUM_ROW, sums[0])
    store_chunks(sent_ref, chunks, SUM_ROW + 16, sums[1])


def owner_kernel(
    first, second, moments_ref, basis_ref, slope_ref, loaded_ref, rate_ref, root_ref, amount_ref,
    carry_ref, message_ref, ahead, behind,
):
    blocks = moments_ref.shape[1]
    modes = rate_ref.shape[0]
    row = lax.broadcasted_iota(jnp.int32, (blocks, LANES), 0)
    lag, sum_u, sum_g, spare = LAG_ROW, SUM_ROW, SUM_ROW + 16, 16 - TERMS

    def later(x, by):
        return jnp.where(row >= by, pltpu.roll(x, by, 0), 0.0)

    def sooner(x, by):
        return jnp.where(row < blocks - by, pltpu.roll(x, blocks - by, 0), 0.0)

    lag_rows = [jnp.sum(moments_ref[lag + k], axis=0, keepdims=True) for k in range(TERMS)]
    first_rows, second_rows = [], []
    for n in range(modes):
        basis = [basis_ref[k, n : n + 1, :] for k in range(TERMS)]
        slope = [slope_ref[k, n : n + 1, :] for k in range(TERMS)]
        state = sum(basis[k] * moments_ref[sum_u + k] for k in range(TERMS))
        state_slope = sum(slope[k] * moments_ref[sum_u + k] for k in range(1, TERMS))
        grad = sum(basis[k] * moments_ref[sum_g + k] for k in range(TERMS))
        grad_slope = sum(slope[k] * moments_ref[sum_g + k] for k in range(1, TERMS))
        rate = rate_ref[n : n + 1, :]
        half = jnp.exp(-float(CENTRE) * rate)
        factor = half * half
        moved = later(state, 1)
        forward = factor * moved
        forward_slope = factor * (later(state_slope, 1) + float(BLOCK) * moved)
        backward = factor * sooner(grad, 1)
        by = 1
        while by < blocks:
            moved = later(forward, by)
            forward_slope = forward_slope + factor * (
                later(forward_slope, by) + float(BLOCK * by) * moved
            )
            forward = forward + factor * moved
            backward = backward + factor * sooner(backward, by)
            factor = factor * factor
            by *= 2
        ahead[n] = forward
        behind[n] = backward
        first_sum = jnp.sum(forward * grad, axis=0, keepdims=True)
        second_sum = jnp.sum(forward_slope * grad + forward * grad_slope, axis=0, keepdims=True)
        near = half * sum(basis[k] * lag_rows[k] for k in range(TERMS))
        near_slope = half * sum(slope[k] * lag_rows[k] for k in range(1, TERMS))
        first_rows.append(first_sum + near)
        second_rows.append(second_sum + near_slope + float(CENTRE) * near)
    totals = [moments_ref[SUM_ROW + 16 * (m // spare) + TERMS + m % spare] for m in range(PRODUCTS)]
    edge_one, edge_two = 0.0, 0.0
    for k in range(TERMS):
        carry = sum(loaded_ref[k, n : n + 1, :] * ahead[n] for n in range(modes))
        back = sum(loaded_ref[k, n : n + 1, :] * behind[n] for n in range(modes))
        for start, value in ((0, carry), (16, back)):
            high = value.astype(BF16)
            carry_ref[start + k] = high
            if k < 16 - TERMS:
                carry_ref[start + TERMS + k] = (value - high.astype(F32)).astype(BF16)
        edge_one = edge_one + first[k] * carry
        edge_two = edge_two + second[k] * carry
        if k < SHORT_TERMS:
            for m in range(PRODUCTS):
                totals[m] = totals[m] + (carry if m < 3 else back) * moments_ref[m * SHORT_TERMS + k]
    carry_ref[32] = sooner(edge_one, 1).astype(BF16)
    carry_ref[33] = sooner(edge_two, 1).astype(BF16)
    root, amount = root_ref[...], amount_ref[...]
    first_sum = jnp.concatenate(first_rows, axis=0)
    second_sum = jnp.concatenate(second_rows, axis=0)
    rate = rate_ref[...]
    steep = amount * (jnp.exp(-2.0 * rate) / root * first_sum - root * second_sum)
    for i in range(34, CARRY_ROWS):
        carry_ref[i] = jnp.zeros((blocks, LANES), BF16)
    rows = [jnp.zeros((2, LANES), F32)]
    rows.extend(jnp.sum(total, axis=0, keepdims=True) for total in totals)
    rows.append(jnp.zeros((14 - PRODUCTS, LANES), F32))
    message = jnp.concatenate([*rows, root * first_sum, rate * steep], axis=0).astype(BF16)
    message_ref[...] = jnp.broadcast_to(message[None], message_ref.shape)


def total_kernel(factor, message_ref, carry_ref, sent_ref, residue_ref, decay_ref):
    total = message_ref[0].astype(F32)
    for i in range(1, message_ref.shape[0]):
        total = total + message_ref[i].astype(F32)
    total = total * factor
    modes = residue_ref.shape[0]
    residue_ref[...] = total[16 : 16 + modes]
    decay_ref[...] = total[16 + modes :]
    shared = total[:16]
    for block in range(sent_ref.shape[0]):
        sent_ref[block, :32, :] = carry_ref[block, :32, :]
        sent_ref[block, 32:48, :] = (carry_ref[block, 32:48, :].astype(F32) + shared).astype(BF16)


def edge_kernel(query_end, key_end, value_end, filter_ref, after_ref, impulse_ref, edge_ref):
    after, impulse = after_ref[...].astype(F32), impulse_ref[...]

    def rounded(x):
        return x.astype(BF16).astype(F32)

    def short_after(i, ref):
        last, following = ref[0].astype(F32)[14:], after[2 * i : 2 * i + 2]
        middle = jnp.concatenate([last[1:2], following[0:1]], axis=0)
        zero, one, two = (filter_ref[i, j : j + 1, :] for j in range(3))
        return zero * following + one * middle + two * last

    query_next, key_next, value_next = (
        short_after(i, ref) for i, ref in enumerate((query_end, key_end, value_end))
    )
    gated_next = rounded(key_next * value_next)
    grad_mixed_next = rounded(after[6:7] * query_next[0:1])
    edge_ref[...] = jnp.concatenate(
        [
            impulse[0:1] * gated_next[0:1],
            impulse[0:1] * gated_next[1:2] + impulse[1:2] * gated_next[0:1],
            -impulse[2:3] * grad_mixed_next,
            jnp.zeros_like(grad_mixed_next),
            key_next,
            value_next,
        ],
        axis=0,
    )


def finish_kernel(
    cot_ref, filter_ref, after_ref, local_edge_ref, key_short_ref, value_short_ref,
    mixed_ref, grad_ref, carry_ref, carried_ref,
    query_out, key_out, value_out, filter_out,
):
    step = min(INNER, mixed_ref.shape[1])
    for start in range(0, mixed_ref.shape[1], step):
        finish_columns(
            slice(start, start + step), slice(start // LANES, (start + step) // LANES),
            cot_ref, filter_ref, after_ref, local_edge_ref, key_short_ref, value_short_ref,
            mixed_ref, grad_ref, carry_ref, carried_ref,
            query_out, key_out, value_out, filter_out,
        )


def finish_columns(
    at, chunks,
    cot_ref, filter_ref, after_ref, local_edge_ref, key_short_ref, value_short_ref,
    mixed_ref, grad_ref, carry_ref, carried_ref,
    query_out, key_out, value_out, filter_out,
):
    after, local_edge = after_ref[:, at].astype(F32), local_edge_ref[:, at]

    def tap(i, j):
        return filter_ref[i, j : j + 1, at]

    both = lanes_of(carry_ref, slice(0, 32), chunks)
    both = jnp.concatenate([both[:16], both[:16], both[16:], both[16:]], axis=0)
    carried = dot(carried_ref[...], both)
    rest = lanes_of(carry_ref, slice(32, 48), chunks).astype(F32)
    for m in range(PRODUCTS):
        filter_out[m // 3, m % 3 : m % 3 + 1, at] = rest[2 + m : 3 + m]
    mixed = mixed_ref[:, at].astype(F32) + carried[:BLOCK]
    grad = grad_ref[:, at].astype(F32) + carried[BLOCK : 2 * BLOCK]
    edge = carried[2 * BLOCK :]
    mixed_next = rest[0:1] + local_edge[0:1], rest[1:2] + local_edge[1:2]
    grad_next = edge[0:1], edge[1:2] + local_edge[2:3]

    cot = cot_ref[0, :, at].astype(F32)
    for i, (out_ref, left, right, left_next, right_next) in enumerate(
        (
            (query_out, cot, mixed, after[6:8], mixed_next),
            (key_out, value_short_ref[:, at].astype(F32), grad, local_edge[6:8], grad_next),
            (value_out, key_short_ref[:, at].astype(F32), grad, local_edge[4:6], grad_next),
        )
    ):
        zero, one, two = (tap(i, j) for j in range(3))
        here = left * right
        following = left_next[0:1] * right_next[0]
        inner = one * here + sooner_rows(two * here, two * following)
        inner_after = one * following + two * (left_next[1:2] * right_next[1])
        out_ref[0, :, at] = (zero * here + sooner_rows(inner, inner_after)).astype(BF16)


def body(query_rows, key_rows, value_rows, cotangent, short_filter, residue, decay_rate):
    width = query_rows.shape[2]
    blocks = lax.axis_size("seq")
    groups = lax.axis_size("dp")
    modes = residue.shape[1]
    length = BLOCK * blocks
    wide = min(WIDE, width)
    parts = wide // LANES
    grid = (width // wide,)
    tables = make_tables()
    first, second = tables.pop("first"), tables.pop("second")
    tables = {name: jnp.asarray(table) for name, table in tables.items()}
    params = pltpu.CompilerParams(vmem_limit_bytes=VMEM_LIMIT)
    full_params = pltpu.CompilerParams(vmem_limit_bytes=FULL_LIMIT)
    small_params = pltpu.CompilerParams(vmem_limit_bytes=SMALL_LIMIT)

    def shape(*dims, dtype=F32):
        return jax.ShapeDtypeStruct(dims, dtype)

    def edge_spec(end):
        return pl.BlockSpec((1, 16, width), lambda c: (0, (BLOCK // 16 - 1) * end, 0))

    flip, small = shape(modes, LANES), shape(TERMS, modes, LANES)
    amount_t, rate_t = residue.T, decay_rate.T
    edges = shape(8, width, dtype=BF16)
    outs = (flip, small, small, small, shape(blocks, 32, LANES, dtype=BF16), edges)
    root_t, basis, slope, loaded, spread, last = pl.pallas_call(
        prep_kernel,
        grid=(1,),
        in_specs=[whole(flip.shape)] * 2 + [edge_spec(1)] * 3,
        out_specs=[whole(out.shape) for out in outs],
        out_shape=outs,
        compiler_params=params,
        name="prep",
    )(amount_t, rate_t, query_rows, key_rows, value_rows)
    before = lax.ppermute(last, "seq", [(i, i + 1) for i in range(blocks - 1)])
    coefs = lax.all_to_all(spread, "seq", 0, 0, tiled=True)

    tall = pl.BlockSpec((1, BLOCK, wide), lambda c: (0, 0, c))
    filters = pl.BlockSpec((3, 3, wide), lambda c: (0, 0, c))

    def flat(rows):
        return pl.BlockSpec((rows, wide), lambda c: (0, c))

    def chunks(rows):
        return pl.BlockSpec((parts, rows, LANES), lambda c: (c, 0, 0))

    def table_specs(names):
        return [whole(tables[name].shape) for name in names]

    names = ("fore_u", "fore_g", "impulse", "back", "moments")
    half = shape(BLOCK, width, dtype=BF16)
    sent, mixed, grad, key_short, value_short, impulse = pl.pallas_call(
        block_kernel,
        grid=grid,
        in_specs=[tall] * 4 + [filters, flat(8), chunks(32)] + table_specs(names),
        out_specs=(chunks(SENT_ROWS), *[flat(BLOCK)] * 4, flat(8)),
        out_shape=(shape(blocks, SENT_ROWS, LANES, dtype=BF16), half, half, half, half, shape(8, width)),
        scratch_shapes=[pltpu.VMEM(((PRODUCTS + 2) * BLOCK, wide), BF16)],
        compiler_params=full_params,
        name="block",
    )(
        query_rows, key_rows, value_rows, cotangent, short_filter, before, coefs,
        *[tables[name] for name in names],
    )
    front = pl.pallas_call(
        front_kernel,
        grid=(1,),
        in_specs=[edge_spec(0)] * 4,
        out_specs=whole((8, width)),
        out_shape=edges,
        compiler_params=params,
        name="front",
    )(query_rows, key_rows, value_rows, cotangent)
    sent, front = lax.optimization_barrier((sent, front))
    moments = lax.all_to_all(sent, "seq", 0, 0, tiled=True)
    after = lax.ppermute(front, "seq", [(i + 1, i) for i in range(blocks - 1)])
    moments, after = lax.optimization_barrier((moments, after))
    moments = moments.transpose(1, 0, 2).astype(F32)

    carry, message = pl.pallas_call(
        lambda *refs: owner_kernel(first, second, *refs),
        out_shape=(
            shape(CARRY_ROWS, blocks, LANES, dtype=BF16),
            shape(groups, 16 + 2 * modes, LANES, dtype=BF16),
        ),
        scratch_shapes=[pltpu.VMEM((modes, blocks, LANES), F32)] * 2,
        compiler_params=small_params,
        name="owner",
    )(moments, basis, slope, loaded, rate_t, root_t, amount_t)
    message = lax.all_to_all(message, "dp", 0, 0, tiled=True)
    local_edge = pl.pallas_call(
        edge_kernel,
        grid=(1,),
        in_specs=[edge_spec(1)] * 3 + [whole((3, 3, width)), whole((8, width)), whole((8, width))],
        out_specs=whole((8, width)),
        out_shape=shape(8, width),
        compiler_params=params,
        name="edge",
    )(query_rows, key_rows, value_rows, short_filter, after, impulse)
    message, local_edge = lax.optimization_barrier((message, local_edge))
    factor = 1.0 / math.sqrt(query_rows.shape[0] * groups * length)
    sent, residue_grad, decay_grad = pl.pallas_call(
        lambda *refs: total_kernel(factor, *refs),
        out_shape=(shape(blocks, CARRY_ROWS, LANES, dtype=BF16), flip, flip),
        compiler_params=small_params,
        name="total",
    )(message, carry.transpose(1, 0, 2))
    carry = lax.all_to_all(sent, "seq", 0, 0, tiled=True)

    names = ("carried",)
    *outs, filter_grad = pl.pallas_call(
        finish_kernel,
        grid=grid,
        in_specs=[tall, filters, flat(8), flat(8)] + [flat(BLOCK)] * 4
        + [chunks(CARRY_ROWS)] + table_specs(names),
        out_specs=[tall] * 3 + [filters],
        out_shape=[jax.ShapeDtypeStruct(query_rows.shape, BF16)] * 3 + [shape(3, 3, width)],
        compiler_params=params,
        name="finish",
    )(
        cotangent, short_filter, after, local_edge, key_short, value_short,
        mixed, grad, carry, *[tables[name] for name in names],
    )
    return (*outs, filter_grad, residue_grad.T, decay_grad.T)


def solution(mesh):
    rows = P("dp", "seq", None)
    return jax.shard_map(
        body,
        mesh=mesh,
        in_specs=(rows, rows, rows, rows, P(), P("seq", None), P("seq", None)),
        out_specs=(rows, rows, rows, P(), P("seq", None), P("seq", None)),
        check_vma=False,
    )
```

time: 106 us -> 95.8 us (0.904)
  the two profiles are of different devices: /device:TPU:30 before, /device:TPU:8 now
where the time goes in v3:
time: 95.8 us; the launch traced here: 95.1 us
  starting transfers between devices  31 us (32%)
  Pallas kernels  28.4 us (30%)
  waiting for transfers between devices  19.5 us (20%)
  blocking collectives  14.8 us (15%)
    all_to_all x1, blocking collectives, body(): carry = lax.all_to_all(sent, 'seq', 0, 0, tiled=True)  14.8 us
    pallas_call x1, Pallas kernels, body(): pl.pallas_call(block_kernel, grid=grid, in_specs=[tall] * 4 + [filters, f...  12.4 us
    all_to_all x1, starting transfers between devices, body(): coefs = lax.all_to_all(spread, 'seq', 0, 0, tiled=True)  8.94 us
    ppermute x1, waiting for transfers between devices, body(): after = lax.ppermute(front, 'seq', [(i + 1, i) for i in range(blocks - 1)])  7.81 us
    all_to_all x1, starting transfers between devices, body(): message = lax.all_to_all(message, 'dp', 0, 0, tiled=True)  7.56 us
    pallas_call x1, Pallas kernels, body(): pl.pallas_call(finish_kernel, grid=grid, in_specs=[tall, filters, flat(8)...  6.94 us
    all_to_all x1, waiting for transfers between devices, body(): message = lax.all_to_all(message, 'dp', 0, 0, tiled=True)  6.93 us
    all_to_all x1, starting transfers between devices, body(): moments = lax.all_to_all(sent, 'seq', 0, 0, tiled=True)  6.36 us
  transfers between devices with their start and end apart: 5, of which 4 were waited for; matrix products, arithmetic and copies ran while one was open for 0% of the time, Pallas kernels for 4%

profile of v3, /device:TPU:8, one launch (start us, length us, event | category | flops | bytes accessed | tf_op | source)
XLA Modules:
  0.0 95.1 jit_solution(12614862087301248264)
XLA Ops:
  0.6 1.9 %prep.1 = (f32[16,128]{1,0:T(8,128)}, f32[10,16,128]{2,1,0:T(8,128)}, f32[10,16,128]{2,1,0:T(8,128)}, f32[10,16,128]{2,1,0:T(8,128)}, bf16[32,32,128]{2,1,0:T(8,128)(2,1)}, /*index=5*/bf16[8,4096]{1,0:T(8,128)(2,1)}) custom-call(f32[16,128]{1,0:T(8,128)} %bitcast.10, f32[16,128]{1,0:T(8,128)} %bitcast.12, bf16[1,128,4096]{2,1,0:T(8,128)(2,1)} %query_end.1, ...), custom_call_target="tpu_custom_call" | custom-call | tf_op jit(solution)/shard_map/prep/pallas_call | solution.py:481
  2.5 8.9 %all-to-all-start = ((bf16[32,32,128]{2,1,0:T(8,128)(2,1)}), bf16[32,32,128]{2,1,0:T(8,128)(2,1)}, u32[]{:S(2)}, u32[]{:S(2)}) async-start(bf16[32,32,128]{2,1,0:T(8,128)(2,1)} %get-tuple-element.34), calls=%async_computation | async-start | bytes 524288 | tf_op jit(solution)/shard_map/all_to_all | solution.py:491
  11.5 3.4 %collective-permute-start = (bf16[8,4096]{1,0:T(8,128)(2,1)}, bf16[8,4096]{1,0:T(8,128)(2,1)}, u32[]{:S(2)}, u32[]{:S(2)}) collective-permute-start(bf16[8,4096]{1,0:T(8,128)(2,1)} %get-tuple-element.33), channel_id=1, source_target_pairs={{0,8},{8,16},{16,24},{24,32},{32,40},{40,48},{48,56},{56,64},{64,7... | collective-permute-start | bytes 196616 | tf_op jit(solution)/shard_map/ppermute | solution.py:490
  14.9 1.8 %front.1 = bf16[8,4096]{1,0:T(8,128)(2,1)} custom-call(bf16[1,128,4096]{2,1,0:T(8,128)(2,1)} %query_end.1, bf16[1,128,4096]{2,1,0:T(8,128)(2,1)} %key_end.1, bf16[1,128,4096]{2,1,0:T(8,128)(2,1)} %value_end.1, bf16[1,128,4096]{2,1,0:T(8,128)(2,1)} %cot_ref.3), custom_call_target="tpu_custom_call" | custom-call | tf_op jit(solution)/shard_map/front/pallas_call | solution.py:520
  16.6 3.4 %collective-permute-done.before_ref = bf16[8,4096]{1,0:T(8,128)(2,1)} collective-permute-done((bf16[8,4096]{1,0:T(8,128)(2,1)}, bf16[8,4096]{1,0:T(8,128)(2,1)}, u32[]{:S(2)}, u32[]{:S(2)}) %collective-permute-start) | collective-permute-done | bytes 65568 | tf_op jit(solution)/shard_map/ppermute | solution.py:490
  20.1 12.4 %block.1 = (bf16[32,128,128]{2,1,0:T(8,128)(2,1)}, bf16[128,4096]{1,0:T(8,128)(2,1)}, bf16[128,4096]{1,0:T(8,128)(2,1)}, bf16[128,4096]{1,0:T(8,128)(2,1)}, bf16...) custom-call(bf16[1,128,4096]{2,1,0:T(8,128)(2,1)} %query_end.1, bf16[1,128,4096]{2,1,0:T(8,128)(2,1)} %key_end.1, ...), custom_call_target="tpu_custom_call" | custom-call | tf_op jit(solution)/shard_map/block/pallas_call | solution.py:507
  32.5 6.4 %all-to-all-start.1 = ((bf16[32,128,128]{2,1,0:T(8,128)(2,1)}), bf16[32,128,128]{2,1,0:T(8,128)(2,1)S(1)}, u32[]{:S(2)}, u32[]{:S(2)}) async-start(bf16[32,128,128]{2,1,0:T(8,128)(2,1)} %get-tuple-element.36), calls=%async_computation.1 | async-start | bytes 2097152 | tf_op jit(solution)/shard_map/all_to_all | solution.py:530
  38.9 0.0 copy-start
  38.9 0.0 copy-start.1
  38.9 0.0 copy-start.3
  38.9 0.0 copy-start.4
  38.9 0.0 copy-start.5
  38.9 4.7 %collective-permute-start.1 = (bf16[8,4096]{1,0:T(8,128)(2,1)S(1)}, bf16[8,4096]{1,0:T(8,128)(2,1)S(1)}, u32[]{:S(2)}, u32[]{:S(2)}) collective-permute-start(bf16[8,4096]{1,0:T(8,128)(2,1)S(1)} %copy-done.7), channel_id=1, source_target_pairs={{8,0},{16,8},{24,16},{32,24},{40,32},{48,40},{56,48},{64,56},{72,6... | collective-permute-start | bytes 196616 | tf_op jit(solution)/shard_map/ppermute | solution.py:531
  43.7 7.8 %collective-permute-done.1.after_ref = bf16[8,4096]{1,0:T(8,128)(2,1)S(1)} collective-permute-done((bf16[8,4096]{1,0:T(8,128)(2,1)S(1)}, bf16[8,4096]{1,0:T(8,128)(2,1)S(1)}, u32[]{:S(2)}, u32[]{:S(2)}) %collective-permute-start.1) | collective-permute-done | bytes 65568 | tf_op jit(solution)/shard_map/ppermute | solution.py:531
  51.5 1.3 %all-to-all-done.1 = bf16[32,128,128]{2,1,0:T(8,128)(2,1)S(1)} async-done(((bf16[32,128,128]{2,1,0:T(8,128)(2,1)}), bf16[32,128,128]{2,1,0:T(8,128)(2,1)S(1)}, u32[]{:S(2)}, u32[]{:S(2)}) %all-to-all-start.1) | async-done | bytes 1048608 | tf_op jit(solution)/shard_map/all_to_all | solution.py:530
  52.7 0.6 convert_bitcast_fusion.refs_0_
  53.4 2.6 %owner.1 = (bf16[48,32,128]{2,1,0:T(8,128)(2,1)S(1)}, bf16[8,48,128]{2,1,0:T(8,128)(2,1)}) custom-call(f32[128,32,128]{2,1,0:T(8,128)S(1)} %convert_bitcast_fusion.refs_0_, f32[10,16,128]{2,1,0:T(8,128)S(1)} %copy-done, f32[10,16,128]{2,1,0:T(8,128)S(1)} %copy-done.1, f32[10,16,128]{2,1,0:T(8,128)S(1)} %copy-done.2, f32[16,128]{1,0:T(8,128)S(1)} %bitcast.13, ...), custom_call_target="tpu_custom_call" | custom-call | tf_op jit(solution)/shard_map/owner/pallas_call | solution.py:535
  56.0 7.6 %all-to-all-start.2 = ((bf16[8,48,128]{2,1,0:T(8,128)(2,1)}), bf16[8,48,128]{2,1,0:T(8,128)(2,1)S(1)}, u32[]{:S(2)}, u32[]{:S(2)}) async-start(bf16[8,48,128]{2,1,0:T(8,128)(2,1)} %get-tuple-element.44), calls=%async_computation.2 | async-start | bytes 196608 | tf_op jit(solution)/shard_map/all_to_all | solution.py:545
  63.6 0.2 copy.25
  63.7 2.1 %edge.1.local_edge_ref = f32[8,4096]{1,0:T(8,128)} custom-call(bf16[1,128,4096]{2,1,0:T(8,128)(2,1)} %query_end.1, bf16[1,128,4096]{2,1,0:T(8,128)(2,1)} %key_end.1, bf16[1,128,4096]{2,1,0:T(8,128)(2,1)} %value_end.1, f32[3,3,4096]{2,1,0:T(4,128)} %filter_ref.5, bf16[8,4096]{1,0:T(8,128)(2,1)} %copy-done.6, f32[8,4096]{1,0:T(8,128)} %get-tuple-element.45.impulse_ref), custom_call_target="tpu_custom_call" | custom-call | tf_op jit(solution)/shard_map/edge/pallas_call | solution.py:546
  65.9 6.9 %all-to-all-done.2.refs_0_ = bf16[8,48,128]{2,1,0:T(8,128)(2,1)S(1)} async-done(((bf16[8,48,128]{2,1,0:T(8,128)(2,1)}), bf16[8,48,128]{2,1,0:T(8,128)(2,1)S(1)}, u32[]{:S(2)}, u32[]{:S(2)}) %all-to-all-start.2) | async-done | bytes 98336 | tf_op jit(solution)/shard_map/all_to_all | solution.py:545
  72.8 0.6 total.1
  73.4 14.8 %all_to_all.20.carry_ref = bf16[32,48,128]{2,1,0:T(8,128)(2,1)} all-to-all(bf16[32,48,128]{2,1,0:T(8,128)(2,1)S(1)} %get-tuple-element.53), channel_id=1, replica_groups=mesh['seq'=32,'dp'=8] {'seq'}, dimensions={0} | all-to-all | bytes 786432 | tf_op jit(solution)/shard_map/all_to_all | solution.py:563
  88.2 6.9 %finish.1 = (bf16[1,128,4096]{2,1,0:T(8,128)(2,1)}, bf16[1,128,4096]{2,1,0:T(8,128)(2,1)}, bf16[1,128,4096]{2,1,0:T(8,128)(2,1)}, f32[3,3,4096]{2,1,0:T(4,128)}) custom-call(bf16[1,128,4096]{2,1,0:T(8,128)(2,1)} %cot_ref.3, f32[3,3,4096]{2,1,0:T(4,128)} %filter_ref.5, bf16[8,4096]{1,0:T(8,128)(2,1)} %copy-done.6, f32[8,4096]{1,0:T(8,128)} %edge.1.local_edge_ref, ...), custom_call_target="tpu_custom_call" | custom-call | tf_op jit(solution)/shard_map/finish/pallas_call | solution.py:566
  (12 shorter events, 0.0 us)
Async XLA Ops:
  2.5 17.5 %all-to-all-start = ((bf16[32,32,128]{2,1,0:T(8,128)(2,1)}), bf16[32,32,128]{2,1,0:T(8,128)(2,1)}, u32[]{:S(2)}, u32[]{:S(2)}) async-start(bf16[32,32,128]{2,1,0:T(8,128)(2,1)} %get-tuple-element.34), calls=%async_computation | async-start | bytes 524288 | tf_op jit(solution)/shard_map/all_to_all | solution.py:491
  11.5 8.6 %collective-permute-start = (bf16[8,4096]{1,0:T(8,128)(2,1)}, bf16[8,4096]{1,0:T(8,128)(2,1)}, u32[]{:S(2)}, u32[]{:S(2)}) collective-permute-start(bf16[8,4096]{1,0:T(8,128)(2,1)} %get-tuple-element.33), channel_id=1, source_target_pairs={{0,8},{8,16},{16,24},{24,32},{32,40},{40,48},{48,56},{56,64},{64,7... | collective-permute-start | bytes 196616 | tf_op jit(solution)/shard_map/ppermute | solution.py:490
  32.5 6.4 %copy-start.7 = (bf16[8,4096]{1,0:T(8,128)(2,1)S(1)}, bf16[8,4096]{1,0:T(8,128)(2,1)}, u32[]{:S(2)}) copy-start(bf16[8,4096]{1,0:T(8,128)(2,1)} %front.1) | copy-start | bytes 196612
  32.5 20.2 %all-to-all-start.1 = ((bf16[32,128,128]{2,1,0:T(8,128)(2,1)}), bf16[32,128,128]{2,1,0:T(8,128)(2,1)S(1)}, u32[]{:S(2)}, u32[]{:S(2)}) async-start(bf16[32,128,128]{2,1,0:T(8,128)(2,1)} %get-tuple-element.36), calls=%async_computation.1 | async-start | bytes 2097152 | tf_op jit(solution)/shard_map/all_to_all | solution.py:530
  38.9 14.5 %copy-start = (f32[10,16,128]{2,1,0:T(8,128)S(1)}, f32[10,16,128]{2,1,0:T(8,128)}, u32[]{:S(2)}) copy-start(f32[10,16,128]{2,1,0:T(8,128)} %get-tuple-element.40.refs_1_) | copy-start | bytes 245764
  38.9 14.5 %copy-start.1 = (f32[10,16,128]{2,1,0:T(8,128)S(1)}, f32[10,16,128]{2,1,0:T(8,128)}, u32[]{:S(2)}) copy-start(f32[10,16,128]{2,1,0:T(8,128)} %get-tuple-element.41.refs_2_) | copy-start | bytes 245764
  38.9 14.5 %copy-start.2 = (f32[10,16,128]{2,1,0:T(8,128)S(1)}, f32[10,16,128]{2,1,0:T(8,128)}, u32[]{:S(2)}) copy-start(f32[10,16,128]{2,1,0:T(8,128)} %get-tuple-element.42.refs_3_) | copy-start | bytes 245764
  38.9 14.5 %copy-start.3 = (f32[128,16]{0,1:T(8,128)S(1)}, f32[128,16]{0,1:T(8,128)}, u32[]{:S(2)}) copy-start(f32[128,16]{0,1:T(8,128)} %param.18) | copy-start | bytes 24580
  38.9 14.5 %copy-start.4 = (f32[128,16]{0,1:T(8,128)S(1)}, f32[128,16]{0,1:T(8,128)}, u32[]{:S(2)}) copy-start(f32[128,16]{0,1:T(8,128)} %param.19) | copy-start | bytes 24580
  38.9 14.5 %copy-start.5 = (f32[16,128]{1,0:T(8,128)S(1)}, f32[16,128]{1,0:T(8,128)}, u32[]{:S(2)}) copy-start(f32[16,128]{1,0:T(8,128)} %get-tuple-element.43.refs_5_) | copy-start | bytes 24580
  38.9 12.5 %collective-permute-start.1 = (bf16[8,4096]{1,0:T(8,128)(2,1)S(1)}, bf16[8,4096]{1,0:T(8,128)(2,1)S(1)}, u32[]{:S(2)}, u32[]{:S(2)}) collective-permute-start(bf16[8,4096]{1,0:T(8,128)(2,1)S(1)} %copy-done.7), channel_id=1, source_target_pairs={{8,0},{16,8},{24,16},{32,24},{40,32},{48,40},{56,48},{64,56},{72,6... | collective-permute-start | bytes 196616 | tf_op jit(solution)/shard_map/ppermute | solution.py:531
  51.5 4.5 %copy-start.6 = (bf16[8,4096]{1,0:T(8,128)(2,1)}, bf16[8,4096]{1,0:T(8,128)(2,1)S(1)}, u32[]{:S(2)}) copy-start(bf16[8,4096]{1,0:T(8,128)(2,1)S(1)} %collective-permute-done.1.after_ref) | copy-start | bytes 196612
  56.0 16.8 %all-to-all-start.2 = ((bf16[8,48,128]{2,1,0:T(8,128)(2,1)}), bf16[8,48,128]{2,1,0:T(8,128)(2,1)S(1)}, u32[]{:S(2)}, u32[]{:S(2)}) async-start(bf16[8,48,128]{2,1,0:T(8,128)(2,1)} %get-tuple-element.44), calls=%async_computation.2 | async-start | bytes 196608 | tf_op jit(solution)/shard_map/all_to_all | solution.py:545

commit v4 on v3

--- a/solution.py
+++ b/solution.py
@@ -236,7 +236,7 @@
     for i, (left, inputs) in enumerate(((cot, queries), (value_short, keys), (key_short, values))):
         for j in range(3):
             start = (3 * i + j) * BLOCK
-            products[start : start + BLOCK, at] = (left * inputs[j]).astype(BF16)
+            products[start : start + BLOCK, at] = left.astype(BF16) * inputs[j].astype(BF16)
 
     yield
     u = dot(fore_u_ref[...], jnp.concatenate([gated, gated], axis=0))
@@ -246,7 +246,7 @@
     impulse_out[:, at] = h[2 * FREQS : 2 * FREQS + 8]
     yield
     ur, ui, gr, gi, hr, hi = (
-        x[part * FREQS : (part + 1) * FREQS] for x in (u, g, h) for part in (0, 1)
+        x[part * FREQS : (part + 1) * FREQS].astype(BF16) for x in (u, g, h) for part in (0, 1)
     )
 
     def spectrum(real, imag):

time: 95.8 us -> 94.7 us (0.989)
  Pallas kernels: 28.4 us -> 27.2 us
    pallas_call x1, Pallas kernels: 12.4 us -> 11.2 us  [body(): pl.pallas_call(block_kernel, grid=grid, in_specs=[tall] * 4 + [filters, f...]
where the time goes in v4:
time: 94.7 us; the launch traced here: 94 us
  starting transfers between devices  30.9 us (33%)
  Pallas kernels  27.2 us (29%)
  waiting for transfers between devices  19.5 us (21%)
  blocking collectives  14.8 us (16%)
    all_to_all x1, blocking collectives, body(): carry = lax.all_to_all(sent, 'seq', 0, 0, tiled=True)  14.8 us
    pallas_call x1, Pallas kernels, body(): pl.pallas_call(block_kernel, grid=grid, in_specs=[tall] * 4 + [filters, f...  11.2 us
    all_to_all x1, starting transfers between devices, body(): coefs = lax.all_to_all(spread, 'seq', 0, 0, tiled=True)  8.94 us
    ppermute x1, waiting for transfers between devices, body(): after = lax.ppermute(front, 'seq', [(i + 1, i) for i in range(blocks - 1)])  7.81 us
    all_to_all x1, starting transfers between devices, body(): message = lax.all_to_all(message, 'dp', 0, 0, tiled=True)  7.56 us
    pallas_call x1, Pallas kernels, body(): pl.pallas_call(finish_kernel, grid=grid, in_specs=[tall, filters, flat(8)...  6.96 us
    all_to_all x1, waiting for transfers between devices, body(): message = lax.all_to_all(message, 'dp', 0, 0, tiled=True)  6.93 us
    all_to_all x1, starting transfers between devices, body(): moments = lax.all_to_all(sent, 'seq', 0, 0, tiled=True)  6.36 us
  transfers between devices with their start and end apart: 5, of which 4 were waited for; matrix products, arithmetic and copies ran while one was open for 0% of the time, Pallas kernels for 4%

profile of v4, /device:TPU:8, one launch (start us, length us, event | category | flops | bytes accessed | tf_op | source)
XLA Modules:
  0.0 94.0 jit_solution(3773886005760218576)
XLA Ops:
  0.6 1.9 %prep.1 = (f32[16,128]{1,0:T(8,128)}, f32[10,16,128]{2,1,0:T(8,128)}, f32[10,16,128]{2,1,0:T(8,128)}, f32[10,16,128]{2,1,0:T(8,128)}, bf16[32,32,128]{2,1,0:T(8,128)(2,1)}, /*index=5*/bf16[8,4096]{1,0:T(8,128)(2,1)}) custom-call(f32[16,128]{1,0:T(8,128)} %bitcast.10, f32[16,128]{1,0:T(8,128)} %bitcast.12, bf16[1,128,4096]{2,1,0:T(8,128)(2,1)} %query_end.1, ...), custom_call_target="tpu_custom_call" | custom-call | tf_op jit(solution)/shard_map/prep/pallas_call | solution.py:481
  2.5 8.9 %all-to-all-start = ((bf16[32,32,128]{2,1,0:T(8,128)(2,1)}), bf16[32,32,128]{2,1,0:T(8,128)(2,1)}, u32[]{:S(2)}, u32[]{:S(2)}) async-start(bf16[32,32,128]{2,1,0:T(8,128)(2,1)} %get-tuple-element.34), calls=%async_computation | async-start | bytes 524288 | tf_op jit(solution)/shard_map/all_to_all | solution.py:491
  11.5 3.4 %collective-permute-start = (bf16[8,4096]{1,0:T(8,128)(2,1)}, bf16[8,4096]{1,0:T(8,128)(2,1)}, u32[]{:S(2)}, u32[]{:S(2)}) collective-permute-start(bf16[8,4096]{1,0:T(8,128)(2,1)} %get-tuple-element.33), channel_id=1, source_target_pairs={{0,8},{8,16},{16,24},{24,32},{32,40},{40,48},{48,56},{56,64},{64,7... | collective-permute-start | bytes 196616 | tf_op jit(solution)/shard_map/ppermute | solution.py:490
  14.9 1.8 %front.1 = bf16[8,4096]{1,0:T(8,128)(2,1)} custom-call(bf16[1,128,4096]{2,1,0:T(8,128)(2,1)} %query_end.1, bf16[1,128,4096]{2,1,0:T(8,128)(2,1)} %key_end.1, bf16[1,128,4096]{2,1,0:T(8,128)(2,1)} %value_end.1, bf16[1,128,4096]{2,1,0:T(8,128)(2,1)} %cot_ref.3), custom_call_target="tpu_custom_call" | custom-call | tf_op jit(solution)/shard_map/front/pallas_call | solution.py:520
  16.6 3.4 %collective-permute-done.before_ref = bf16[8,4096]{1,0:T(8,128)(2,1)} collective-permute-done((bf16[8,4096]{1,0:T(8,128)(2,1)}, bf16[8,4096]{1,0:T(8,128)(2,1)}, u32[]{:S(2)}, u32[]{:S(2)}) %collective-permute-start) | collective-permute-done | bytes 65568 | tf_op jit(solution)/shard_map/ppermute | solution.py:490
  20.1 11.2 %block.1 = (bf16[32,128,128]{2,1,0:T(8,128)(2,1)}, bf16[128,4096]{1,0:T(8,128)(2,1)}, bf16[128,4096]{1,0:T(8,128)(2,1)}, bf16[128,4096]{1,0:T(8,128)(2,1)}, bf16...) custom-call(bf16[1,128,4096]{2,1,0:T(8,128)(2,1)} %query_end.1, bf16[1,128,4096]{2,1,0:T(8,128)(2,1)} %key_end.1, ...), custom_call_target="tpu_custom_call" | custom-call | tf_op jit(solution)/shard_map/block/pallas_call | solution.py:507
  31.3 6.4 %all-to-all-start.1 = ((bf16[32,128,128]{2,1,0:T(8,128)(2,1)}), bf16[32,128,128]{2,1,0:T(8,128)(2,1)S(1)}, u32[]{:S(2)}, u32[]{:S(2)}) async-start(bf16[32,128,128]{2,1,0:T(8,128)(2,1)} %get-tuple-element.36), calls=%async_computation.1 | async-start | bytes 2097152 | tf_op jit(solution)/shard_map/all_to_all | solution.py:530
  37.7 0.0 copy-start
  37.7 0.0 copy-start.1
  37.7 0.0 copy-start.3
  37.8 0.0 copy-start.4
  37.8 0.0 copy-start.5
  37.8 4.7 %collective-permute-start.1 = (bf16[8,4096]{1,0:T(8,128)(2,1)S(1)}, bf16[8,4096]{1,0:T(8,128)(2,1)S(1)}, u32[]{:S(2)}, u32[]{:S(2)}) collective-permute-start(bf16[8,4096]{1,0:T(8,128)(2,1)S(1)} %copy-done.7), channel_id=1, source_target_pairs={{8,0},{16,8},{24,16},{32,24},{40,32},{48,40},{56,48},{64,56},{72,6... | collective-permute-start | bytes 196616 | tf_op jit(solution)/shard_map/ppermute | solution.py:531
  42.5 7.8 %collective-permute-done.1.after_ref = bf16[8,4096]{1,0:T(8,128)(2,1)S(1)} collective-permute-done((bf16[8,4096]{1,0:T(8,128)(2,1)S(1)}, bf16[8,4096]{1,0:T(8,128)(2,1)S(1)}, u32[]{:S(2)}, u32[]{:S(2)}) %collective-permute-start.1) | collective-permute-done | bytes 65568 | tf_op jit(solution)/shard_map/ppermute | solution.py:531
  50.3 1.3 %all-to-all-done.1 = bf16[32,128,128]{2,1,0:T(8,128)(2,1)S(1)} async-done(((bf16[32,128,128]{2,1,0:T(8,128)(2,1)}), bf16[32,128,128]{2,1,0:T(8,128)(2,1)S(1)}, u32[]{:S(2)}, u32[]{:S(2)}) %all-to-all-start.1) | async-done | bytes 1048608 | tf_op jit(solution)/shard_map/all_to_all | solution.py:530
  51.6 0.6 convert_bitcast_fusion.refs_0_
  52.3 2.6 %owner.1 = (bf16[48,32,128]{2,1,0:T(8,128)(2,1)S(1)}, bf16[8,48,128]{2,1,0:T(8,128)(2,1)}) custom-call(f32[128,32,128]{2,1,0:T(8,128)S(1)} %convert_bitcast_fusion.refs_0_, f32[10,16,128]{2,1,0:T(8,128)S(1)} %copy-done, f32[10,16,128]{2,1,0:T(8,128)S(1)} %copy-done.1, f32[10,16,128]{2,1,0:T(8,128)S(1)} %copy-done.2, f32[16,128]{1,0:T(8,128)S(1)} %bitcast.13, ...), custom_call_target="tpu_custom_call" | custom-call | tf_op jit(solution)/shard_map/owner/pallas_call | solution.py:535
  54.8 7.6 %all-to-all-start.2 = ((bf16[8,48,128]{2,1,0:T(8,128)(2,1)}), bf16[8,48,128]{2,1,0:T(8,128)(2,1)S(1)}, u32[]{:S(2)}, u32[]{:S(2)}) async-start(bf16[8,48,128]{2,1,0:T(8,128)(2,1)} %get-tuple-element.44), calls=%async_computation.2 | async-start | bytes 196608 | tf_op jit(solution)/shard_map/all_to_all | solution.py:545
  62.4 0.2 copy.25
  62.6 2.1 %edge.1.local_edge_ref = f32[8,4096]{1,0:T(8,128)} custom-call(bf16[1,128,4096]{2,1,0:T(8,128)(2,1)} %query_end.1, bf16[1,128,4096]{2,1,0:T(8,128)(2,1)} %key_end.1, bf16[1,128,4096]{2,1,0:T(8,128)(2,1)} %value_end.1, f32[3,3,4096]{2,1,0:T(4,128)} %filter_ref.5, bf16[8,4096]{1,0:T(8,128)(2,1)} %copy-done.6, f32[8,4096]{1,0:T(8,128)} %get-tuple-element.45.impulse_ref), custom_call_target="tpu_custom_call" | custom-call | tf_op jit(solution)/shard_map/edge/pallas_call | solution.py:546
  64.7 6.9 %all-to-all-done.2.refs_0_ = bf16[8,48,128]{2,1,0:T(8,128)(2,1)S(1)} async-done(((bf16[8,48,128]{2,1,0:T(8,128)(2,1)}), bf16[8,48,128]{2,1,0:T(8,128)(2,1)S(1)}, u32[]{:S(2)}, u32[]{:S(2)}) %all-to-all-start.2) | async-done | bytes 98336 | tf_op jit(solution)/shard_map/all_to_all | solution.py:545
  71.6 0.6 total.1
  72.3 14.8 %all_to_all.20.carry_ref = bf16[32,48,128]{2,1,0:T(8,128)(2,1)} all-to-all(bf16[32,48,128]{2,1,0:T(8,128)(2,1)S(1)} %get-tuple-element.53), channel_id=1, replica_groups=mesh['seq'=32,'dp'=8] {'seq'}, dimensions={0} | all-to-all | bytes 786432 | tf_op jit(solution)/shard_map/all_to_all | solution.py:563
  87.0 7.0 %finish.1 = (bf16[1,128,4096]{2,1,0:T(8,128)(2,1)}, bf16[1,128,4096]{2,1,0:T(8,128)(2,1)}, bf16[1,128,4096]{2,1,0:T(8,128)(2,1)}, f32[3,3,4096]{2,1,0:T(4,128)}) custom-call(bf16[1,128,4096]{2,1,0:T(8,128)(2,1)} %cot_ref.3, f32[3,3,4096]{2,1,0:T(4,128)} %filter_ref.5, bf16[8,4096]{1,0:T(8,128)(2,1)} %copy-done.6, f32[8,4096]{1,0:T(8,128)} %edge.1.local_edge_ref, ...), custom_call_target="tpu_custom_call" | custom-call | tf_op jit(solution)/shard_map/finish/pallas_call | solution.py:566
  (12 shorter events, 0.0 us)
Async XLA Ops:
  2.5 17.5 %all-to-all-start = ((bf16[32,32,128]{2,1,0:T(8,128)(2,1)}), bf16[32,32,128]{2,1,0:T(8,128)(2,1)}, u32[]{:S(2)}, u32[]{:S(2)}) async-start(bf16[32,32,128]{2,1,0:T(8,128)(2,1)} %get-tuple-element.34), calls=%async_computation | async-start | bytes 524288 | tf_op jit(solution)/shard_map/all_to_all | solution.py:491
  11.5 8.6 %collective-permute-start = (bf16[8,4096]{1,0:T(8,128)(2,1)}, bf16[8,4096]{1,0:T(8,128)(2,1)}, u32[]{:S(2)}, u32[]{:S(2)}) collective-permute-start(bf16[8,4096]{1,0:T(8,128)(2,1)} %get-tuple-element.33), channel_id=1, source_target_pairs={{0,8},{8,16},{16,24},{24,32},{32,40},{40,48},{48,56},{56,64},{64,7... | collective-permute-start | bytes 196616 | tf_op jit(solution)/shard_map/ppermute | solution.py:490
  31.3 6.4 %copy-start.7 = (bf16[8,4096]{1,0:T(8,128)(2,1)S(1)}, bf16[8,4096]{1,0:T(8,128)(2,1)}, u32[]{:S(2)}) copy-start(bf16[8,4096]{1,0:T(8,128)(2,1)} %front.1) | copy-start | bytes 196612
  31.3 20.3 %all-to-all-start.1 = ((bf16[32,128,128]{2,1,0:T(8,128)(2,1)}), bf16[32,128,128]{2,1,0:T(8,128)(2,1)S(1)}, u32[]{:S(2)}, u32[]{:S(2)}) async-start(bf16[32,128,128]{2,1,0:T(8,128)(2,1)} %get-tuple-element.36), calls=%async_computation.1 | async-start | bytes 2097152 | tf_op jit(solution)/shard_map/all_to_all | solution.py:530
  37.7 14.5 %copy-start = (f32[10,16,128]{2,1,0:T(8,128)S(1)}, f32[10,16,128]{2,1,0:T(8,128)}, u32[]{:S(2)}) copy-start(f32[10,16,128]{2,1,0:T(8,128)} %get-tuple-element.40.refs_1_) | copy-start | bytes 245764
  37.7 14.5 %copy-start.1 = (f32[10,16,128]{2,1,0:T(8,128)S(1)}, f32[10,16,128]{2,1,0:T(8,128)}, u32[]{:S(2)}) copy-start(f32[10,16,128]{2,1,0:T(8,128)} %get-tuple-element.41.refs_2_) | copy-start | bytes 245764
  37.7 14.5 %copy-start.2 = (f32[10,16,128]{2,1,0:T(8,128)S(1)}, f32[10,16,128]{2,1,0:T(8,128)}, u32[]{:S(2)}) copy-start(f32[10,16,128]{2,1,0:T(8,128)} %get-tuple-element.42.refs_3_) | copy-start | bytes 245764
  37.7 14.5 %copy-start.3 = (f32[128,16]{0,1:T(8,128)S(1)}, f32[128,16]{0,1:T(8,128)}, u32[]{:S(2)}) copy-start(f32[128,16]{0,1:T(8,128)} %param.18) | copy-start | bytes 24580
  37.8 14.5 %copy-start.4 = (f32[128,16]{0,1:T(8,128)S(1)}, f32[128,16]{0,1:T(8,128)}, u32[]{:S(2)}) copy-start(f32[128,16]{0,1:T(8,128)} %param.19) | copy-start | bytes 24580
  37.8 14.5 %copy-start.5 = (f32[16,128]{1,0:T(8,128)S(1)}, f32[16,128]{1,0:T(8,128)}, u32[]{:S(2)}) copy-start(f32[16,128]{1,0:T(8,128)} %get-tuple-element.43.refs_5_) | copy-start | bytes 24580
  37.8 12.5 %collective-permute-start.1 = (bf16[8,4096]{1,0:T(8,128)(2,1)S(1)}, bf16[8,4096]{1,0:T(8,128)(2,1)S(1)}, u32[]{:S(2)}, u32[]{:S(2)}) collective-permute-start(bf16[8,4096]{1,0:T(8,128)(2,1)S(1)} %copy-done.7), channel_id=1, source_target_pairs={{8,0},{16,8},{24,16},{32,24},{40,32},{48,40},{56,48},{64,56},{72,6... | collective-permute-start | bytes 196616 | tf_op jit(solution)/shard_map/ppermute | solution.py:531
  50.3 4.5 %copy-start.6 = (bf16[8,4096]{1,0:T(8,128)(2,1)}, bf16[8,4096]{1,0:T(8,128)(2,1)S(1)}, u32[]{:S(2)}) copy-start(bf16[8,4096]{1,0:T(8,128)(2,1)S(1)} %collective-permute-done.1.after_ref) | copy-start | bytes 196612
  54.8 16.8 %all-to-all-start.2 = ((bf16[8,48,128]{2,1,0:T(8,128)(2,1)}), bf16[8,48,128]{2,1,0:T(8,128)(2,1)S(1)}, u32[]{:S(2)}, u32[]{:S(2)}) async-start(bf16[8,48,128]{2,1,0:T(8,128)(2,1)} %get-tuple-element.44), calls=%async_computation.2 | async-start | bytes 196608 | tf_op jit(solution)/shard_map/all_to_all | solution.py:545

commit v5 on v4

--- a/solution.py
+++ b/solution.py
@@ -350,7 +350,12 @@
     rows = [jnp.zeros((2, LANES), F32)]
     rows.extend(jnp.sum(total, axis=0, keepdims=True) for total in totals)
     rows.append(jnp.zeros((14 - PRODUCTS, LANES), F32))
-    message = jnp.concatenate([*rows, root * first_sum, rate * steep], axis=0).astype(BF16)
+    message = jnp.concatenate([*rows, root * first_sum, rate * steep], axis=0)
+    message_ref[...] = message
+
+
+def pair_kernel(own_ref, other_ref, message_ref):
+    message = (own_ref[...] + other_ref[...]).astype(BF16)
     message_ref[...] = jnp.broadcast_to(message[None], message_ref.shape)
 
 
@@ -536,13 +541,21 @@
         lambda *refs: owner_kernel(first, second, *refs),
         out_shape=(
             shape(CARRY_ROWS, blocks, LANES, dtype=BF16),
-            shape(groups, 16 + 2 * modes, LANES, dtype=BF16),
+            shape(16 + 2 * modes, LANES),
         ),
         scratch_shapes=[pltpu.VMEM((modes, blocks, LANES), F32)] * 2,
         compiler_params=small_params,
         name="owner",
     )(moments, basis, slope, loaded, rate_t, root_t, amount_t)
-    message = lax.all_to_all(message, "dp", 0, 0, tiled=True)
+    other = lax.ppermute(message, "dp", [(i, i ^ 1) for i in range(groups)])
+    message = pl.pallas_call(
+        pair_kernel,
+        out_shape=shape(groups // 2, 16 + 2 * modes, LANES, dtype=BF16),
+        compiler_params=small_params,
+        name="pair",
+    )(message, other)
+    alike = [list(range(i, groups, 2)) for i in range(2)]
+    message = lax.all_to_all(message, "dp", 0, 0, axis_index_groups=alike, tiled=True)
     local_edge = pl.pallas_call(
         edge_kernel,
         grid=(1,),

time: 94.7 us -> 95 us (level)
    ppermute x0 -> x1, waiting for transfers between devices: none -> 1.18 us  [body(): other = lax.ppermute(message, 'dp', [(i, i ^ 1) for i in range(groups)])]
    all_to_all x1, waiting for transfers between devices: 6.93 us -> 5.91 us  [body(): lax.all_to_all(message, 'dp', 0, 0, axis_index_groups=alike, tiled=True)]
  transfers between devices with their start and end apart: 5 -> 6, of which waited for: 4 -> 5; matrix products, arithmetic and copies ran while one was open for 0% -> 0% of each run, Pallas kernels for 4% -> 4%
where the time goes in v5:
time: 95 us; the launch traced here: 94.3 us
  starting transfers between devices  31 us (33%)
  Pallas kernels  27.2 us (29%)
  waiting for transfers between devices  19.6 us (21%)
  blocking collectives  14.9 us (16%)
    all_to_all x1, blocking collectives, body(): carry = lax.all_to_all(sent, 'seq', 0, 0, tiled=True)  14.9 us
    pallas_call x1, Pallas kernels, body(): pl.pallas_call(block_kernel, grid=grid, in_specs=[tall] * 4 + [filters, f...  11.2 us
    all_to_all x1, starting transfers between devices, body(): coefs = lax.all_to_all(spread, 'seq', 0, 0, tiled=True)  8.94 us
    ppermute x1, waiting for transfers between devices, body(): after = lax.ppermute(front, 'seq', [(i + 1, i) for i in range(blocks - 1)])  7.81 us
    all_to_all x1, starting transfers between devices, body(): lax.all_to_all(message, 'dp', 0, 0, axis_index_groups=alike, tiled=True)  7.55 us
    pallas_call x1, Pallas kernels, body(): pl.pallas_call(finish_kernel, grid=grid, in_specs=[tall, filters, flat(8)...  6.95 us
    all_to_all x1, starting transfers between devices, body(): moments = lax.all_to_all(sent, 'seq', 0, 0, tiled=True)  6.36 us
    all_to_all x1, waiting for transfers between devices, body(): lax.all_to_all(message, 'dp', 0, 0, axis_index_groups=alike, tiled=True)  5.91 us
  transfers between devices with their start and end apart: 6, of which 5 were waited for; matrix products, arithmetic and copies ran while one was open for 0% of the time, Pallas kernels for 4%

profile of v5, /device:TPU:8, one launch (start us, length us, event | category | flops | bytes accessed | tf_op | source)
XLA Modules:
  0.0 94.3 jit_solution(18224902155743760692)
XLA Ops:
  0.6 1.9 %prep.1 = (f32[16,128]{1,0:T(8,128)}, f32[10,16,128]{2,1,0:T(8,128)}, f32[10,16,128]{2,1,0:T(8,128)}, f32[10,16,128]{2,1,0:T(8,128)}, bf16[32,32,128]{2,1,0:T(8,128)(2,1)}, /*index=5*/bf16[8,4096]{1,0:T(8,128)(2,1)}) custom-call(f32[16,128]{1,0:T(8,128)} %bitcast.10, f32[16,128]{1,0:T(8,128)} %bitcast.12, bf16[1,128,4096]{2,1,0:T(8,128)(2,1)} %query_end.1, ...), custom_call_target="tpu_custom_call" | custom-call | tf_op jit(solution)/shard_map/prep/pallas_call | solution.py:486
  2.5 8.9 %all-to-all-start = ((bf16[32,32,128]{2,1,0:T(8,128)(2,1)}), bf16[32,32,128]{2,1,0:T(8,128)(2,1)}, u32[]{:S(2)}, u32[]{:S(2)}) async-start(bf16[32,32,128]{2,1,0:T(8,128)(2,1)} %get-tuple-element.34), calls=%async_computation | async-start | bytes 524288 | tf_op jit(solution)/shard_map/all_to_all | solution.py:496
  11.5 3.4 %collective-permute-start = (bf16[8,4096]{1,0:T(8,128)(2,1)}, bf16[8,4096]{1,0:T(8,128)(2,1)}, u32[]{:S(2)}, u32[]{:S(2)}) collective-permute-start(bf16[8,4096]{1,0:T(8,128)(2,1)} %get-tuple-element.33), channel_id=1, source_target_pairs={{0,8},{8,16},{16,24},{24,32},{32,40},{40,48},{48,56},{56,64},{64,7... | collective-permute-start | bytes 196616 | tf_op jit(solution)/shard_map/ppermute | solution.py:495
  14.9 1.8 %front.1 = bf16[8,4096]{1,0:T(8,128)(2,1)} custom-call(bf16[1,128,4096]{2,1,0:T(8,128)(2,1)} %query_end.1, bf16[1,128,4096]{2,1,0:T(8,128)(2,1)} %key_end.1, bf16[1,128,4096]{2,1,0:T(8,128)(2,1)} %value_end.1, bf16[1,128,4096]{2,1,0:T(8,128)(2,1)} %cot_ref.3), custom_call_target="tpu_custom_call" | custom-call | tf_op jit(solution)/shard_map/front/pallas_call | solution.py:525
  16.6 3.4 %collective-permute-done.before_ref = bf16[8,4096]{1,0:T(8,128)(2,1)} collective-permute-done((bf16[8,4096]{1,0:T(8,128)(2,1)}, bf16[8,4096]{1,0:T(8,128)(2,1)}, u32[]{:S(2)}, u32[]{:S(2)}) %collective-permute-start) | collective-permute-done | bytes 65568 | tf_op jit(solution)/shard_map/ppermute | solution.py:495
  20.1 11.2 %block.1 = (bf16[32,128,128]{2,1,0:T(8,128)(2,1)}, bf16[128,4096]{1,0:T(8,128)(2,1)}, bf16[128,4096]{1,0:T(8,128)(2,1)}, bf16[128,4096]{1,0:T(8,128)(2,1)}, bf16...) custom-call(bf16[1,128,4096]{2,1,0:T(8,128)(2,1)} %query_end.1, bf16[1,128,4096]{2,1,0:T(8,128)(2,1)} %key_end.1, ...), custom_call_target="tpu_custom_call" | custom-call | tf_op jit(solution)/shard_map/block/pallas_call | solution.py:512
  31.3 6.4 %all-to-all-start.1 = ((bf16[32,128,128]{2,1,0:T(8,128)(2,1)}), bf16[32,128,128]{2,1,0:T(8,128)(2,1)S(1)}, u32[]{:S(2)}, u32[]{:S(2)}) async-start(bf16[32,128,128]{2,1,0:T(8,128)(2,1)} %get-tuple-element.36), calls=%async_computation.1 | async-start | bytes 2097152 | tf_op jit(solution)/shard_map/all_to_all | solution.py:535
  37.7 0.0 copy-start
  37.8 0.0 copy-start.4
  37.8 4.7 %collective-permute-start.1 = (bf16[8,4096]{1,0:T(8,128)(2,1)S(1)}, bf16[8,4096]{1,0:T(8,128)(2,1)S(1)}, u32[]{:S(2)}, u32[]{:S(2)}) collective-permute-start(bf16[8,4096]{1,0:T(8,128)(2,1)S(1)} %copy-done.7), channel_id=1, source_target_pairs={{8,0},{16,8},{24,16},{32,24},{40,32},{48,40},{56,48},{64,56},{72,6... | collective-permute-start | bytes 196616 | tf_op jit(solution)/shard_map/ppermute | solution.py:536
  42.5 7.8 %collective-permute-done.1.after_ref = bf16[8,4096]{1,0:T(8,128)(2,1)S(1)} collective-permute-done((bf16[8,4096]{1,0:T(8,128)(2,1)S(1)}, bf16[8,4096]{1,0:T(8,128)(2,1)S(1)}, u32[]{:S(2)}, u32[]{:S(2)}) %collective-permute-start.1) | collective-permute-done | bytes 65568 | tf_op jit(solution)/shard_map/ppermute | solution.py:536
  50.3 1.3 %all-to-all-done.1 = bf16[32,128,128]{2,1,0:T(8,128)(2,1)S(1)} async-done(((bf16[32,128,128]{2,1,0:T(8,128)(2,1)}), bf16[32,128,128]{2,1,0:T(8,128)(2,1)S(1)}, u32[]{:S(2)}, u32[]{:S(2)}) %all-to-all-start.1) | async-done | bytes 1048608 | tf_op jit(solution)/shard_map/all_to_all | solution.py:535
  51.6 0.6 convert_bitcast_fusion.refs_0_
  52.3 2.0 %owner.1 = (bf16[48,32,128]{2,1,0:T(8,128)(2,1)S(1)}, f32[48,128]{1,0:T(8,128)S(1)}) custom-call(f32[128,32,128]{2,1,0:T(8,128)S(1)} %convert_bitcast_fusion.refs_0_, f32[10,16,128]{2,1,0:T(8,128)S(1)} %copy-done, f32[10,16,128]{2,1,0:T(8,128)S(1)} %copy-done.1, f32[10,16,128]{2,1,0:T(8,128)S(1)} %copy-done.2, f32[16,128]{1,0:T(8,128)S(1)} %bitcast.13, ...), custom_call_target="tpu_custom_call" | custom-call | tf_op jit(solution)/shard_map/owner/pallas_call | solution.py:540
  54.2 0.1 collective-permute-start.2
  54.3 1.2 %collective-permute-done.2.other_ref = f32[48,128]{1,0:T(8,128)S(1)} collective-permute-done((f32[48,128]{1,0:T(8,128)S(1)}, f32[48,128]{1,0:T(8,128)S(1)}, u32[]{:S(2)}, u32[]{:S(2)}) %collective-permute-start.2) | collective-permute-done | bytes 24608 | tf_op jit(solution)/shard_map/ppermute | solution.py:550
  55.5 0.6 pair.1
  56.1 7.6 %all-to-all-start.2 = ((bf16[4,48,128]{2,1,0:T(8,128)(2,1)}), bf16[4,48,128]{2,1,0:T(8,128)(2,1)S(1)}, u32[]{:S(2)}, u32[]{:S(2)}) async-start(bf16[4,48,128]{2,1,0:T(8,128)(2,1)} %pair.1), calls=%async_computation.2 | async-start | bytes 98304 | tf_op jit(solution)/shard_map/all_to_all | solution.py:558
  63.7 0.2 copy.25
  63.8 2.1 %edge.1.local_edge_ref = f32[8,4096]{1,0:T(8,128)} custom-call(bf16[1,128,4096]{2,1,0:T(8,128)(2,1)} %query_end.1, bf16[1,128,4096]{2,1,0:T(8,128)(2,1)} %key_end.1, bf16[1,128,4096]{2,1,0:T(8,128)(2,1)} %value_end.1, f32[3,3,4096]{2,1,0:T(4,128)} %filter_ref.5, bf16[8,4096]{1,0:T(8,128)(2,1)} %copy-done.6, f32[8,4096]{1,0:T(8,128)} %get-tuple-element.45.impulse_ref), custom_call_target="tpu_custom_call" | custom-call | tf_op jit(solution)/shard_map/edge/pallas_call | solution.py:559
  66.0 5.9 %all-to-all-done.2.refs_0_ = bf16[4,48,128]{2,1,0:T(8,128)(2,1)S(1)} async-done(((bf16[4,48,128]{2,1,0:T(8,128)(2,1)}), bf16[4,48,128]{2,1,0:T(8,128)(2,1)S(1)}, u32[]{:S(2)}, u32[]{:S(2)}) %all-to-all-start.2) | async-done | bytes 49184 | tf_op jit(solution)/shard_map/all_to_all | solution.py:558
  71.9 0.6 total.1
  72.5 14.9 %all_to_all.20.carry_ref = bf16[32,48,128]{2,1,0:T(8,128)(2,1)} all-to-all(bf16[32,48,128]{2,1,0:T(8,128)(2,1)S(1)} %get-tuple-element.53), channel_id=1, replica_groups=mesh['seq'=32,'dp'=8] {'seq'}, dimensions={0} | all-to-all | bytes 786432 | tf_op jit(solution)/shard_map/all_to_all | solution.py:576
  87.4 6.9 %finish.1 = (bf16[1,128,4096]{2,1,0:T(8,128)(2,1)}, bf16[1,128,4096]{2,1,0:T(8,128)(2,1)}, bf16[1,128,4096]{2,1,0:T(8,128)(2,1)}, f32[3,3,4096]{2,1,0:T(4,128)}) custom-call(bf16[1,128,4096]{2,1,0:T(8,128)(2,1)} %cot_ref.3, f32[3,3,4096]{2,1,0:T(4,128)} %filter_ref.5, bf16[8,4096]{1,0:T(8,128)(2,1)} %copy-done.6, f32[8,4096]{1,0:T(8,128)} %edge.1.local_edge_ref, ...), custom_call_target="tpu_custom_call" | custom-call | tf_op jit(solution)/shard_map/finish/pallas_call | solution.py:579
  (15 shorter events, 0.0 us)
Async XLA Ops:
  2.5 17.5 %all-to-all-start = ((bf16[32,32,128]{2,1,0:T(8,128)(2,1)}), bf16[32,32,128]{2,1,0:T(8,128)(2,1)}, u32[]{:S(2)}, u32[]{:S(2)}) async-start(bf16[32,32,128]{2,1,0:T(8,128)(2,1)} %get-tuple-element.34), calls=%async_computation | async-start | bytes 524288 | tf_op jit(solution)/shard_map/all_to_all | solution.py:496
  11.5 8.6 %collective-permute-start = (bf16[8,4096]{1,0:T(8,128)(2,1)}, bf16[8,4096]{1,0:T(8,128)(2,1)}, u32[]{:S(2)}, u32[]{:S(2)}) collective-permute-start(bf16[8,4096]{1,0:T(8,128)(2,1)} %get-tuple-element.33), channel_id=1, source_target_pairs={{0,8},{8,16},{16,24},{24,32},{32,40},{40,48},{48,56},{56,64},{64,7... | collective-permute-start | bytes 196616 | tf_op jit(solution)/shard_map/ppermute | solution.py:495
  31.3 6.4 %copy-start.7 = (bf16[8,4096]{1,0:T(8,128)(2,1)S(1)}, bf16[8,4096]{1,0:T(8,128)(2,1)}, u32[]{:S(2)}) copy-start(bf16[8,4096]{1,0:T(8,128)(2,1)} %front.1) | copy-start | bytes 196612
  31.3 20.3 %all-to-all-start.1 = ((bf16[32,128,128]{2,1,0:T(8,128)(2,1)}), bf16[32,128,128]{2,1,0:T(8,128)(2,1)S(1)}, u32[]{:S(2)}, u32[]{:S(2)}) async-start(bf16[32,128,128]{2,1,0:T(8,128)(2,1)} %get-tuple-element.36), calls=%async_computation.1 | async-start | bytes 2097152 | tf_op jit(solution)/shard_map/all_to_all | solution.py:535
  37.7 14.5 %copy-start = (f32[10,16,128]{2,1,0:T(8,128)S(1)}, f32[10,16,128]{2,1,0:T(8,128)}, u32[]{:S(2)}) copy-start(f32[10,16,128]{2,1,0:T(8,128)} %get-tuple-element.40.refs_1_) | copy-start | bytes 245764
  37.7 14.5 %copy-start.1 = (f32[10,16,128]{2,1,0:T(8,128)S(1)}, f32[10,16,128]{2,1,0:T(8,128)}, u32[]{:S(2)}) copy-start(f32[10,16,128]{2,1,0:T(8,128)} %get-tuple-element.41.refs_2_) | copy-start | bytes 245764
  37.7 14.5 %copy-start.2 = (f32[10,16,128]{2,1,0:T(8,128)S(1)}, f32[10,16,128]{2,1,0:T(8,128)}, u32[]{:S(2)}) copy-start(f32[10,16,128]{2,1,0:T(8,128)} %get-tuple-element.42.refs_3_) | copy-start | bytes 245764
  37.7 14.5 %copy-start.3 = (f32[128,16]{0,1:T(8,128)S(1)}, f32[128,16]{0,1:T(8,128)}, u32[]{:S(2)}) copy-start(f32[128,16]{0,1:T(8,128)} %param.18) | copy-start | bytes 24580
  37.8 14.5 %copy-start.4 = (f32[128,16]{0,1:T(8,128)S(1)}, f32[128,16]{0,1:T(8,128)}, u32[]{:S(2)}) copy-start(f32[128,16]{0,1:T(8,128)} %param.19) | copy-start | bytes 24580
  37.8 14.5 %copy-start.5 = (f32[16,128]{1,0:T(8,128)S(1)}, f32[16,128]{1,0:T(8,128)}, u32[]{:S(2)}) copy-start(f32[16,128]{1,0:T(8,128)} %get-tuple-element.43.refs_5_) | copy-start | bytes 24580
  37.8 12.5 %collective-permute-start.1 = (bf16[8,4096]{1,0:T(8,128)(2,1)S(1)}, bf16[8,4096]{1,0:T(8,128)(2,1)S(1)}, u32[]{:S(2)}, u32[]{:S(2)}) collective-permute-start(bf16[8,4096]{1,0:T(8,128)(2,1)S(1)} %copy-done.7), channel_id=1, source_target_pairs={{8,0},{16,8},{24,16},{32,24},{40,32},{48,40},{56,48},{64,56},{72,6... | collective-permute-start | bytes 196616 | tf_op jit(solution)/shard_map/ppermute | solution.py:536
  50.3 3.9 %copy-start.6 = (bf16[8,4096]{1,0:T(8,128)(2,1)}, bf16[8,4096]{1,0:T(8,128)(2,1)S(1)}, u32[]{:S(2)}) copy-start(bf16[8,4096]{1,0:T(8,128)(2,1)S(1)} %collective-permute-done.1.after_ref) | copy-start | bytes 196612
  54.2 1.3 %collective-permute-start.2 = (f32[48,128]{1,0:T(8,128)S(1)}, f32[48,128]{1,0:T(8,128)S(1)}, u32[]{:S(2)}, u32[]{:S(2)}) collective-permute-start(f32[48,128]{1,0:T(8,128)S(1)} %get-tuple-element.44.own_ref), channel_id=1, source_target_pairs={{0,1},{1,0},{2,3},{3,2},{4,5},{5,4},{6,7},{7,6},{8,9},{9,8},{10,11... | collective-permute-start | bytes 73736 | tf_op jit(solution)/shard_map/ppermute | solution.py:550
  56.1 15.8 %all-to-all-start.2 = ((bf16[4,48,128]{2,1,0:T(8,128)(2,1)}), bf16[4,48,128]{2,1,0:T(8,128)(2,1)S(1)}, u32[]{:S(2)}, u32[]{:S(2)}) async-start(bf16[4,48,128]{2,1,0:T(8,128)(2,1)} %pair.1), calls=%async_computation.2 | async-start | bytes 98304 | tf_op jit(solution)/shard_map/all_to_all | solution.py:558

commit v6 on v4

--- a/solution.py
+++ b/solution.py
@@ -403,7 +403,7 @@
     mixed_ref, grad_ref, carry_ref, carried_ref,
     query_out, key_out, value_out, filter_out,
 ):
-    step = min(INNER, mixed_ref.shape[1])
+    step = mixed_ref.shape[1]
     for start in range(0, mixed_ref.shape[1], step):
         finish_columns(
             slice(start, start + step), slice(start // LANES, (start + step) // LANES),

time: 94.7 us -> 94.6 us (level)
  no operation moved by 1% of the time
where the time goes in v6:
time: 94.6 us; the launch traced here: 94 us
  starting transfers between devices  30.9 us (33%)
  Pallas kernels  27.2 us (29%)
  waiting for transfers between devices  19.5 us (21%)
  blocking collectives  14.8 us (16%)
    all_to_all x1, blocking collectives, body(): carry = lax.all_to_all(sent, 'seq', 0, 0, tiled=True)  14.8 us
    pallas_call x1, Pallas kernels, body(): pl.pallas_call(block_kernel, grid=grid, in_specs=[tall] * 4 + [filters, f...  11.2 us
    all_to_all x1, starting transfers between devices, body(): coefs = lax.all_to_all(spread, 'seq', 0, 0, tiled=True)  8.94 us
    ppermute x1, waiting for transfers between devices, body(): after = lax.ppermute(front, 'seq', [(i + 1, i) for i in range(blocks - 1)])  7.81 us
    all_to_all x1, starting transfers between devices, body(): message = lax.all_to_all(message, 'dp', 0, 0, tiled=True)  7.56 us
    all_to_all x1, waiting for transfers between devices, body(): message = lax.all_to_all(message, 'dp', 0, 0, tiled=True)  6.93 us
    pallas_call x1, Pallas kernels, body(): pl.pallas_call(finish_kernel, grid=grid, in_specs=[tall, filters, flat(8)...  6.93 us
    all_to_all x1, starting transfers between devices, body(): moments = lax.all_to_all(sent, 'seq', 0, 0, tiled=True)  6.36 us
  transfers between devices with their start and end apart: 5, of which 4 were waited for; matrix products, arithmetic and copies ran while one was open for 0% of the time, Pallas kernels for 4%

profile of v6, /device:TPU:8, one launch (start us, length us, event | category | flops | bytes accessed | tf_op | source)
XLA Modules:
  0.0 94.0 jit_solution(8817390628303081564)
XLA Ops:
  0.6 1.9 %prep.1 = (f32[16,128]{1,0:T(8,128)}, f32[10,16,128]{2,1,0:T(8,128)}, f32[10,16,128]{2,1,0:T(8,128)}, f32[10,16,128]{2,1,0:T(8,128)}, bf16[32,32,128]{2,1,0:T(8,128)(2,1)}, /*index=5*/bf16[8,4096]{1,0:T(8,128)(2,1)}) custom-call(f32[16,128]{1,0:T(8,128)} %bitcast.10, f32[16,128]{1,0:T(8,128)} %bitcast.12, bf16[1,128,4096]{2,1,0:T(8,128)(2,1)} %query_end.1, ...), custom_call_target="tpu_custom_call" | custom-call | tf_op jit(solution)/shard_map/prep/pallas_call | solution.py:481
  2.5 8.9 %all-to-all-start = ((bf16[32,32,128]{2,1,0:T(8,128)(2,1)}), bf16[32,32,128]{2,1,0:T(8,128)(2,1)}, u32[]{:S(2)}, u32[]{:S(2)}) async-start(bf16[32,32,128]{2,1,0:T(8,128)(2,1)} %get-tuple-element.34), calls=%async_computation | async-start | bytes 524288 | tf_op jit(solution)/shard_map/all_to_all | solution.py:491
  11.5 3.4 %collective-permute-start = (bf16[8,4096]{1,0:T(8,128)(2,1)}, bf16[8,4096]{1,0:T(8,128)(2,1)}, u32[]{:S(2)}, u32[]{:S(2)}) collective-permute-start(bf16[8,4096]{1,0:T(8,128)(2,1)} %get-tuple-element.33), channel_id=1, source_target_pairs={{0,8},{8,16},{16,24},{24,32},{32,40},{40,48},{48,56},{56,64},{64,7... | collective-permute-start | bytes 196616 | tf_op jit(solution)/shard_map/ppermute | solution.py:490
  14.9 1.8 %front.1 = bf16[8,4096]{1,0:T(8,128)(2,1)} custom-call(bf16[1,128,4096]{2,1,0:T(8,128)(2,1)} %query_end.1, bf16[1,128,4096]{2,1,0:T(8,128)(2,1)} %key_end.1, bf16[1,128,4096]{2,1,0:T(8,128)(2,1)} %value_end.1, bf16[1,128,4096]{2,1,0:T(8,128)(2,1)} %cot_ref.3), custom_call_target="tpu_custom_call" | custom-call | tf_op jit(solution)/shard_map/front/pallas_call | solution.py:520
  16.6 3.4 %collective-permute-done.before_ref = bf16[8,4096]{1,0:T(8,128)(2,1)} collective-permute-done((bf16[8,4096]{1,0:T(8,128)(2,1)}, bf16[8,4096]{1,0:T(8,128)(2,1)}, u32[]{:S(2)}, u32[]{:S(2)}) %collective-permute-start) | collective-permute-done | bytes 65568 | tf_op jit(solution)/shard_map/ppermute | solution.py:490
  20.1 11.2 %block.1 = (bf16[32,128,128]{2,1,0:T(8,128)(2,1)}, bf16[128,4096]{1,0:T(8,128)(2,1)}, bf16[128,4096]{1,0:T(8,128)(2,1)}, bf16[128,4096]{1,0:T(8,128)(2,1)}, bf16...) custom-call(bf16[1,128,4096]{2,1,0:T(8,128)(2,1)} %query_end.1, bf16[1,128,4096]{2,1,0:T(8,128)(2,1)} %key_end.1, ...), custom_call_target="tpu_custom_call" | custom-call | tf_op jit(solution)/shard_map/block/pallas_call | solution.py:507
  31.3 6.4 %all-to-all-start.1 = ((bf16[32,128,128]{2,1,0:T(8,128)(2,1)}), bf16[32,128,128]{2,1,0:T(8,128)(2,1)S(1)}, u32[]{:S(2)}, u32[]{:S(2)}) async-start(bf16[32,128,128]{2,1,0:T(8,128)(2,1)} %get-tuple-element.36), calls=%async_computation.1 | async-start | bytes 2097152 | tf_op jit(solution)/shard_map/all_to_all | solution.py:530
  37.7 0.0 copy-start
  37.7 0.0 copy-start.1
  37.7 0.0 copy-start.3
  37.8 0.0 copy-start.4
  37.8 0.0 copy-start.5
  37.8 4.7 %collective-permute-start.1 = (bf16[8,4096]{1,0:T(8,128)(2,1)S(1)}, bf16[8,4096]{1,0:T(8,128)(2,1)S(1)}, u32[]{:S(2)}, u32[]{:S(2)}) collective-permute-start(bf16[8,4096]{1,0:T(8,128)(2,1)S(1)} %copy-done.7), channel_id=1, source_target_pairs={{8,0},{16,8},{24,16},{32,24},{40,32},{48,40},{56,48},{64,56},{72,6... | collective-permute-start | bytes 196616 | tf_op jit(solution)/shard_map/ppermute | solution.py:531
  42.5 7.8 %collective-permute-done.1.after_ref = bf16[8,4096]{1,0:T(8,128)(2,1)S(1)} collective-permute-done((bf16[8,4096]{1,0:T(8,128)(2,1)S(1)}, bf16[8,4096]{1,0:T(8,128)(2,1)S(1)}, u32[]{:S(2)}, u32[]{:S(2)}) %collective-permute-start.1) | collective-permute-done | bytes 65568 | tf_op jit(solution)/shard_map/ppermute | solution.py:531
  50.3 1.3 %all-to-all-done.1 = bf16[32,128,128]{2,1,0:T(8,128)(2,1)S(1)} async-done(((bf16[32,128,128]{2,1,0:T(8,128)(2,1)}), bf16[32,128,128]{2,1,0:T(8,128)(2,1)S(1)}, u32[]{:S(2)}, u32[]{:S(2)}) %all-to-all-start.1) | async-done | bytes 1048608 | tf_op jit(solution)/shard_map/all_to_all | solution.py:530
  51.6 0.6 convert_bitcast_fusion.refs_0_
  52.3 2.6 %owner.1 = (bf16[48,32,128]{2,1,0:T(8,128)(2,1)S(1)}, bf16[8,48,128]{2,1,0:T(8,128)(2,1)}) custom-call(f32[128,32,128]{2,1,0:T(8,128)S(1)} %convert_bitcast_fusion.refs_0_, f32[10,16,128]{2,1,0:T(8,128)S(1)} %copy-done, f32[10,16,128]{2,1,0:T(8,128)S(1)} %copy-done.1, f32[10,16,128]{2,1,0:T(8,128)S(1)} %copy-done.2, f32[16,128]{1,0:T(8,128)S(1)} %bitcast.13, ...), custom_call_target="tpu_custom_call" | custom-call | tf_op jit(solution)/shard_map/owner/pallas_call | solution.py:535
  54.8 7.6 %all-to-all-start.2 = ((bf16[8,48,128]{2,1,0:T(8,128)(2,1)}), bf16[8,48,128]{2,1,0:T(8,128)(2,1)S(1)}, u32[]{:S(2)}, u32[]{:S(2)}) async-start(bf16[8,48,128]{2,1,0:T(8,128)(2,1)} %get-tuple-element.44), calls=%async_computation.2 | async-start | bytes 196608 | tf_op jit(solution)/shard_map/all_to_all | solution.py:545
  62.4 0.2 copy.25
  62.6 2.1 %edge.1.local_edge_ref = f32[8,4096]{1,0:T(8,128)} custom-call(bf16[1,128,4096]{2,1,0:T(8,128)(2,1)} %query_end.1, bf16[1,128,4096]{2,1,0:T(8,128)(2,1)} %key_end.1, bf16[1,128,4096]{2,1,0:T(8,128)(2,1)} %value_end.1, f32[3,3,4096]{2,1,0:T(4,128)} %filter_ref.5, bf16[8,4096]{1,0:T(8,128)(2,1)} %copy-done.6, f32[8,4096]{1,0:T(8,128)} %get-tuple-element.45.impulse_ref), custom_call_target="tpu_custom_call" | custom-call | tf_op jit(solution)/shard_map/edge/pallas_call | solution.py:546
  64.7 6.9 %all-to-all-done.2.refs_0_ = bf16[8,48,128]{2,1,0:T(8,128)(2,1)S(1)} async-done(((bf16[8,48,128]{2,1,0:T(8,128)(2,1)}), bf16[8,48,128]{2,1,0:T(8,128)(2,1)S(1)}, u32[]{:S(2)}, u32[]{:S(2)}) %all-to-all-start.2) | async-done | bytes 98336 | tf_op jit(solution)/shard_map/all_to_all | solution.py:545
  71.6 0.6 total.1
  72.3 14.8 %all_to_all.20.carry_ref = bf16[32,48,128]{2,1,0:T(8,128)(2,1)} all-to-all(bf16[32,48,128]{2,1,0:T(8,128)(2,1)S(1)} %get-tuple-element.53), channel_id=1, replica_groups=mesh['seq'=32,'dp'=8] {'seq'}, dimensions={0} | all-to-all | bytes 786432 | tf_op jit(solution)/shard_map/all_to_all | solution.py:563
  87.0 6.9 %finish.1 = (bf16[1,128,4096]{2,1,0:T(8,128)(2,1)}, bf16[1,128,4096]{2,1,0:T(8,128)(2,1)}, bf16[1,128,4096]{2,1,0:T(8,128)(2,1)}, f32[3,3,4096]{2,1,0:T(4,128)}) custom-call(bf16[1,128,4096]{2,1,0:T(8,128)(2,1)} %cot_ref.3, f32[3,3,4096]{2,1,0:T(4,128)} %filter_ref.5, bf16[8,4096]{1,0:T(8,128)(2,1)} %copy-done.6, f32[8,4096]{1,0:T(8,128)} %edge.1.local_edge_ref, ...), custom_call_target="tpu_custom_call" | custom-call | tf_op jit(solution)/shard_map/finish/pallas_call | solution.py:566
  (12 shorter events, 0.0 us)
Async XLA Ops:
  2.5 17.5 %all-to-all-start = ((bf16[32,32,128]{2,1,0:T(8,128)(2,1)}), bf16[32,32,128]{2,1,0:T(8,128)(2,1)}, u32[]{:S(2)}, u32[]{:S(2)}) async-start(bf16[32,32,128]{2,1,0:T(8,128)(2,1)} %get-tuple-element.34), calls=%async_computation | async-start | bytes 524288 | tf_op jit(solution)/shard_map/all_to_all | solution.py:491
  11.5 8.6 %collective-permute-start = (bf16[8,4096]{1,0:T(8,128)(2,1)}, bf16[8,4096]{1,0:T(8,128)(2,1)}, u32[]{:S(2)}, u32[]{:S(2)}) collective-permute-start(bf16[8,4096]{1,0:T(8,128)(2,1)} %get-tuple-element.33), channel_id=1, source_target_pairs={{0,8},{8,16},{16,24},{24,32},{32,40},{40,48},{48,56},{56,64},{64,7... | collective-permute-start | bytes 196616 | tf_op jit(solution)/shard_map/ppermute | solution.py:490
  31.3 6.4 %copy-start.7 = (bf16[8,4096]{1,0:T(8,128)(2,1)S(1)}, bf16[8,4096]{1,0:T(8,128)(2,1)}, u32[]{:S(2)}) copy-start(bf16[8,4096]{1,0:T(8,128)(2,1)} %front.1) | copy-start | bytes 196612
  31.3 20.3 %all-to-all-start.1 = ((bf16[32,128,128]{2,1,0:T(8,128)(2,1)}), bf16[32,128,128]{2,1,0:T(8,128)(2,1)S(1)}, u32[]{:S(2)}, u32[]{:S(2)}) async-start(bf16[32,128,128]{2,1,0:T(8,128)(2,1)} %get-tuple-element.36), calls=%async_computation.1 | async-start | bytes 2097152 | tf_op jit(solution)/shard_map/all_to_all | solution.py:530
  37.7 14.5 %copy-start = (f32[10,16,128]{2,1,0:T(8,128)S(1)}, f32[10,16,128]{2,1,0:T(8,128)}, u32[]{:S(2)}) copy-start(f32[10,16,128]{2,1,0:T(8,128)} %get-tuple-element.40.refs_1_) | copy-start | bytes 245764
  37.7 14.5 %copy-start.1 = (f32[10,16,128]{2,1,0:T(8,128)S(1)}, f32[10,16,128]{2,1,0:T(8,128)}, u32[]{:S(2)}) copy-start(f32[10,16,128]{2,1,0:T(8,128)} %get-tuple-element.41.refs_2_) | copy-start | bytes 245764
  37.7 14.5 %copy-start.2 = (f32[10,16,128]{2,1,0:T(8,128)S(1)}, f32[10,16,128]{2,1,0:T(8,128)}, u32[]{:S(2)}) copy-start(f32[10,16,128]{2,1,0:T(8,128)} %get-tuple-element.42.refs_3_) | copy-start | bytes 245764
  37.7 14.5 %copy-start.3 = (f32[128,16]{0,1:T(8,128)S(1)}, f32[128,16]{0,1:T(8,128)}, u32[]{:S(2)}) copy-start(f32[128,16]{0,1:T(8,128)} %param.18) | copy-start | bytes 24580
  37.8 14.5 %copy-start.4 = (f32[128,16]{0,1:T(8,128)S(1)}, f32[128,16]{0,1:T(8,128)}, u32[]{:S(2)}) copy-start(f32[128,16]{0,1:T(8,128)} %param.19) | copy-start | bytes 24580
  37.8 14.5 %copy-start.5 = (f32[16,128]{1,0:T(8,128)S(1)}, f32[16,128]{1,0:T(8,128)}, u32[]{:S(2)}) copy-start(f32[16,128]{1,0:T(8,128)} %get-tuple-element.43.refs_5_) | copy-start | bytes 24580
  37.8 12.5 %collective-permute-start.1 = (bf16[8,4096]{1,0:T(8,128)(2,1)S(1)}, bf16[8,4096]{1,0:T(8,128)(2,1)S(1)}, u32[]{:S(2)}, u32[]{:S(2)}) collective-permute-start(bf16[8,4096]{1,0:T(8,128)(2,1)S(1)} %copy-done.7), channel_id=1, source_target_pairs={{8,0},{16,8},{24,16},{32,24},{40,32},{48,40},{56,48},{64,56},{72,6... | collective-permute-start | bytes 196616 | tf_op jit(solution)/shard_map/ppermute | solution.py:531
  50.3 4.5 %copy-start.6 = (bf16[8,4096]{1,0:T(8,128)(2,1)}, bf16[8,4096]{1,0:T(8,128)(2,1)S(1)}, u32[]{:S(2)}) copy-start(bf16[8,4096]{1,0:T(8,128)(2,1)S(1)} %collective-permute-done.1.after_ref) | copy-start | bytes 196612
  54.8 16.8 %all-to-all-start.2 = ((bf16[8,48,128]{2,1,0:T(8,128)(2,1)}), bf16[8,48,128]{2,1,0:T(8,128)(2,1)S(1)}, u32[]{:S(2)}, u32[]{:S(2)}) async-start(bf16[8,48,128]{2,1,0:T(8,128)(2,1)} %get-tuple-element.44), calls=%async_computation.2 | async-start | bytes 196608 | tf_op jit(solution)/shard_map/all_to_all | solution.py:545
